TPU v7x, 512 devices: a whole 4x8x8 slice. The times are simulated.
512 devices in a mesh: group: 4 (over x), dp: 32 (over y_lo, z, core), fsdp: 4 (over y_hi).
Axes of the slice: x: 4, y: 8 (y_hi: 4, y_lo: 2; y = y_hi * 2 + y_lo), z: 8, core: 2. Of those that a mesh axis runs over, the one named last changes fastest.
Arguments:
- student_tokens: bfloat16 [65536, 1280], P(('group', 'dp', 'fsdp')), may hold values from -6 to 6
- sam_maps: bfloat16 [4, 16384, 256], P(None, ('dp', 'fsdp'), 'group'), may hold values from -8 to 8
- dino_maps: bfloat16 [4, 16384, 1536], P(None, ('dp', 'fsdp'), 'group'), may hold values from -8 to 8
- sam_gain: float32 [256], replicated, may hold values from 0.1 to 1.9
- dino_gain: float32 [1536], replicated, may hold values from 0.1 to 1.9
- patch_counts: int32 [64], replicated, may hold values from 256 to 1024
- sam_in: bfloat16 [1280, 1280], P(('dp', 'fsdp')), may hold values from -0.15625 to 0.15625
- sam_out: bfloat16 [1280, 256], P(('dp', 'fsdp')), may hold values from -1 to 1
- dino_in: bfloat16 [1280, 1280], P(('dp', 'fsdp')), may hold values from -0.15625 to 0.15625
- dino_out: bfloat16 [1280, 1536], P(('dp', 'fsdp')), may hold values from -1 to 1
Outputs:
- token_grad: bfloat16 [65536, 1280], P(('group', 'dp', 'fsdp'))
- loss: float32 [], replicated
All inputs are finite; a program needn't handle non-finite values.
Results may differ from a plain program's by a relative error of at most 0.018.
Values may be sent and summed in bfloat16 or wider, within the bound.
No kernel may reach another device: no remote copies, remote signals or barrier semaphores. Data moves between devices by JAX's collectives and lax.ppermute only.
A program may use at most 64 MiB of HBM per device.

v0:
```python
import jax
import jax.numpy as jnp
from jax import lax
from jax.sharding import PartitionSpec as P

IMG_TOK = 1024


def teacher_targets(features, gain):
    values = features.astype(jnp.float32)
    center = jnp.mean(values, axis=-1, keepdims=True)
    spread = jnp.mean(values * values, axis=-1, keepdims=True) - center * center
    return ((values - center) * lax.rsqrt(spread + 1e-06) * gain).astype(jnp.bfloat16)


def head_forward(tokens, w_first, w_second, target):
    pre = jnp.dot(tokens, w_first, preferred_element_type=jnp.float32)
    act = jax.nn.gelu(pre).astype(jnp.bfloat16)
    pred = jnp.dot(act, w_second, preferred_element_type=jnp.float32)
    goal = target.astype(jnp.float32)
    pp_mean = jnp.mean(pred * pred, axis=-1) + 1e-05
    tt_mean = jnp.mean(goal * goal, axis=-1) + 1e-05
    pt_mean = jnp.mean(pred * goal, axis=-1)
    inv_root = lax.rsqrt(pp_mean * tt_mean)
    cosine = pt_mean * inv_root
    return (pre, pred, goal, pp_mean, inv_root, cosine)


def head_backward(pre, pred, goal, pp_mean, inv_root, cosine, weight_row, w_first, w_second):
    chans = pred.shape[1]
    back = (
        -weight_row[:, None]
        * (goal * inv_root[:, None] - (cosine / pp_mean)[:, None] * pred)
        / chans
    )
    back = back.astype(jnp.bfloat16)
    hid_back = jnp.dot(back, w_second.T, preferred_element_type=jnp.float32)
    hid_back = jax.vjp(jax.nn.gelu, pre)[1](hid_back)[0].astype(jnp.bfloat16)
    return jnp.dot(hid_back, w_first.T, preferred_element_type=jnp.float32)


def shards(
    student_tokens,
    sam_maps,
    dino_maps,
    sam_gain,
    dino_gain,
    patch_counts,
    sam_in,
    sam_out,
    dino_in,
    dino_out,
):
    rows = student_tokens.shape[0]
    sam_got, dino_got = (
        lax.all_to_all(sam_maps, "group", split_axis=0, concat_axis=2, tiled=True),
        lax.all_to_all(dino_maps, "group", split_axis=0, concat_axis=2, tiled=True),
    )
    sam_got = sam_got.reshape(rows, -1)
    dino_got = dino_got.reshape(rows, -1)
    target_s = teacher_targets(sam_got, sam_gain)
    target_d = teacher_targets(dino_got, dino_gain)
    start = lax.axis_index(("group", "dp", "fsdp")) * rows
    position = start + jnp.arange(rows, dtype=jnp.int32)
    image = position // IMG_TOK
    image_ids = jnp.arange(patch_counts.shape[0], dtype=jnp.int32)
    limit = jnp.sum(
        jnp.where(image[:, None] == image_ids[None, :], patch_counts[None, :], 0), axis=1
    )
    live = (position % IMG_TOK < limit).astype(jnp.float32)
    full_sam_in, full_sam_out, full_dino_in, full_dino_out = (
        lax.all_gather(sam_in, ("dp", "fsdp"), axis=0, tiled=True),
        lax.all_gather(sam_out, ("dp", "fsdp"), axis=0, tiled=True),
        lax.all_gather(dino_in, ("dp", "fsdp"), axis=0, tiled=True),
        lax.all_gather(dino_out, ("dp", "fsdp"), axis=0, tiled=True),
    )
    fwd_s = head_forward(student_tokens, full_sam_in, full_sam_out, target_s)
    fwd_d = head_forward(student_tokens, full_dino_in, full_dino_out, target_d)
    local_loss = jnp.sum(live * (2.0 - fwd_s[5] - fwd_d[5]))
    count, loss_sum = lax.psum((jnp.sum(live), local_loss), ("group", "dp", "fsdp"))
    scale = live / count
    grad = head_backward(*fwd_s, scale, full_sam_in, full_sam_out) + head_backward(
        *fwd_d, scale, full_dino_in, full_dino_out
    )
    return (grad.astype(jnp.bfloat16), loss_sum / count)


def solution(mesh):
    return jax.shard_map(
        shards,
        mesh=mesh,
        in_specs=(
            P(("group", "dp", "fsdp"), None),
            P(None, ("dp", "fsdp"), "group"),
            P(None, ("dp", "fsdp"), "group"),
            P(),
            P(),
            P(),
            P(("dp", "fsdp"), None),
            P(("dp", "fsdp"), None),
            P(("dp", "fsdp"), None),
            P(("dp", "fsdp"), None),
        ),
        out_specs=(P(("group", "dp", "fsdp"), None), P()),
        check_vma=False,
    )
```

profile of v0, /device:TPU:1, one launch (start us, length us, event | category | flops | bytes accessed | tf_op | source)
XLA Modules:
  0.0 1268.0 jit_solution(5212057020002992776)
XLA Ops:
  7.2 0.0 copy-start
  7.2 0.0 all-gather.8.cloned.1.call-start
  7.2 0.7 all-gather.8.cloned.1.call-update
  7.9 0.0 all-gather.10.cloned.1.call-start
  8.0 0.7 all-gather.10.cloned.1.call-update
  8.7 0.0 all-gather.12.cloned.1.call-start
  8.7 0.7 all-gather.12.cloned.1.call-update
  9.4 4.9 all-to-all-start
  14.3 258.0 %all-gather.1 = bf16[128,10,256]{2,1,0:T(8,128)(2,1)S(1)} all-gather(bf16[1,10,256]{2,1,0:T(8,128)(2,1)} %bitcast.60), channel_id=1, replica_groups=mesh['group'=4,'dp'=32,'fsdp'=4] {'dp','fsdp'}, dimensions={0}, use_global_device_ids=true | all-gather | bytes 660480 | tf_op jit(solution)/shard_map/all_gather | solution.py:73
  272.3 0.7 select_reduce_fusion
  273.0 0.8 mul.306
  273.8 0.7 mul.343
  274.5 0.2 reshape.178
  274.7 0.0 all-to-all-done
  274.7 4.2 all-to-all-start.1
  279.0 0.1 copy.18
  279.1 0.0 copy-start.2
  279.1 0.1 convert_reduce_fusion.1
  279.1 0.1 fusion.68
  279.2 0.1 multiply_reduce_fusion.2
  279.3 5.9 all-to-all-done.1
  285.2 0.1 convert_bitcast_fusion
  285.2 0.5 copy.19
  285.8 0.1 copy.20
  285.8 0.1 convert_reduce_fusion
  286.0 0.2 fusion.6
  286.1 0.3 multiply_reduce_fusion
  286.4 100.7 %all-gather.8.cloned.1.call-done = bf16[128,10,1280]{2,1,0:T(8,128)(2,1)} async-done(((bf16[1,10,1280]{2,1,0:T(8,128)(2,1)}), bf16[128,10,1280]{2,1,0:T(8,128)(2,1)}) %all-gather.8.cloned.1.call-update) | async-done | bytes 3276816 | tf_op jit(solution)/shard_map/all_gather | solution.py:72
  387.1 7.0 reshape.176
  394.1 364.4 %all-gather.10.cloned.1.call-done = bf16[128,10,1280]{2,1,0:T(8,128)(2,1)} async-done(((bf16[1,10,1280]{2,1,0:T(8,128)(2,1)}), bf16[128,10,1280]{2,1,0:T(8,128)(2,1)}) %all-gather.10.cloned.1.call-update) | async-done | bytes 3276816 | tf_op jit(solution)/shard_map/all_gather | solution.py:74
  758.5 7.0 reshape.180
  765.5 0.0 copy-done
  765.5 0.0 copy-start.5
  765.5 0.0 copy-start.1
  765.5 2.7 fusion.111
  768.2 0.0 copy-done.2
  768.2 0.0 copy-done.5
  768.2 0.4 fusion.64
  768.7 0.0 copy-done.1
  768.7 0.6 fusion.112
  769.3 0.0 copy-start.4
  769.3 363.4 %all-gather.12.cloned.1.call-done = bf16[128,10,1536]{2,1,0:T(8,128)(2,1)} async-done(((bf16[1,10,1536]{2,1,0:T(8,128)(2,1)}), bf16[128,10,1536]{2,1,0:T(8,128)(2,1)}) %all-gather.12.cloned.1.call-update) | async-done | bytes 3932176 | tf_op jit(solution)/shard_map/all_gather | solution.py:75
  1132.8 7.5 reshape.182
  1140.3 0.0 copy-start.3
  1140.3 0.0 copy-done.4
  1140.3 3.9 fusion.11
  1144.2 0.6 select_reduce_fusion.1
  1144.8 102.5 %all-reduce = (f32[]{:T(128)}, f32[]{:T(128)}) all-reduce(f32[]{:T(128)} %get-tuple-element.7, f32[]{:T(128)} %get-tuple-element.6), channel_id=1, replica_groups=mesh['group'=4,'dp'=32,'fsdp'=4] {'group','dp','fsdp'}, use_global_device_ids=true, to_apply=%region_2.0 | all-reduce | flops 2 | bytes 16 | tf_op jit(solution)/shard_map/psum | solution.py:80
  1249.3 0.0 copy-done.3
  1249.3 4.2 fusion.41
  1253.5 6.8 fusion
  (7 shorter events, 0.1 us)
Async XLA Ops:
  7.2 758.4 %copy-start = (bf16[128,1280]{1,0:T(8,128)(2,1)S(1)}, bf16[128,1280]{1,0:T(8,128)(2,1)}, u32[]{:S(2)}) copy-start(bf16[128,1280]{1,0:T(8,128)(2,1)} %param.10) | copy-start | bytes 983044
  7.2 379.9 %all-gather.8.cloned.1.call-start = ((), (), s32[]{:S(2)}) async-start(), calls=%async_computation.2 | async-start | bytes 5283840 | tf_op jit(solution)/shard_map/all_gather | solution.py:72
  7.9 750.6 %all-gather.10.cloned.1.call-start = ((), (), s32[]{:S(2)}) async-start(), calls=%async_computation.3 | async-start | bytes 5283840 | tf_op jit(solution)/shard_map/all_gather | solution.py:74
  8.7 1124.1 %all-gather.12.cloned.1.call-start = ((), (), s32[]{:S(2)}) async-start(), calls=%async_computation.4 | async-start | bytes 6340608 | tf_op jit(solution)/shard_map/all_gather | solution.py:75
  9.4 265.3 %all-to-all-start = ((bf16[4,128,64]{1,2,0:T(8,128)(2,1)}), bf16[4,128,64]{1,2,0:T(8,128)(2,1)S(1)}, u32[]{:S(2)}, u32[]{:S(2)}) async-start(bf16[4,128,64]{1,2,0:T(8,128)(2,1)} %param.11), calls=%async_computation | async-start | bytes 131072 | tf_op jit(solution)/shard_map/all_to_all | solution.py:56
  274.7 10.4 all-to-all-start.1
  279.1 489.1 %copy-start.2 = (f32[128,256]{1,0:T(8,128)}, f32[128,256]{1,0:T(8,128)S(1)}, u32[]{:S(2)}) copy-start(f32[128,256]{1,0:T(8,128)S(1)} %copy.18) | copy-start | bytes 393220
  765.5 2.7 copy-start.5
  765.5 3.2 copy-start.1
  769.3 370.9 %copy-start.4 = (f32[1536]{0:T(1024)S(1)}, f32[1536]{0:T(1024)}, u32[]{:S(2)}) copy-start(f32[1536]{0:T(1024)} %param.14) | copy-start | bytes 18436
  1140.3 109.1 %copy-start.3 = (f32[128,256]{1,0:T(8,128)S(1)}, f32[128,256]{1,0:T(8,128)}, u32[]{:S(2)}) copy-start(f32[128,256]{1,0:T(8,128)} %copy-done.2) | copy-start | bytes 393220
Sparse Core Ops, SparseCore 0:
  10.1 376.9 all-gather.7
  389.2 369.2 all-gather.9
  760.6 372.0 all-gather.11
where the time goes:
time: 1270 us
  waiting for transfers between devices  836 us (66%)
  blocking collectives  361 us (28%)
  local copies, waits for them, and re-layouts  23.9 us (2%)
  matrix products  18.6 us (1%)
  between operations  17 us (1%)
    all_gather x1, waiting for transfers between devices, shards(): lax.all_gather(dino_in, ('dp', 'fsdp'), axis=0, tiled=True)  364 us
    all_gather x1, waiting for transfers between devices, shards(): lax.all_gather(dino_out, ('dp', 'fsdp'), axis=0, tiled=True)  363 us
    all_gather x1, blocking collectives, shards(): lax.all_gather(sam_out, ('dp', 'fsdp'), axis=0, tiled=True)  258 us
    psum x1, blocking collectives, shards(): lax.psum((jnp.sum(live), local_loss), ('group', 'dp', 'fsdp'))  103 us
    all_gather x1, waiting for transfers between devices, shards(): lax.all_gather(sam_in, ('dp', 'fsdp'), axis=0, tiled=True)  101 us
  transfers between devices with their start and end apart: 5, of which 4 were waited for; matrix products, arithmetic and copies ran while one was open for 2% of the time, Pallas kernels for 0%

commit v1 on v0

v1 whole, which is shorter than its diff:
```python
import jax
import jax.numpy as jnp
from jax import lax
from jax.sharding import Mesh, PartitionSpec as P

IMG_TOK = 1024
AXES = ("x", "ylo", "z", "core", "yhi")
PLANE = ("ylo", "z", "yhi")
IN_Q = 640
DINO_Q = 384
SAM_Q = 64
PAD_Q = 64


def ring(n, shift):
    return [(i, (i + shift) % n) for i in range(n)]


def quarter_of(q, w_in, dino_out, sam_out):
    rows = w_in.shape[0]
    part_in = lax.dynamic_slice(w_in, (0, q * IN_Q), (rows, IN_Q))
    part_d = lax.dynamic_slice(dino_out, (0, q * DINO_Q), (rows, DINO_Q))
    sam = sam_out.reshape(rows, 4, SAM_Q)
    part_s = lax.dynamic_index_in_dim(sam, q, axis=1, keepdims=False)
    pad = jnp.zeros((rows, PAD_Q), w_in.dtype)
    return jnp.concatenate([part_in, part_d, part_s, pad], axis=1)


def gather_plane(part):
    rows, cols = part.shape
    part = part.reshape(1, rows // 2, 2, cols)
    many = jnp.broadcast_to(part, (64, rows // 2, 2, cols))
    return lax.all_to_all(many, PLANE, split_axis=0, concat_axis=0, tiled=True)


def swap_core(value):
    return lax.ppermute(value, "core", ring(2, 1))


def natural_rows(mine, other, core):
    first = jnp.where(core == 0, mine, other)
    second = jnp.where(core == 0, other, mine)
    cols = mine.shape[-1]
    both = jnp.stack([first.reshape(16, 4, 5, 2, cols), second.reshape(16, 4, 5, 2, cols)], axis=1)
    return both.reshape(1280, cols)


def shards(
    student_tokens,
    sam_maps,
    dino_maps,
    sam_gain,
    dino_gain,
    patch_counts,
    sam_in,
    sam_out,
    dino_in,
    dino_out,
):
    rows = student_tokens.shape[0]
    x = lax.axis_index("x")
    core = lax.axis_index("core")
    f32 = jnp.float32
    bf16 = jnp.bfloat16

    def dot(a, b):
        return jnp.dot(a, b, preferred_element_type=f32)

    w_in = jnp.concatenate([sam_in, dino_in], axis=1)
    own_g = gather_plane(quarter_of(x, w_in, dino_out, sam_out))
    opp_part = quarter_of((x + 2) % 4, w_in, dino_out, sam_out)
    own_g, opp_part = lax.optimization_barrier((own_g, opp_part))
    opp_g = gather_plane(opp_part)

    feats = jnp.concatenate([dino_maps, sam_maps], axis=2)

    def feat_for(slot):
        return lax.dynamic_index_in_dim(feats, (x - slot) % 4, axis=0, keepdims=False)

    got = [feat_for(0)] + [lax.ppermute(feat_for(s), "x", ring(4, -s)) for s in (1, 2, 3)]

    own_full = natural_rows(own_g, swap_core(own_g), core)
    half = IN_Q

    def halves(full):
        mine = lax.dynamic_slice(full, (core * half, 0), (half, full.shape[1]))
        other = lax.dynamic_slice(full, ((1 - core) * half, 0), (half, full.shape[1]))
        return mine, other

    own = halves(own_full)
    next_m = lax.ppermute(own[0], "x", ring(4, -1))
    prev_m = lax.ppermute(own[0], "x", ring(4, 1))
    next_o = swap_core(next_m)
    prev_o = swap_core(prev_m)
    opp_full = natural_rows(opp_g, swap_core(opp_g), core)
    opp = halves(opp_full)
    slots = [own, (next_m, next_o), opp, (prev_m, prev_o)]

    feat = [g.astype(f32) for g in got]
    gains_d = dino_gain.reshape(4, DINO_Q)
    gains_s = sam_gain.reshape(4, SAM_Q)

    def targets(parts, gains):
        chans = 4 * parts[0].shape[1]
        center = sum(jnp.sum(p, axis=1, keepdims=True) for p in parts) / chans
        spread = sum(jnp.sum(p * p, axis=1, keepdims=True) for p in parts) / chans - center * center
        root = lax.rsqrt(spread + 1e-06)
        out = []
        for j, p in enumerate(parts):
            gain = lax.dynamic_index_in_dim(gains, (x + j) % 4, axis=0, keepdims=True)
            out.append(((p - center) * root * gain).astype(bf16).astype(f32))
        return out

    goal_d = targets([f[:, :DINO_Q] for f in feat], gains_d)
    goal_s = targets([f[:, DINO_Q:] for f in feat], gains_s)

    tok_m = lax.dynamic_slice(student_tokens, (0, core * half), (rows, half))
    tok_o = lax.dynamic_slice(student_tokens, (0, (1 - core) * half), (rows, half))
    pre_slots = jnp.stack([dot(tok_m, m[:, :IN_Q]) + dot(tok_o, o[:, :IN_Q]) for m, o in slots])
    pre = [lax.dynamic_index_in_dim(pre_slots, (q - x) % 4, axis=0, keepdims=False) for q in range(4)]
    act = jnp.stack([jax.nn.gelu(p).astype(bf16) for p in pre])

    def act_of(head, h):
        return lax.dynamic_index_in_dim(act, 2 * head + h, axis=0, keepdims=False)

    def preds(head, lo, hi):
        am, ao = act_of(head, core), act_of(head, 1 - core)
        return [dot(am, m[:, lo:hi]) + dot(ao, o[:, lo:hi]) for m, o in slots]

    s_cols = (IN_Q + DINO_Q, IN_Q + DINO_Q + SAM_Q)
    d_cols = (IN_Q, IN_Q + DINO_Q)
    pred_s = preds(0, *s_cols)
    pred_d = preds(1, *d_cols)

    def scores(pred, goal):
        chans = 4 * pred[0].shape[1]
        pp = sum(jnp.sum(p * p, axis=1, keepdims=True) for p in pred) / chans + 1e-05
        tt = sum(jnp.sum(g * g, axis=1, keepdims=True) for g in goal) / chans + 1e-05
        pt = sum(jnp.sum(p * g, axis=1, keepdims=True) for p, g in zip(pred, goal)) / chans
        inv_root = lax.rsqrt(pp * tt)
        return pp, inv_root, pt * inv_root

    sc_s = scores(pred_s, goal_s)
    sc_d = scores(pred_d, goal_d)

    start = lax.axis_index(AXES) * rows
    image = start // IMG_TOK
    limit = lax.dynamic_index_in_dim(patch_counts, image, keepdims=False)
    slot_at = start % IMG_TOK + jnp.arange(rows, dtype=jnp.int32)
    live = (slot_at < limit).astype(f32)[:, None]
    count = jnp.sum(jnp.clip(patch_counts, 0, IMG_TOK)).astype(f32)

    local = jnp.sum(live * (2.0 - sc_s[2] - sc_d[2]))
    local = lax.psum(local, "core")
    local = lax.psum(local, "x")
    spread_out = jnp.broadcast_to(local, (64, 1, 128))
    all_parts = lax.all_to_all(spread_out, PLANE, split_axis=0, concat_axis=0, tiled=True)
    loss = jnp.sum(all_parts[:, 0, 0]) / count

    scale = live / count

    def backs(pred, goal, score):
        pp, inv_root, cosine = score
        chans = 4 * pred[0].shape[1]
        return [
            (-scale * (g * inv_root - (cosine / pp) * p) / chans).astype(bf16)
            for p, g in zip(pred, goal)
        ]

    back_s = backs(pred_s, goal_s, sc_s)
    back_d = backs(pred_d, goal_d, sc_d)

    def hid_backs(back, lo, hi):
        m = sum(dot(b, w[0][:, lo:hi].T) for b, w in zip(back, slots))
        o = sum(dot(b, w[1][:, lo:hi].T) for b, w in zip(back, slots))
        return jnp.where(core == 0, m, o), jnp.where(core == 0, o, m)

    hid = [*hid_backs(back_s, *s_cols), *hid_backs(back_d, *d_cols)]
    hid = jnp.stack([jax.vjp(jax.nn.gelu, p)[1](h)[0].astype(bf16) for p, h in zip(pre, hid)])
    grad_m = jnp.zeros((rows, half), f32)
    grad_o = jnp.zeros((rows, half), f32)
    for j, (m, o) in enumerate(slots):
        h = lax.dynamic_index_in_dim(hid, (x + j) % 4, axis=0, keepdims=False)
        grad_m += dot(h, m[:, :IN_Q].T)
        grad_o += dot(h, o[:, :IN_Q].T)
    first = jnp.where(core == 0, grad_m, grad_o)
    second = jnp.where(core == 0, grad_o, grad_m)
    grad = jnp.concatenate([first, second], axis=1).astype(bf16)
    return (grad, loss)


def solution(mesh):
    fine = Mesh(mesh.devices.reshape(4, 2, 8, 2, 4), AXES)
    tokens = P(AXES, None)
    rest = ("ylo", "z", "core", "yhi")
    return jax.shard_map(
        shards,
        mesh=fine,
        in_specs=(
            tokens,
            P(None, rest, "x"),
            P(None, rest, "x"),
            P(),
            P(),
            P(),
            P(rest, None),
            P(rest, None),
            P(rest, None),
            P(rest, None),
        ),
        out_specs=(tokens, P()),
        check_vma=False,
    )
```

time: 1270 us -> 252 us (0.20)
  waiting for transfers between devices: 836 us -> 53.3 us
  blocking collectives: 361 us -> 9.91 us
  starting transfers between devices: 9.18 us -> 72.4 us
  other arithmetic: 2.31 us -> 35.2 us
  matrix products: 18.6 us -> 47.1 us
  between operations: 17 us -> 4.24 us
    all_gather x3 -> x0, waiting for transfers between devices: 828 us -> none  [the longest x1 364 us: shards(): lax.all_gather(dino_in, ('dp', 'fsdp'), axis=0, tiled=True)]
    all_gather x1 -> x0, blocking collectives: 258 us -> none  [shards(): lax.all_gather(sam_out, ('dp', 'fsdp'), axis=0, tiled=True)]
    psum x1 -> x2, blocking collectives: 103 us -> 9.91 us  [the longest x1 6.8 us: shards(): local = lax.psum(local, 'x')]
    all_to_all x2 -> x3, waiting for transfers between devices: 5.88 us -> 48 us  [the longest x2 41.2 us: gather_plane(): return lax.all_to_all(many, PLANE, split_axis=0, concat_axis=0, tiled=True)]
    ppermute x0 -> x9, starting transfers between devices: none -> 36.2 us  [the longest x4 20.8 us: swap_core(): return lax.ppermute(value, 'core', ring(2, 1))]
    dot_general x6 -> x48, matrix products: 18.6 us -> 47.1 us  [dot(): return jnp.dot(a, b, preferred_element_type=f32)]
    all_to_all x2 -> x3, starting transfers between devices: 9.07 us -> 36.2 us  [the longest x2 24.3 us: gather_plane(): return lax.all_to_all(many, PLANE, split_axis=0, concat_axis=0, tiled=True)]
    unnamed x17 -> x43, local copies, waits for them, and re-layouts: 21.9 us -> 2.01 us
  transfers between devices with their start and end apart: 5 -> 12, of which waited for: 4 -> 5; matrix products, arithmetic and copies ran while one was open for 2% -> 26% of each run, Pallas kernels for 0% -> 0%
where the time goes in v1:
time: 252 us; the launch traced here: 247 us
  starting transfers between devices  72.4 us (29%)
  waiting for transfers between devices  53.3 us (21%)
  matrix products  47.1 us (19%)
  other arithmetic  35.2 us (14%)
  local copies, waits for them, and re-layouts  24.9 us (10%)
  blocking collectives  9.91 us (4%)
  between operations  4.24 us (2%)
    dot_general x48, matrix products, dot(): return jnp.dot(a, b, preferred_element_type=f32)  47.1 us
    all_to_all x2, waiting for transfers between devices, gather_plane(): return lax.all_to_all(many, PLANE, split_axis=0, concat_axis=0, tiled=True)  41.2 us
    all_to_all x2, starting transfers between devices, gather_plane(): return lax.all_to_all(many, PLANE, split_axis=0, concat_axis=0, tiled=True)  24.3 us
    ppermute x4, starting transfers between devices, swap_core(): return lax.ppermute(value, 'core', ring(2, 1))  20.8 us
    reshape x2, local copies, waits for them, and re-layouts, natural_rows(): return both.reshape(1280, cols)  13.1 us
    all_to_all x1, starting transfers between devices, shards(): lax.all_to_all(spread_out, PLANE, split_axis=0, concat_axis=0, tiled=True)  12 us
    another operation x2, other arithmetic, natural_rows(): jnp.stack([first.reshape(16, 4, 5, 2, cols), second.reshape(16, 4, 5, 2,...  11.5 us
    ppermute x3, starting transfers between devices, shards(): lax.ppermute(feat_for(s), 'x', ring(4, -s))  9.32 us
  transfers between devices with their start and end apart: 12, of which 5 were waited for; matrix products, arithmetic and copies ran while one was open for 26% of the time, Pallas kernels for 0%

profile of v1, /device:TPU:1, one launch (start us, length us, event | category | flops | bytes accessed | tf_op | source)
XLA Modules:
  0.0 247.1 jit_solution(15512289982856307478)
XLA Ops:
  4.0 1.9 broadcast_in_dim.11
  5.9 17.3 %all-to-all-start = ((bf16[64,5,2,1152]{3,2,1,0:T(2,128)(2,1)}), bf16[64,5,2,1152]{3,2,1,0:T(2,128)(2,1)S(1)}, u32[]{:S(2)}, u32[]{:S(2)}) async-start(bf16[64,5,2,1152]{3,2,1,0:T(2,128)(2,1)} %broadcast_in_dim.11), calls=%async_computation | async-start | bytes 2949120 | tf_op jit(solution)/shard_map/all_to_all | solution.py:33
  23.3 34.9 %all-to-all-done = bf16[64,5,2,1152]{3,2,1,0:T(2,128)(2,1)S(1)} async-done(((bf16[64,5,2,1152]{3,2,1,0:T(2,128)(2,1)}), bf16[64,5,2,1152]{3,2,1,0:T(2,128)(2,1)S(1)}, u32[]{:S(2)}, u32[]{:S(2)}) %all-to-all-start) | async-done | bytes 1474592 | tf_op jit(solution)/shard_map/all_to_all | solution.py:33
  58.2 6.3 %collective-permute-start.3 = (bf16[64,5,2,1152]{3,2,1,0:T(2,128)(2,1)S(1)}, bf16[64,5,2,1152]{3,2,1,0:T(2,128)(2,1)}, u32[]{:S(2)}, u32[]{:S(2)}) collective-permute-start(bf16[64,5,2,1152]{3,2,1,0:T(2,128)(2,1)S(1)} %all-to-all-done), channel_id=1, source_target_pairs={{0,4},{4,0},{1,5},{5,1},{2,6},{6,2},{3,7},{7,3},{8,12},{12,8},{9,1... | collective-permute-start | bytes 4423688 | tf_op jit(solution)/shard_map/ppermute | solution.py:37
  65.6 4.4 %collective-permute-start = (bf16[128,448]{0,1:T(8,128)(2,1)}, bf16[128,448]{0,1:T(8,128)(2,1)}, u32[]{:S(2)}, u32[]{:S(2)}) collective-permute-start(bf16[128,448]{0,1:T(8,128)(2,1)} %get-tuple-element.83), channel_id=1, source_target_pairs={{0,384},{128,0},{256,128},{384,256},{1,385},{129,1},{257,129},{385... | collective-permute-start | bytes 344072 | tf_op jit(solution)/shard_map/ppermute | solution.py:80
  70.0 2.4 collective-permute-start.1
  72.4 2.5 %collective-permute-start.2 = (bf16[128,448]{0,1:T(8,128)(2,1)}, bf16[128,448]{0,1:T(8,128)(2,1)}, u32[]{:S(2)}, u32[]{:S(2)}) collective-permute-start(bf16[128,448]{0,1:T(8,128)(2,1)} %get-tuple-element.86), channel_id=1, source_target_pairs={{0,128},{128,256},{256,384},{384,0},{1,129},{129,257},{257,385},{3... | collective-permute-start | bytes 344072 | tf_op jit(solution)/shard_map/ppermute | solution.py:80
  78.3 1.9 broadcast_in_dim.13
  80.2 7.0 %all-to-all-start.1 = ((bf16[64,5,2,1152]{3,2,1,0:T(2,128)(2,1)}), bf16[64,5,2,1152]{3,2,1,0:T(2,128)(2,1)}, u32[]{:S(2)}, u32[]{:S(2)}) async-start(bf16[64,5,2,1152]{3,2,1,0:T(2,128)(2,1)} %broadcast_in_dim.13), calls=%async_computation.1 | async-start | bytes 2949120 | tf_op jit(solution)/shard_map/all_to_all | solution.py:33
  87.3 3.7 %broadcast_select_fusion.3 = (bf16[64,5,2,1152]{3,2,1,0:T(2,128)(2,1)S(1)}, bf16[64,5,2,1152]{3,2,1,0:T(2,128)(2,1)S(1)}) fusion(bf16[64,5,2,1152]{3,2,1,0:T(2,128)(2,1)S(1)} %all-to-all-done, bf16[64,5,2,1152]{3,2,1,0:T(2,128)(2,1)} %collective-permute-done.3, pred[]{:T(512)S(6)} %eq.35), kind=kLoop, calls=%fused_computation.5 | loop fusion | flops 1474560 | bytes 5898241 | tf_op jit(solution)/shard_map/jit(_where)/select_n | solution.py:41
  91.0 5.7 %pad_maximum_fusion = bf16[16,2,4,5,2,1152]{5,4,3,2,1,0:T(2,128)(2,1)} fusion(bf16[16,1,4,5,2,1152]{5,4,3,2,1,0:T(2,128)(2,1)S(1)} %bitcast.179, bf16[16,1,4,5,2,1152]{5,4,3,2,1,0:T(2,128)(2,1)S(1)} %bitcast.178), kind=kLoop, calls=%fused_computation | loop fusion | flops 1474560 | bytes 5898240 | tf_op jit(solution)/shard_map/stack | solution.py:44
  96.7 6.0 %reshape.317 = bf16[1280,1152]{1,0:T(8,128)(2,1)S(1)} reshape(bf16[16,2,4,5,2,1152]{5,4,3,2,1,0:T(2,128)(2,1)} %pad_maximum_fusion) | data formatting | bytes 5898240 | tf_op jit(solution)/shard_map/reshape | solution.py:45
  102.7 1.3 constant_dynamic-slice_fusion.7
  104.0 4.0 %collective-permute-start.4 = (bf16[640,1152]{1,0:T(8,128)(2,1)}, bf16[640,1152]{1,0:T(8,128)(2,1)}, u32[]{:S(2)}, u32[]{:S(2)}) collective-permute-start(bf16[640,1152]{1,0:T(8,128)(2,1)} %constant_dynamic-slice_fusion.7), channel_id=1, source_target_pairs={{0,384},{128,0},{256,128},{384,256},{1,385},{129,1},{257,129},{385... | collective-permute-start | bytes 4423688 | tf_op jit(solution)/shard_map/ppermute | solution.py:91
  108.0 2.1 collective-permute-start.7
  110.9 0.9 convert_element_type.126
  111.8 1.0 convert_element_type.127
  112.9 1.7 convert_element_type.128
  115.7 6.4 %all-to-all-done.1 = bf16[64,5,2,1152]{3,2,1,0:T(2,128)(2,1)} async-done(((bf16[64,5,2,1152]{3,2,1,0:T(2,128)(2,1)}), bf16[64,5,2,1152]{3,2,1,0:T(2,128)(2,1)}, u32[]{:S(2)}, u32[]{:S(2)}) %all-to-all-start.1) | async-done | bytes 1474592 | tf_op jit(solution)/shard_map/all_to_all | solution.py:33
  122.1 6.3 %collective-permute-start.6 = (bf16[64,5,2,1152]{3,2,1,0:T(2,128)(2,1)}, bf16[64,5,2,1152]{3,2,1,0:T(2,128)(2,1)S(1)}, u32[]{:S(2)}, u32[]{:S(2)}) collective-permute-start(bf16[64,5,2,1152]{3,2,1,0:T(2,128)(2,1)} %all-to-all-done.1), channel_id=1, source_target_pairs={{0,4},{4,0},{1,5},{5,1},{2,6},{6,2},{3,7},{7,3},{8,12},{12,8},{9,1... | collective-permute-start | bytes 4423688 | tf_op jit(solution)/shard_map/ppermute | solution.py:37
  129.2 1.0 multiply_reduce_fusion.5
  130.2 1.0 multiply_reduce_fusion.4
  131.2 1.3 add_rsqrt_fusion
  133.5 1.0 fusion.3
  134.6 4.4 %collective-permute-done.4 = bf16[640,1152]{1,0:T(8,128)(2,1)} collective-permute-done((bf16[640,1152]{1,0:T(8,128)(2,1)}, bf16[640,1152]{1,0:T(8,128)(2,1)}, u32[]{:S(2)}, u32[]{:S(2)}) %collective-permute-start.4) | collective-permute-done | bytes 1474592 | tf_op jit(solution)/shard_map/ppermute | solution.py:91
  139.0 3.9 %collective-permute-start.5 = (bf16[640,1152]{1,0:T(8,128)(2,1)}, bf16[640,1152]{1,0:T(8,128)(2,1)}, u32[]{:S(2)}, u32[]{:S(2)}) collective-permute-start(bf16[640,1152]{1,0:T(8,128)(2,1)} %collective-permute-done.4), channel_id=1, source_target_pairs={{0,4},{4,0},{1,5},{5,1},{2,6},{6,2},{3,7},{7,3},{8,12},{12,8},{9,1... | collective-permute-start | bytes 4423688 | tf_op jit(solution)/shard_map/ppermute | solution.py:37
  143.8 4.2 %collective-permute-start.8 = (bf16[640,1152]{1,0:T(8,128)(2,1)}, bf16[640,1152]{1,0:T(8,128)(2,1)}, u32[]{:S(2)}, u32[]{:S(2)}) collective-permute-start(bf16[640,1152]{1,0:T(8,128)(2,1)} %collective-permute-done.7), channel_id=1, source_target_pairs={{0,4},{4,0},{1,5},{5,1},{2,6},{6,2},{3,7},{7,3},{8,12},{12,8},{9,1... | collective-permute-start | bytes 4423688 | tf_op jit(solution)/shard_map/ppermute | solution.py:37
  148.0 2.2 fusion.12
  150.2 2.2 fusion.7
  152.4 3.7 %broadcast_select_fusion.1 = (bf16[64,5,2,1152]{3,2,1,0:T(2,128)(2,1)S(1)}, bf16[64,5,2,1152]{3,2,1,0:T(2,128)(2,1)S(1)}) fusion(bf16[64,5,2,1152]{3,2,1,0:T(2,128)(2,1)} %all-to-all-done.1, bf16[64,5,2,1152]{3,2,1,0:T(2,128)(2,1)S(1)} %collective-permute-done.6, pred[]{:T(512)S(6)} %eq.35), kind=kLoop, calls=%fused_computation.3 | loop fusion | flops 1474560 | bytes 5898241 | tf_op jit(solution)/shard_map/jit(_where)/select_n | solution.py:41
  156.1 5.8 %pad_maximum_fusion.1 = bf16[16,2,4,5,2,1152]{5,4,3,2,1,0:T(2,128)(2,1)} fusion(bf16[16,1,4,5,2,1152]{5,4,3,2,1,0:T(2,128)(2,1)S(1)} %bitcast.181, bf16[16,1,4,5,2,1152]{5,4,3,2,1,0:T(2,128)(2,1)S(1)} %bitcast.180), kind=kLoop, calls=%fused_computation.1 | loop fusion | flops 1474560 | bytes 5898240 | tf_op jit(solution)/shard_map/stack | solution.py:44
  161.9 7.1 %reshape.318 = bf16[1280,1152]{1,0:T(8,128)(2,1)} reshape(bf16[16,2,4,5,2,1152]{5,4,3,2,1,0:T(2,128)(2,1)} %pad_maximum_fusion.1) | data formatting | bytes 5898240 | tf_op jit(solution)/shard_map/reshape | solution.py:45
  169.0 1.5 fusion.17
  170.5 1.5 fusion.1
  172.0 1.5 fusion.2
  173.6 1.5 fusion
  179.1 1.4 fusion.34
  180.6 1.5 fusion.29
  182.0 1.2 fusion.164
  183.2 1.2 fusion.160
  184.4 1.4 convolution_add_fusion.22
  185.8 1.2 convolution_add_fusion.26
  187.0 1.6 fusion.123
  188.6 1.2 fusion.238
  189.8 1.2 fusion.293
  192.4 1.3 convolution_add_fusion.5
  194.1 1.3 convolution_add_fusion.2
  195.7 1.1 convolution_add_fusion.8
  197.1 1.1 convolution_add_fusion.11
  198.5 1.3 convolution_add_fusion.3
  199.8 1.3 convolution_add_fusion
  201.1 1.1 convolution_add_fusion.9
  202.3 1.9 fusion.171
  204.7 1.1 fusion.22
  205.8 1.6 convolution_add_fusion.14
  207.8 3.1 %psum.14 = f32[]{:T(128)} all-reduce(f32[]{:T(128)} %get-tuple-element.50), channel_id=1, replica_groups=mesh['x'=4,'ylo'=2,'z'=8,'core'=2,'yhi'=4] {'core'}, use_global_device_ids=true, to_apply=%region_42.43 | all-reduce | flops 1 | bytes 8 | tf_op jit(solution)/shard_map/psum | solution.py:154
  210.9 1.6 convolution_add_fusion.17
  212.5 1.5 convolution_add_fusion.16
  214.0 6.8 %psum.15 = f32[]{:T(128)} all-reduce(f32[]{:T(128)} %psum.14), channel_id=1, replica_groups=mesh['x'=4,'ylo'=2,'z'=8,'core'=2,'yhi'=4] {'x'}, use_global_device_ids=true, to_apply=%region_43.44 | all-reduce | flops 1 | bytes 8 | tf_op jit(solution)/shard_map/psum | solution.py:155
  220.8 1.3 broadcast_in_dim.14
  222.1 12.0 %all-to-all-start.2 = ((f32[64,1,128]{2,1,0:T(1,128)}), f32[64,1,128]{2,1,0:T(1,128)S(1)}, u32[]{:S(2)}, u32[]{:S(2)}) async-start(f32[64,1,128]{2,1,0:T(1,128)} %broadcast_in_dim.14), calls=%async_computation.2 | async-start | bytes 65536 | tf_op jit(solution)/shard_map/all_to_all | solution.py:157
  234.1 1.5 convolution_add_fusion.15
  235.6 1.5 select_convert_fusion.1
  237.9 6.7 %all-to-all-done.2 = f32[64,1,128]{2,1,0:T(1,128)S(1)} async-done(((f32[64,1,128]{2,1,0:T(1,128)}), f32[64,1,128]{2,1,0:T(1,128)S(1)}, u32[]{:S(2)}, u32[]{:S(2)}) %all-to-all-start.2) | async-done | bytes 32800 | tf_op jit(solution)/shard_map/all_to_all | solution.py:157
  (108 shorter events, 20.2 us)
Async XLA Ops:
  0.6 132.6 %copy-start = (bf16[128,1280]{1,0:T(8,128)(2,1)S(1)}, bf16[128,1280]{1,0:T(8,128)(2,1)}, u32[]{:S(2)}) copy-start(bf16[128,1280]{1,0:T(8,128)(2,1)} %param.10) | copy-start | bytes 983044
  5.9 58.7 %copy-start.13 = (bf16[4,128,384]{2,1,0:T(8,128)(2,1)S(1)}, bf16[4,128,384]{2,1,0:T(8,128)(2,1)}, u32[]{:S(2)}) copy-start(bf16[4,128,384]{2,1,0:T(8,128)(2,1)} %param.12) | copy-start | bytes 1179652
  5.9 58.9 %copy-start.14 = (bf16[4,128,64]{1,2,0:T(8,128)(2,1)S(1)}, bf16[4,128,64]{1,2,0:T(8,128)(2,1)}, u32[]{:S(2)}) copy-start(bf16[4,128,64]{1,2,0:T(8,128)(2,1)} %param.11) | copy-start | bytes 196612
  5.9 52.3 %all-to-all-start = ((bf16[64,5,2,1152]{3,2,1,0:T(2,128)(2,1)}), bf16[64,5,2,1152]{3,2,1,0:T(2,128)(2,1)S(1)}, u32[]{:S(2)}, u32[]{:S(2)}) async-start(bf16[64,5,2,1152]{3,2,1,0:T(2,128)(2,1)} %broadcast_in_dim.11), calls=%async_computation | async-start | bytes 2949120 | tf_op jit(solution)/shard_map/all_to_all | solution.py:33
  23.2 51.8 %copy-start.18 = (f32[256]{0:T(256)S(1)}, f32[256]{0:T(256)}, u32[]{:S(2)}) copy-start(f32[256]{0:T(256)} %param.13) | copy-start | bytes 3076
  23.2 51.9 %copy-start.19 = (s32[64]{0:T(128)S(1)}, s32[64]{0:T(128)}, u32[]{:S(2)}) copy-start(s32[64]{0:T(128)} %param.15) | copy-start | bytes 772
  58.2 29.1 %collective-permute-start.3 = (bf16[64,5,2,1152]{3,2,1,0:T(2,128)(2,1)S(1)}, bf16[64,5,2,1152]{3,2,1,0:T(2,128)(2,1)}, u32[]{:S(2)}, u32[]{:S(2)}) collective-permute-start(bf16[64,5,2,1152]{3,2,1,0:T(2,128)(2,1)S(1)} %all-to-all-done), channel_id=1, source_target_pairs={{0,4},{4,0},{1,5},{5,1},{2,6},{6,2},{3,7},{7,3},{8,12},{12,8},{9,1... | collective-permute-start | bytes 4423688 | tf_op jit(solution)/shard_map/ppermute | solution.py:37
  65.6 45.3 %collective-permute-start = (bf16[128,448]{0,1:T(8,128)(2,1)}, bf16[128,448]{0,1:T(8,128)(2,1)}, u32[]{:S(2)}, u32[]{:S(2)}) collective-permute-start(bf16[128,448]{0,1:T(8,128)(2,1)} %get-tuple-element.83), channel_id=1, source_target_pairs={{0,384},{128,0},{256,128},{384,256},{1,385},{129,1},{257,129},{385... | collective-permute-start | bytes 344072 | tf_op jit(solution)/shard_map/ppermute | solution.py:80
  70.0 41.8 %collective-permute-start.1 = (bf16[128,448]{0,1:T(8,128)(2,1)}, bf16[128,448]{0,1:T(8,128)(2,1)}, u32[]{:S(2)}, u32[]{:S(2)}) collective-permute-start(bf16[128,448]{0,1:T(8,128)(2,1)} %get-tuple-element.85), channel_id=1, source_target_pairs={{0,256},{128,384},{256,0},{384,128},{1,257},{129,385},{257,1},{385... | collective-permute-start | bytes 344072 | tf_op jit(solution)/shard_map/ppermute | solution.py:80
  72.4 40.4 %collective-permute-start.2 = (bf16[128,448]{0,1:T(8,128)(2,1)}, bf16[128,448]{0,1:T(8,128)(2,1)}, u32[]{:S(2)}, u32[]{:S(2)}) collective-permute-start(bf16[128,448]{0,1:T(8,128)(2,1)} %get-tuple-element.86), channel_id=1, source_target_pairs={{0,128},{128,256},{256,384},{384,0},{1,129},{129,257},{257,385},{3... | collective-permute-start | bytes 344072 | tf_op jit(solution)/shard_map/ppermute | solution.py:80
  80.2 41.9 %all-to-all-start.1 = ((bf16[64,5,2,1152]{3,2,1,0:T(2,128)(2,1)}), bf16[64,5,2,1152]{3,2,1,0:T(2,128)(2,1)}, u32[]{:S(2)}, u32[]{:S(2)}) async-start(bf16[64,5,2,1152]{3,2,1,0:T(2,128)(2,1)} %broadcast_in_dim.13), calls=%async_computation.1 | async-start | bytes 2949120 | tf_op jit(solution)/shard_map/all_to_all | solution.py:33
  102.7 8.1 %copy-start.15 = (f32[1536]{0:T(1024)S(1)}, f32[1536]{0:T(1024)}, u32[]{:S(2)}) copy-start(f32[1536]{0:T(1024)} %param.14) | copy-start | bytes 18436
  104.0 35.0 %collective-permute-start.4 = (bf16[640,1152]{1,0:T(8,128)(2,1)}, bf16[640,1152]{1,0:T(8,128)(2,1)}, u32[]{:S(2)}, u32[]{:S(2)}) collective-permute-start(bf16[640,1152]{1,0:T(8,128)(2,1)} %constant_dynamic-slice_fusion.7), channel_id=1, source_target_pairs={{0,384},{128,0},{256,128},{384,256},{1,385},{129,1},{257,129},{385... | collective-permute-start | bytes 4423688 | tf_op jit(solution)/shard_map/ppermute | solution.py:91
  108.0 35.8 %collective-permute-start.7 = (bf16[640,1152]{1,0:T(8,128)(2,1)}, bf16[640,1152]{1,0:T(8,128)(2,1)}, u32[]{:S(2)}, u32[]{:S(2)}) collective-permute-start(bf16[640,1152]{1,0:T(8,128)(2,1)} %constant_dynamic-slice_fusion.7), channel_id=1, source_target_pairs={{0,128},{128,256},{256,384},{384,0},{1,129},{129,257},{257,385},{3... | collective-permute-start | bytes 4423688 | tf_op jit(solution)/shard_map/ppermute | solution.py:92
  111.8 3.9 %copy-start.4 = (f32[128,448]{0,1:T(8,128)}, f32[128,448]{0,1:T(8,128)S(1)}, u32[]{:S(2)}) copy-start(f32[128,448]{0,1:T(8,128)S(1)} %convert_element_type.126) | copy-start | bytes 688132
  112.8 1.7 copy-start.6
  122.1 30.2 %collective-permute-start.6 = (bf16[64,5,2,1152]{3,2,1,0:T(2,128)(2,1)}, bf16[64,5,2,1152]{3,2,1,0:T(2,128)(2,1)S(1)}, u32[]{:S(2)}, u32[]{:S(2)}) collective-permute-start(bf16[64,5,2,1152]{3,2,1,0:T(2,128)(2,1)} %all-to-all-done.1), channel_id=1, source_target_pairs={{0,4},{4,0},{1,5},{5,1},{2,6},{6,2},{3,7},{7,3},{8,12},{12,8},{9,1... | collective-permute-start | bytes 4423688 | tf_op jit(solution)/shard_map/ppermute | solution.py:37
  139.0 33.0 %collective-permute-start.5 = (bf16[640,1152]{1,0:T(8,128)(2,1)}, bf16[640,1152]{1,0:T(8,128)(2,1)}, u32[]{:S(2)}, u32[]{:S(2)}) collective-permute-start(bf16[640,1152]{1,0:T(8,128)(2,1)} %collective-permute-done.4), channel_id=1, source_target_pairs={{0,4},{4,0},{1,5},{5,1},{2,6},{6,2},{3,7},{7,3},{8,12},{12,8},{9,1... | collective-permute-start | bytes 4423688 | tf_op jit(solution)/shard_map/ppermute | solution.py:37
  143.8 29.8 %collective-permute-start.8 = (bf16[640,1152]{1,0:T(8,128)(2,1)}, bf16[640,1152]{1,0:T(8,128)(2,1)}, u32[]{:S(2)}, u32[]{:S(2)}) collective-permute-start(bf16[640,1152]{1,0:T(8,128)(2,1)} %collective-permute-done.7), channel_id=1, source_target_pairs={{0,4},{4,0},{1,5},{5,1},{2,6},{6,2},{3,7},{7,3},{8,12},{12,8},{9,1... | collective-permute-start | bytes 4423688 | tf_op jit(solution)/shard_map/ppermute | solution.py:37
  169.0 3.1 %copy-start.11 = (f32[128,640]{1,0:T(8,128)S(1)}, f32[128,640]{1,0:T(8,128)}, u32[]{:S(2)}) copy-start(f32[128,640]{1,0:T(8,128)} %fusion.12) | copy-start | bytes 983044
  170.5 3.1 %copy-start.10 = (f32[128,640]{1,0:T(8,128)S(1)}, f32[128,640]{1,0:T(8,128)}, u32[]{:S(2)}) copy-start(f32[128,640]{1,0:T(8,128)} %fusion.7) | copy-start | bytes 983044
  172.0 3.0 %copy-start.9 = (f32[1,128,640]{2,1,0:T(8,128)S(1)}, f32[1,128,640]{2,1,0:T(8,128)}, u32[]{:S(2)}) copy-start(f32[1,128,640]{2,1,0:T(8,128)} %fusion.3) | copy-start | bytes 983044
  175.1 1.8 copy-start.1
  180.5 6.4 %copy-start.5 = (f32[128,448]{0,1:T(8,128)S(1)}, f32[128,448]{0,1:T(8,128)}, u32[]{:S(2)}) copy-start(f32[128,448]{0,1:T(8,128)} %copy-done.4) | copy-start | bytes 688132
  180.5 6.4 %copy-start.7 = (f32[128,448]{0,1:T(8,128)S(1)}, f32[128,448]{0,1:T(8,128)}, u32[]{:S(2)}) copy-start(f32[128,448]{0,1:T(8,128)} %copy-done.6) | copy-start | bytes 688132
  180.5 6.4 %copy-start.8 = (f32[128,448]{0,1:T(8,128)S(1)}, f32[128,448]{0,1:T(8,128)}, u32[]{:S(2)}) copy-start(f32[128,448]{0,1:T(8,128)} %convert_element_type.128) | copy-start | bytes 688132
  180.6 6.4 %copy-start.16 = (f32[128]{0:T(128)S(1)}, f32[128]{0:T(128)}, u32[]{:S(2)}) copy-start(f32[128]{0:T(128)} %get-tuple-element.67) | copy-start | bytes 1540
  180.6 6.4 %copy-start.17 = (f32[128]{0:T(128)S(1)}, f32[128]{0:T(128)}, u32[]{:S(2)}) copy-start(f32[128]{0:T(128)} %get-tuple-element.68) | copy-start | bytes 1540
  204.3 3.0 %copy-start.2 = (bf16[4,128,640]{2,1,0:T(8,128)(2,1)}, bf16[4,128,640]{2,1,0:T(8,128)(2,1)S(1)}, u32[]{:S(2)}) copy-start(bf16[4,128,640]{2,1,0:T(8,128)(2,1)S(1)} %pad_maximum_fusion.4) | copy-start | bytes 1966084
  205.8 5.1 %copy-start.12 = (f32[128,640]{1,0:T(8,128)S(1)}, f32[128,640]{1,0:T(8,128)}, u32[]{:S(2)}) copy-start(f32[128,640]{1,0:T(8,128)} %fusion.22) | copy-start | bytes 983044
  207.8 4.7 %copy-start.3 = (bf16[4,128,640]{2,1,0:T(8,128)(2,1)S(1)}, bf16[4,128,640]{2,1,0:T(8,128)(2,1)}, u32[]{:S(2)}) copy-start(bf16[4,128,640]{2,1,0:T(8,128)(2,1)} %copy-done.2) | copy-start | bytes 1966084
  222.1 22.5 %all-to-all-start.2 = ((f32[64,1,128]{2,1,0:T(1,128)}), f32[64,1,128]{2,1,0:T(1,128)S(1)}, u32[]{:S(2)}, u32[]{:S(2)}) async-start(f32[64,1,128]{2,1,0:T(1,128)} %broadcast_in_dim.14), calls=%async_computation.2 | async-start | bytes 65536 | tf_op jit(solution)/shard_map/all_to_all | solution.py:157

commit v2 on v0

v2 whole, which is shorter than its diff:
```python
import functools

import jax
import jax.numpy as jnp
from jax import lax
from jax.experimental import pallas as pl
from jax.experimental.pallas import tpu as pltpu
from jax.sharding import Mesh, PartitionSpec as P

IMG_TOK = 1024
AXES = ("x", "ylo", "z", "core", "yhi")
PLANE = ("ylo", "z", "yhi")
HALF = 640
DINO_Q = 384
SAM_Q = 64
OUT_Q = 512
COLS = HALF + OUT_Q
S_AT = HALF + DINO_Q
F32 = jnp.float32
BF16 = jnp.bfloat16
VMEM_LIMIT = 56 * 1024 * 1024


def ring(n, shift):
    return [(i, (i + shift) % n) for i in range(n)]


def dot(a, b):
    return jnp.dot(a, b, preferred_element_type=F32)


def dot_t(a, b):
    return lax.dot_general(a, b, (((1,), (1,)), ((), ())), preferred_element_type=F32)


def pick_cols(half):
    source = lax.broadcasted_iota(jnp.int32, (2 * HALF, HALF), 0)
    at = lax.broadcasted_iota(jnp.int32, (2 * HALF, HALF), 1)
    return (source == (at // 40) * 80 + half * 40 + at % 40).astype(BF16)


def gelu_slope(v):
    c = 0.7978845608028654
    t = jnp.tanh(c * (v + 0.044715 * (v * v * v)))
    return 0.5 * (1.0 + t) + 0.5 * v * (1.0 - t * t) * (c * (1.0 + 3.0 * 0.044715 * (v * v)))


def forward_kernel(
    where, tok_m, tok_o, pre0, pre1, pre3, goal, tt, live,
    m0, o0, m1, o1, m2, o2, m3, o3,
    pred, pre2, score, part, act,
):
    x, core = where[0], where[1]
    pre2[...] = dot(tok_m[...], m2[:, :HALF]) + dot(tok_o[...], o2[:, :HALF])
    for j, ref in enumerate((pre0, pre1, pre2, pre3)):
        act[lax.rem(x + j, 4)] = jax.nn.gelu(ref[...]).astype(BF16)
    sm, so = act[core], act[1 - core]
    dm, do = act[2 + core], act[3 - core]
    slots = ((m0, o0), (m1, o1), (m2, o2), (m3, o3))
    pp = [0.0, 0.0]
    pt = [0.0, 0.0]
    for j, (m, o) in enumerate(slots):
        for head, (am, ao, lo, hi) in enumerate(((sm, so, DINO_Q, OUT_Q), (dm, do, 0, DINO_Q))):
            value = dot(am, m[:, HALF + lo:HALF + hi]) + dot(ao, o[:, HALF + lo:HALF + hi])
            pred[j, :, lo:hi] = value
            aim = goal[j, :, lo:hi].astype(F32)
            pp[head] += jnp.sum(value * value, axis=1, keepdims=True)
            pt[head] += jnp.sum(value * aim, axis=1, keepdims=True)
    total = 0.0
    for head, chans in enumerate((4 * SAM_Q, 4 * DINO_Q)):
        mean = pp[head] / chans + 1e-05
        inv_root = lax.rsqrt(mean * tt[:, head:head + 1])
        cosine = pt[head] / chans * inv_root
        score[:, 2 * head:2 * head + 1] = inv_root
        score[:, 2 * head + 1:2 * head + 2] = cosine / mean
        total += cosine
    part[...] = jnp.sum(live[...] * (2.0 - total), axis=0, keepdims=True) + jnp.zeros((1, 128), F32)


def backward_kernel(
    where, pred, goal, score, scale, pre0, pre1, pre2, pre3,
    m0, o0, m1, o1, m2, o2, m3, o3,
    grad, pre, hid,
):
    x, core = where[0], where[1]
    for j, ref in enumerate((pre0, pre1, pre2, pre3)):
        pre[lax.rem(x + j, 4)] = ref[...]
    slots = ((m0, o0), (m1, o1), (m2, o2), (m3, o3))
    sums = [[0.0, 0.0], [0.0, 0.0]]
    for j, (m, o) in enumerate(slots):
        for head, (lo, hi, chans) in enumerate(((DINO_Q, OUT_Q, 4 * SAM_Q), (0, DINO_Q, 4 * DINO_Q))):
            aim = goal[j, :, lo:hi].astype(F32)
            inv_root = score[:, 2 * head:2 * head + 1]
            ratio = score[:, 2 * head + 1:2 * head + 2]
            back = (-scale[...] * (aim * inv_root - ratio * pred[j, :, lo:hi]) / chans).astype(BF16)
            sums[head][0] += dot_t(back, m[:, HALF + lo:HALF + hi])
            sums[head][1] += dot_t(back, o[:, HALF + lo:HALF + hi])
    for head in range(2):
        for side in range(2):
            at = 2 * head + (core if side == 0 else 1 - core)
            hid[at] = (sums[head][side] * gelu_slope(pre[at])).astype(BF16)
    for side in range(2):
        total = 0.0
        for j, pair in enumerate(slots):
            total += dot_t(hid[lax.rem(x + j, 4)], pair[side][:, :HALF])
        grad[core if side == 0 else 1 - core] = total.astype(BF16)


def shards(
    student_tokens,
    sam_maps,
    dino_maps,
    sam_gain,
    dino_gain,
    patch_counts,
    sam_in,
    sam_out,
    dino_in,
    dino_out,
):
    rows = student_tokens.shape[0]
    x = lax.axis_index("x")
    core = lax.axis_index("core")
    shard = sam_in.shape[0]

    both = jnp.concatenate([sam_in, dino_in], axis=0)
    picked = dot(both, pick_cols(x % 2)).astype(BF16).reshape(2, shard, HALF)
    sam4 = sam_out.reshape(shard, 4, SAM_Q)

    def payload(q):
        part_in = lax.dynamic_index_in_dim(picked, q // 2, axis=0, keepdims=False)
        part_d = lax.dynamic_slice(dino_out, (0, q * DINO_Q), (shard, DINO_Q))
        part_s = lax.dynamic_index_in_dim(sam4, q, axis=1, keepdims=False)
        pad = jnp.zeros((shard, COLS - S_AT - SAM_Q), BF16)
        part = jnp.concatenate([part_in, part_d, part_s, pad], axis=1)
        return jnp.broadcast_to(part.reshape(1, shard // 2, 2, COLS), (64, shard // 2, 2, COLS))

    def gather_plane(many):
        got = lax.all_to_all(many, PLANE, split_axis=0, concat_axis=0, tiled=True)
        return got

    own_b, opp_b, feats = lax.optimization_barrier(
        (payload(x), payload((x + 2) % 4), jnp.concatenate(
            [dino_maps, sam_maps, jnp.zeros((4, rows, OUT_Q - DINO_Q - SAM_Q), BF16)], axis=2)))

    def feat_for(slot):
        return lax.dynamic_index_in_dim(feats, (x - slot) % 4, axis=0, keepdims=False)

    got = [feat_for(0)] + [lax.ppermute(feat_for(s), "x", ring(4, -s)) for s in (1, 2, 3)]
    tok_m = dot(student_tokens, pick_cols(core)).astype(BF16)
    tok_o = dot(student_tokens, pick_cols(1 - core)).astype(BF16)

    own_g = gather_plane(own_b)
    own_g, got, tok_m, tok_o = lax.optimization_barrier((own_g, got, tok_m, tok_o))
    opp_b, own_g = lax.optimization_barrier((opp_b, own_g))
    opp_g = gather_plane(opp_b)

    own = own_g.reshape(HALF, COLS)
    next_m = lax.ppermute(own, "x", ring(4, -1))
    prev_m = lax.ppermute(own, "x", ring(4, 1))

    def swap(value):
        return lax.ppermute(value, "core", ring(2, 1))

    opp = opp_g.reshape(HALF, COLS)
    slots = [(w, swap(w)) for w in (own, next_m, opp, prev_m)]

    def gain_of(slot):
        q = (x + slot) % 4
        d = lax.dynamic_slice(dino_gain, (q * DINO_Q,), (DINO_Q,))
        s = lax.dynamic_slice(sam_gain, (q * SAM_Q,), (SAM_Q,))
        return jnp.concatenate([d, s, jnp.zeros((OUT_Q - DINO_Q - SAM_Q,), F32)])

    feat = jnp.stack(got).astype(F32)
    gain = jnp.stack([gain_of(j) for j in range(4)])[:, None, :]

    def targets(part, weight):
        chans = 4 * (DINO_Q if part.shape[2] == DINO_Q else SAM_Q)
        center = jnp.sum(part, axis=(0, 2), keepdims=True) / chans
        spread = jnp.sum(part * part, axis=(0, 2), keepdims=True) / chans - center * center
        value = ((part - center) * lax.rsqrt(spread + 1e-06) * weight).astype(BF16)
        wide = value.astype(F32)
        return value, jnp.sum(wide * wide, axis=(0, 2))[:, None] / chans + 1e-05

    goal_d, tt_d = targets(feat[:, :, :DINO_Q], gain[:, :, :DINO_Q])
    goal_s, tt_s = targets(feat[:, :, DINO_Q:], gain[:, :, DINO_Q:])
    goal = jnp.concatenate([goal_d, goal_s], axis=2)
    tt = jnp.concatenate([tt_s, tt_d], axis=1)

    start = lax.axis_index(AXES) * rows
    limit = lax.dynamic_index_in_dim(patch_counts, start // IMG_TOK, keepdims=False)
    slot_at = start % IMG_TOK + jnp.arange(rows, dtype=jnp.int32)
    live = (slot_at < limit).astype(F32)[:, None]
    count = jnp.sum(jnp.clip(patch_counts, 0, IMG_TOK)).astype(F32)

    pre = {j: dot(tok_m, slots[j][0][:, :HALF]) + dot(tok_o, slots[j][1][:, :HALF]) for j in (0, 1, 3)}
    goal, tt, live, pre = lax.optimization_barrier((goal, tt, live, pre))
    place = jnp.stack([x, core]).astype(jnp.int32)
    flat = [w for pair in slots for w in pair]
    in_vmem = pl.BlockSpec(memory_space=pltpu.VMEM)
    in_smem = pl.BlockSpec(memory_space=pltpu.SMEM)
    pred, pre2, score, part = pl.pallas_call(
        forward_kernel,
        out_shape=(
            jax.ShapeDtypeStruct((4, rows, OUT_Q), F32),
            jax.ShapeDtypeStruct((rows, HALF), F32),
            jax.ShapeDtypeStruct((rows, 4), F32),
            jax.ShapeDtypeStruct((1, 128), F32),
        ),
        in_specs=[in_smem] + [in_vmem] * 16,
        out_specs=(in_vmem,) * 4,
        scratch_shapes=[pltpu.VMEM((4, rows, HALF), BF16)],
        compiler_params=pltpu.CompilerParams(vmem_limit_bytes=VMEM_LIMIT),
        name="forward",
    )(place, tok_m, tok_o, pre[0], pre[1], pre[3], goal, tt, live, *flat)

    local = lax.psum(lax.psum(part[0, 0], "core"), "x")
    spread_out = jnp.broadcast_to(local, (64, 1, 128))
    all_parts = lax.all_to_all(spread_out, PLANE, split_axis=0, concat_axis=0, tiled=True)
    loss = jnp.sum(all_parts[:, 0, 0]) / count

    grad = pl.pallas_call(
        backward_kernel,
        out_shape=jax.ShapeDtypeStruct((2, rows, HALF), BF16),
        in_specs=[in_smem] + [in_vmem] * 16,
        out_specs=in_vmem,
        scratch_shapes=[pltpu.VMEM((4, rows, HALF), F32), pltpu.VMEM((4, rows, HALF), BF16)],
        compiler_params=pltpu.CompilerParams(vmem_limit_bytes=VMEM_LIMIT),
        name="backward",
    )(place, pred, goal, score, live / count, pre[0], pre[1], pre2, pre[3], *flat)
    grad = dot_t(grad[0], pick_cols(0)) + dot_t(grad[1], pick_cols(1))
    return (grad.astype(BF16), loss)


def solution(mesh):
    fine = Mesh(mesh.devices.reshape(4, 2, 8, 2, 4), AXES)
    tokens = P(AXES, None)
    rest = ("ylo", "z", "core", "yhi")
    return jax.shard_map(
        shards,
        mesh=fine,
        in_specs=(
            tokens,
            P(None, rest, "x"),
            P(None, rest, "x"),
            P(),
            P(),
            P(),
            P(rest, None),
            P(rest, None),
            P(rest, None),
            P(rest, None),
        ),
        out_specs=(tokens, P()),
        check_vma=False,
    )
```

time: 1270 us -> 195 us (0.15)
  waiting for transfers between devices: 836 us -> 52 us
  blocking collectives: 361 us -> 12.1 us
  starting transfers between devices: 9.18 us -> 68.2 us
  Pallas kernels: 0 us -> 18.7 us
  between operations: 17 us -> 3.83 us
    all_gather x3 -> x0, waiting for transfers between devices: 828 us -> none  [the longest x1 364 us: shards(): lax.all_gather(dino_in, ('dp', 'fsdp'), axis=0, tiled=True)]
    all_gather x1 -> x0, blocking collectives: 258 us -> none  [shards(): lax.all_gather(sam_out, ('dp', 'fsdp'), axis=0, tiled=True)]
    psum x1 -> x2, blocking collectives: 103 us -> 12.1 us  [shards(): local = lax.psum(lax.psum(part[0, 0], 'core'), 'x')]
    all_to_all x2 -> x3, starting transfers between devices: 9.07 us -> 39.4 us  [the longest x2 27.4 us: gather_plane(): got = lax.all_to_all(many, PLANE, split_axis=0, concat_axis=0, tiled=True)]
    ppermute x0 -> x9, starting transfers between devices: none -> 28.9 us  [the longest x4 13.1 us: swap(): return lax.ppermute(value, 'core', ring(2, 1))]
    ppermute x0 -> x9, waiting for transfers between devices: none -> 24.2 us  [the longest x1 22.7 us: shards(): prev_m = lax.ppermute(own, 'x', ring(4, 1))]
    all_to_all x2 -> x3, waiting for transfers between devices: 5.88 us -> 27.8 us  [the longest x2 18.8 us: gather_plane(): got = lax.all_to_all(many, PLANE, split_axis=0, concat_axis=0, tiled=True)]
    unnamed x17 -> x43, local copies, waits for them, and re-layouts: 21.9 us -> 0.23 us
  transfers between devices with their start and end apart: 5 -> 12, of which waited for: 4 -> 4; matrix products, arithmetic and copies ran while one was open for 2% -> 14% of each run, Pallas kernels for 0% -> 0%
where the time goes in v2:
time: 195 us; the launch traced here: 192 us
  starting transfers between devices  68.2 us (35%)
  waiting for transfers between devices  52 us (27%)
  Pallas kernels  18.7 us (10%)
  matrix products  17.5 us (9%)
  local copies, waits for them, and re-layouts  13.6 us (7%)
  blocking collectives  12.1 us (6%)
  other arithmetic  6.45 us (3%)
  between operations  3.83 us (2%)
    all_to_all x2, starting transfers between devices, gather_plane(): got = lax.all_to_all(many, PLANE, split_axis=0, concat_axis=0, tiled=True)  27.4 us
    ppermute x1, waiting for transfers between devices, shards(): prev_m = lax.ppermute(own, 'x', ring(4, 1))  22.7 us
    all_to_all x2, waiting for transfers between devices, gather_plane(): got = lax.all_to_all(many, PLANE, split_axis=0, concat_axis=0, tiled=True)  18.8 us
    dot_general x9, matrix products, dot(): return jnp.dot(a, b, preferred_element_type=F32)  14.3 us
    ppermute x4, starting transfers between devices, swap(): return lax.ppermute(value, 'core', ring(2, 1))  13.1 us
    psum x2, blocking collectives, shards(): local = lax.psum(lax.psum(part[0, 0], 'core'), 'x')  12.1 us
    all_to_all x1, starting transfers between devices, shards(): lax.all_to_all(spread_out, PLANE, split_axis=0, concat_axis=0, tiled=True)  12 us
    pallas_call x1, Pallas kernels, shards(): pl.pallas_call(backward_kernel, out_shape=jax.ShapeDtypeStruct((2, rows,...  10.5 us
  transfers between devices with their start and end apart: 12, of which 4 were waited for; matrix products, arithmetic and copies ran while one was open for 14% of the time, Pallas kernels for 0%

profile of v2, /device:TPU:1, one launch (start us, length us, event | category | flops | bytes accessed | tf_op | source)
XLA Modules:
  0.0 192.4 jit_solution(11958488324589097092)
XLA Ops:
  0.6 0.0 copy-start
  0.8 0.8 reshape.112
  1.5 0.1 dynamic-slice_reduce_fusion
  1.6 0.7 constant_dynamic-slice_fusion
  2.4 1.5 fusion.72
  4.1 0.1 copy.38
  4.2 0.1 pad.26.clone
  4.3 0.1 concatenate.55
  4.4 0.1 concatenate.51
  4.5 0.1 maximum_maximum_fusion
  4.6 1.9 broadcast_in_dim.33
  6.5 1.9 broadcast_in_dim.15
  8.4 17.3 %all-to-all-start = ((bf16[64,5,2,1152]{3,2,1,0:T(2,128)(2,1)}), bf16[64,5,2,1152]{3,2,1,0:T(2,128)(2,1)S(1)}, u32[]{:S(2)}, u32[]{:S(2)}) async-start(bf16[64,5,2,1152]{3,2,1,0:T(2,128)(2,1)} %broadcast_in_dim.15), calls=%async_computation | async-start | bytes 2949120 | tf_op jit(solution)/shard_map/all_to_all | solution.py:139
  25.8 0.7 dynamic-slice_bitcast_fusion
  26.5 4.4 %collective-permute-start = (bf16[128,512]{1,0:T(8,128)(2,1)S(1)}, bf16[128,512]{1,0:T(8,128)(2,1)S(1)}, u32[]{:S(2)}, u32[]{:S(2)}) collective-permute-start(bf16[128,512]{1,0:T(8,128)(2,1)S(1)} %get-tuple-element.59), channel_id=1, source_target_pairs={{0,384},{128,0},{256,128},{384,256},{1,385},{129,1},{257,129},{385... | collective-permute-start | bytes 393224 | tf_op jit(solution)/shard_map/ppermute | solution.py:149
  30.8 2.4 %collective-permute-start.1 = (bf16[128,512]{1,0:T(8,128)(2,1)S(1)}, bf16[128,512]{1,0:T(8,128)(2,1)S(1)}, u32[]{:S(2)}, u32[]{:S(2)}) collective-permute-start(bf16[128,512]{1,0:T(8,128)(2,1)S(1)} %get-tuple-element.58), channel_id=1, source_target_pairs={{0,256},{128,384},{256,0},{384,128},{1,257},{129,385},{257,1},{385... | collective-permute-start | bytes 393224 | tf_op jit(solution)/shard_map/ppermute | solution.py:149
  33.3 2.5 %collective-permute-start.2 = (bf16[128,512]{1,0:T(8,128)(2,1)S(1)}, bf16[128,512]{1,0:T(8,128)(2,1)S(1)}, u32[]{:S(2)}, u32[]{:S(2)}) collective-permute-start(bf16[128,512]{1,0:T(8,128)(2,1)S(1)} %get-tuple-element.57), channel_id=1, source_target_pairs={{0,128},{128,256},{256,384},{384,0},{1,129},{129,257},{257,385},{3... | collective-permute-start | bytes 393224 | tf_op jit(solution)/shard_map/ppermute | solution.py:149
  35.9 0.1 fusion.107
  36.0 0.1 fusion.106
  36.1 0.1 pad_maximum_fusion.5
  36.1 0.8 fusion.66.tok_o
  36.9 0.0 copy-start.20
  36.9 1.4 fusion.69.tok_m
  38.3 0.7 clamp_reduce_fusion
  39.0 0.7 dynamic_slice.79
  40.4 1.5 collective-permute-done.2
  41.9 18.8 %all-to-all-done = bf16[64,5,2,1152]{3,2,1,0:T(2,128)(2,1)S(1)} async-done(((bf16[64,5,2,1152]{3,2,1,0:T(2,128)(2,1)}), bf16[64,5,2,1152]{3,2,1,0:T(2,128)(2,1)S(1)}, u32[]{:S(2)}, u32[]{:S(2)}) %all-to-all-start) | async-done | bytes 1474592 | tf_op jit(solution)/shard_map/all_to_all | solution.py:139
  60.7 10.1 %all-to-all-start.1 = ((bf16[64,5,2,1152]{3,2,1,0:T(2,128)(2,1)}), bf16[64,5,2,1152]{3,2,1,0:T(2,128)(2,1)}, u32[]{:S(2)}, u32[]{:S(2)}) async-start(bf16[64,5,2,1152]{3,2,1,0:T(2,128)(2,1)} %broadcast_in_dim.33), calls=%async_computation.1 | async-start | bytes 2949120 | tf_op jit(solution)/shard_map/all_to_all | solution.py:139
  70.8 0.6 pad_add_fusion.where
  71.4 0.7 fusion.88.live
  72.2 0.6 reshape.113.m0
  72.8 3.1 %collective-permute-start.6 = (bf16[640,1152]{1,0:T(8,128)(2,1)S(1)}, bf16[640,1152]{1,0:T(8,128)(2,1)}, u32[]{:S(2)}, u32[]{:S(2)}) collective-permute-start(bf16[640,1152]{1,0:T(8,128)(2,1)S(1)} %reshape.113.m0), channel_id=1, source_target_pairs={{0,128},{128,256},{256,384},{384,0},{1,129},{129,257},{257,385},{3... | collective-permute-start | bytes 4423688 | tf_op jit(solution)/shard_map/ppermute | solution.py:160
  75.9 3.4 %collective-permute-start.4 = (bf16[640,1152]{1,0:T(8,128)(2,1)S(1)}, bf16[640,1152]{1,0:T(8,128)(2,1)}, u32[]{:S(2)}, u32[]{:S(2)}) collective-permute-start(bf16[640,1152]{1,0:T(8,128)(2,1)S(1)} %reshape.113.m0), channel_id=1, source_target_pairs={{0,384},{128,0},{256,128},{384,256},{1,385},{129,1},{257,129},{385... | collective-permute-start | bytes 4423688 | tf_op jit(solution)/shard_map/ppermute | solution.py:159
  79.3 4.0 %collective-permute-start.3 = (bf16[640,1152]{1,0:T(8,128)(2,1)S(1)}, bf16[640,1152]{1,0:T(8,128)(2,1)}, u32[]{:S(2)}, u32[]{:S(2)}) collective-permute-start(bf16[640,1152]{1,0:T(8,128)(2,1)S(1)} %reshape.113.m0), channel_id=1, source_target_pairs={{0,4},{4,0},{1,5},{5,1},{2,6},{6,2},{3,7},{7,3},{8,12},{12,8},{9,1... | collective-permute-start | bytes 4423688 | tf_op jit(solution)/shard_map/ppermute | solution.py:163
  83.4 0.0 copy-start.7
  83.4 1.2 maximum_convert_fusion
  84.7 0.2 slice_reduce_fusion
  84.8 0.3 multiply_reduce_fusion
  85.2 0.1 convert_reduce_fusion
  85.3 0.2 multiply_reduce_fusion.2
  85.5 22.7 %collective-permute-done.6.m3 = bf16[640,1152]{1,0:T(8,128)(2,1)} collective-permute-done((bf16[640,1152]{1,0:T(8,128)(2,1)S(1)}, bf16[640,1152]{1,0:T(8,128)(2,1)}, u32[]{:S(2)}, u32[]{:S(2)}) %collective-permute-start.6) | collective-permute-done | bytes 1474592 | tf_op jit(solution)/shard_map/ppermute | solution.py:160
  108.2 4.4 %collective-permute-start.7 = (bf16[640,1152]{1,0:T(8,128)(2,1)}, bf16[640,1152]{1,0:T(8,128)(2,1)}, u32[]{:S(2)}, u32[]{:S(2)}) collective-permute-start(bf16[640,1152]{1,0:T(8,128)(2,1)} %collective-permute-done.6.m3), channel_id=1, source_target_pairs={{0,4},{4,0},{1,5},{5,1},{2,6},{6,2},{3,7},{7,3},{8,12},{12,8},{9,1... | collective-permute-start | bytes 4423688 | tf_op jit(solution)/shard_map/ppermute | solution.py:163
  112.6 1.9 collective-permute-start.5
  114.6 0.9 pad_maximum_fusion.goal
  115.5 2.2 %fusion.76 = f32[128,640]{1,0:T(8,128)} fusion(bf16[128,640]{1,0:T(8,128)(2,1)S(1)} %copy-done.4, bf16[640,1152]{1,0:T(8,128)(2,1)} %collective-permute-done.6.m3), kind=kOutput, calls=%fused_computation.66 | convolution fusion | flops 104857600 | bytes 1310720 | tf_op jit(solution)/shard_map/dot_general | solution.py:29
  117.6 3.5 %reshape.114.m2 = bf16[640,1152]{1,0:T(8,128)(2,1)S(1)} reshape(bf16[64,5,2,1152]{3,2,1,0:T(2,128)(2,1)} %all-to-all-done.1) | data formatting | bytes 2949120 | tf_op jit(solution)/shard_map/reshape | solution.py:165
  121.2 2.7 %collective-permute-start.8 = (bf16[640,1152]{1,0:T(8,128)(2,1)S(1)}, bf16[640,1152]{1,0:T(8,128)(2,1)}, u32[]{:S(2)}, u32[]{:S(2)}) collective-permute-start(bf16[640,1152]{1,0:T(8,128)(2,1)S(1)} %reshape.114.m2), channel_id=1, source_target_pairs={{0,4},{4,0},{1,5},{5,1},{2,6},{6,2},{3,7},{7,3},{8,12},{12,8},{9,1... | collective-permute-start | bytes 4423688 | tf_op jit(solution)/shard_map/ppermute | solution.py:163
  123.9 1.5 fusion.79
  125.5 1.5 fusion.81
  127.0 1.0 convolution_add_fusion.2.pre0
  128.0 2.2 %convolution_add_fusion.pre3 = f32[128,640]{1,0:T(8,128)} fusion(f32[128,640]{1,0:T(8,128)S(1)} %copy-done.6, bf16[128,640]{1,0:T(8,128)(2,1)S(1)} %fusion.66.tok_o, bf16[640,1152]{1,0:T(8,128)(2,1)} %collective-permute-done.7.o3), kind=kOutput, calls=%fused_computation.57 | convolution fusion | flops 104939520 | bytes 1638400 | tf_op jit(solution)/shard_map/dot_general | solution.py:29
  130.2 2.2 %convolution_add_fusion.1.pre1 = f32[128,640]{1,0:T(8,128)} fusion(f32[128,640]{1,0:T(8,128)S(1)} %fusion.79, bf16[128,640]{1,0:T(8,128)(2,1)S(1)} %fusion.66.tok_o, bf16[640,1152]{1,0:T(8,128)(2,1)} %collective-permute-done.5.o1), kind=kOutput, calls=%fused_computation.58 | convolution fusion | flops 104939520 | bytes 1638400 | tf_op jit(solution)/shard_map/dot_general | solution.py:29
  132.4 0.7 copy.41.tt
  133.1 0.6 broadcast_divide_fusion.scale
  133.8 8.2 %forward.1 = (f32[4,128,512]{2,1,0:T(8,128)}, f32[128,640]{1,0:T(8,128)}, f32[128,4]{1,0:T(8,128)}, f32[1,128]{1,0:T(1,128)}) custom-call(s32[2]{0:T(128)} %pad_add_fusion.where, bf16[128,640]{1,0:T(8,128)(2,1)} %fusion.69.tok_m, bf16[128,640]{1,0:T(8,128)(2,1)} %copy-done.3, f32[128,640]{1,0:T(8,128)} %convolution_add_fusion.2.pre0, ...), custom_call_target="tpu_custom_call" | custom-call | tf_op jit(solution)/shard_map/forward/pallas_call | solution.py:202
  141.9 3.1 %psum.14 = f32[]{:T(128)} all-reduce(f32[]{:T(128)} %bitcast.65), channel_id=1, replica_groups=mesh['x'=4,'ylo'=2,'z'=8,'core'=2,'yhi'=4] {'core'}, use_global_device_ids=true, to_apply=%region_7.8 | all-reduce | flops 1 | bytes 8 | tf_op jit(solution)/shard_map/psum | solution.py:217
  145.0 10.5 %backward.1 = bf16[2,128,640]{2,1,0:T(8,128)(2,1)} custom-call(s32[2]{0:T(128)} %pad_add_fusion.where, f32[4,128,512]{2,1,0:T(8,128)} %get-tuple-element.42.pred, bf16[4,128,512]{2,1,0:T(8,128)(2,1)} %pad_maximum_fusion.goal, f32[128,4]{1,0:T(8,128)} %get-tuple-element.43.score, f32[128,1]{1,0:T(8,128)} %broadcast_divide_fusion.scale, ...), custom_call_target="tpu_custom_call" | custom-call | tf_op jit(solution)/shard_map/backward/pallas_call | solution.py:222
  155.6 1.7 fusion.5
  157.3 9.0 %psum.15 = f32[]{:T(128)} all-reduce(f32[]{:T(128)} %psum.14), channel_id=1, replica_groups=mesh['x'=4,'ylo'=2,'z'=8,'core'=2,'yhi'=4] {'x'}, use_global_device_ids=true, to_apply=%region_8.9 | all-reduce | flops 1 | bytes 8 | tf_op jit(solution)/shard_map/psum | solution.py:217
  166.2 1.3 broadcast_in_dim.36
  167.5 12.0 %all-to-all-start.2 = ((f32[64,1,128]{2,1,0:T(1,128)}), f32[64,1,128]{2,1,0:T(1,128)S(1)}, u32[]{:S(2)}, u32[]{:S(2)}) async-start(f32[64,1,128]{2,1,0:T(1,128)} %broadcast_in_dim.36), calls=%async_computation.2 | async-start | bytes 65536 | tf_op jit(solution)/shard_map/all_to_all | solution.py:219
  179.5 1.5 fusion.18
  181.0 9.0 %all-to-all-done.2 = f32[64,1,128]{2,1,0:T(1,128)S(1)} async-done(((f32[64,1,128]{2,1,0:T(1,128)}), f32[64,1,128]{2,1,0:T(1,128)S(1)}, u32[]{:S(2)}, u32[]{:S(2)}) %all-to-all-start.2) | async-done | bytes 32800 | tf_op jit(solution)/shard_map/all_to_all | solution.py:219
  190.0 0.7 slice_reduce_fusion.1
  (69 shorter events, 0.3 us)
Async XLA Ops:
  0.6 35.5 %copy-start = (bf16[128,1280]{1,0:T(8,128)(2,1)S(1)}, bf16[128,1280]{1,0:T(8,128)(2,1)}, u32[]{:S(2)}) copy-start(bf16[128,1280]{1,0:T(8,128)(2,1)} %param.10) | copy-start | bytes 983044
  2.4 1.7 copy-start.17
  2.4 2.1 %copy-start.15 = (bf16[4,128,384]{2,1,0:T(8,128)(2,1)S(1)}, bf16[4,128,384]{2,1,0:T(8,128)(2,1)}, u32[]{:S(2)}) copy-start(bf16[4,128,384]{2,1,0:T(8,128)(2,1)} %param.12) | copy-start | bytes 1179652
  8.4 27.5 %copy-start.19 = (f32[256]{0:T(256)S(1)}, f32[256]{0:T(256)}, u32[]{:S(2)}) copy-start(f32[256]{0:T(256)} %param.13) | copy-start | bytes 3076
  8.4 27.6 %copy-start.18 = (f32[1536]{0:T(1024)S(1)}, f32[1536]{0:T(1024)}, u32[]{:S(2)}) copy-start(f32[1536]{0:T(1024)} %param.14) | copy-start | bytes 18436
  8.4 52.3 %all-to-all-start = ((bf16[64,5,2,1152]{3,2,1,0:T(2,128)(2,1)}), bf16[64,5,2,1152]{3,2,1,0:T(2,128)(2,1)S(1)}, u32[]{:S(2)}, u32[]{:S(2)}) async-start(bf16[64,5,2,1152]{3,2,1,0:T(2,128)(2,1)} %broadcast_in_dim.15), calls=%async_computation | async-start | bytes 2949120 | tf_op jit(solution)/shard_map/all_to_all | solution.py:139
  26.5 13.9 %collective-permute-start = (bf16[128,512]{1,0:T(8,128)(2,1)S(1)}, bf16[128,512]{1,0:T(8,128)(2,1)S(1)}, u32[]{:S(2)}, u32[]{:S(2)}) collective-permute-start(bf16[128,512]{1,0:T(8,128)(2,1)S(1)} %get-tuple-element.59), channel_id=1, source_target_pairs={{0,384},{128,0},{256,128},{384,256},{1,385},{129,1},{257,129},{385... | collective-permute-start | bytes 393224 | tf_op jit(solution)/shard_map/ppermute | solution.py:149
  30.8 9.5 %collective-permute-start.1 = (bf16[128,512]{1,0:T(8,128)(2,1)S(1)}, bf16[128,512]{1,0:T(8,128)(2,1)S(1)}, u32[]{:S(2)}, u32[]{:S(2)}) collective-permute-start(bf16[128,512]{1,0:T(8,128)(2,1)S(1)} %get-tuple-element.58), channel_id=1, source_target_pairs={{0,256},{128,384},{256,0},{384,128},{1,257},{129,385},{257,1},{385... | collective-permute-start | bytes 393224 | tf_op jit(solution)/shard_map/ppermute | solution.py:149
  33.3 8.6 %collective-permute-start.2 = (bf16[128,512]{1,0:T(8,128)(2,1)S(1)}, bf16[128,512]{1,0:T(8,128)(2,1)S(1)}, u32[]{:S(2)}, u32[]{:S(2)}) collective-permute-start(bf16[128,512]{1,0:T(8,128)(2,1)S(1)} %get-tuple-element.57), channel_id=1, source_target_pairs={{0,128},{128,256},{256,384},{384,0},{1,129},{129,257},{257,385},{3... | collective-permute-start | bytes 393224 | tf_op jit(solution)/shard_map/ppermute | solution.py:149
  36.9 93.3 %copy-start.3 = (bf16[128,640]{1,0:T(8,128)(2,1)}, bf16[128,640]{1,0:T(8,128)(2,1)S(1)}, u32[]{:S(2)}) copy-start(bf16[128,640]{1,0:T(8,128)(2,1)S(1)} %fusion.66.tok_o) | copy-start | bytes 491524
  36.9 1.4 copy-start.20
  40.3 20.3 %copy-start.9 = (bf16[128,512]{1,0:T(8,128)(2,1)}, bf16[128,512]{1,0:T(8,128)(2,1)S(1)}, u32[]{:S(2)}) copy-start(bf16[128,512]{1,0:T(8,128)(2,1)S(1)} %collective-permute-done) | copy-start | bytes 393220
  40.4 31.8 %copy-start.11 = (bf16[128,512]{1,0:T(8,128)(2,1)}, bf16[128,512]{1,0:T(8,128)(2,1)S(1)}, u32[]{:S(2)}) copy-start(bf16[128,512]{1,0:T(8,128)(2,1)S(1)} %collective-permute-done.1) | copy-start | bytes 393220
  41.9 18.8 %copy-start.13 = (bf16[128,512]{1,0:T(8,128)(2,1)}, bf16[128,512]{1,0:T(8,128)(2,1)S(1)}, u32[]{:S(2)}) copy-start(bf16[128,512]{1,0:T(8,128)(2,1)S(1)} %collective-permute-done.2) | copy-start | bytes 393220
  60.7 57.0 %all-to-all-start.1 = ((bf16[64,5,2,1152]{3,2,1,0:T(2,128)(2,1)}), bf16[64,5,2,1152]{3,2,1,0:T(2,128)(2,1)}, u32[]{:S(2)}, u32[]{:S(2)}) async-start(bf16[64,5,2,1152]{3,2,1,0:T(2,128)(2,1)} %broadcast_in_dim.33), calls=%async_computation.1 | async-start | bytes 2949120 | tf_op jit(solution)/shard_map/all_to_all | solution.py:139
  72.1 61.0 %copy-start.8 = (f32[128,1]{1,0:T(8,128)}, f32[128,1]{1,0:T(8,128)S(1)}, u32[]{:S(2)}) copy-start(f32[128,1]{1,0:T(8,128)S(1)} %fusion.88.live) | copy-start | bytes 1540
  72.8 54.2 %copy-start.1 = (bf16[640,1152]{1,0:T(8,128)(2,1)}, bf16[640,1152]{1,0:T(8,128)(2,1)S(1)}, u32[]{:S(2)}) copy-start(bf16[640,1152]{1,0:T(8,128)(2,1)S(1)} %reshape.113.m0) | copy-start | bytes 4423684
  72.8 35.4 %collective-permute-start.6 = (bf16[640,1152]{1,0:T(8,128)(2,1)S(1)}, bf16[640,1152]{1,0:T(8,128)(2,1)}, u32[]{:S(2)}, u32[]{:S(2)}) collective-permute-start(bf16[640,1152]{1,0:T(8,128)(2,1)S(1)} %reshape.113.m0), channel_id=1, source_target_pairs={{0,128},{128,256},{256,384},{384,0},{1,129},{129,257},{257,385},{3... | collective-permute-start | bytes 4423688 | tf_op jit(solution)/shard_map/ppermute | solution.py:160
  75.9 36.7 %collective-permute-start.4 = (bf16[640,1152]{1,0:T(8,128)(2,1)S(1)}, bf16[640,1152]{1,0:T(8,128)(2,1)}, u32[]{:S(2)}, u32[]{:S(2)}) collective-permute-start(bf16[640,1152]{1,0:T(8,128)(2,1)S(1)} %reshape.113.m0), channel_id=1, source_target_pairs={{0,384},{128,0},{256,128},{384,256},{1,385},{129,1},{257,129},{385... | collective-permute-start | bytes 4423688 | tf_op jit(solution)/shard_map/ppermute | solution.py:159
  79.3 46.1 %collective-permute-start.3 = (bf16[640,1152]{1,0:T(8,128)(2,1)S(1)}, bf16[640,1152]{1,0:T(8,128)(2,1)}, u32[]{:S(2)}, u32[]{:S(2)}) collective-permute-start(bf16[640,1152]{1,0:T(8,128)(2,1)S(1)} %reshape.113.m0), channel_id=1, source_target_pairs={{0,4},{4,0},{1,5},{5,1},{2,6},{6,2},{3,7},{7,3},{8,12},{12,8},{9,1... | collective-permute-start | bytes 4423688 | tf_op jit(solution)/shard_map/ppermute | solution.py:163
  83.4 1.8 copy-start.7
  83.4 1.8 copy-start.10
  83.4 1.8 copy-start.12
  83.4 1.8 copy-start.14
  84.8 30.6 %copy-start.4 = (bf16[128,640]{1,0:T(8,128)(2,1)S(1)}, bf16[128,640]{1,0:T(8,128)(2,1)}, u32[]{:S(2)}) copy-start(bf16[128,640]{1,0:T(8,128)(2,1)} %fusion.69.tok_m) | copy-start | bytes 491524
  108.2 19.8 %collective-permute-start.7 = (bf16[640,1152]{1,0:T(8,128)(2,1)}, bf16[640,1152]{1,0:T(8,128)(2,1)}, u32[]{:S(2)}, u32[]{:S(2)}) collective-permute-start(bf16[640,1152]{1,0:T(8,128)(2,1)} %collective-permute-done.6.m3), channel_id=1, source_target_pairs={{0,4},{4,0},{1,5},{5,1},{2,6},{6,2},{3,7},{7,3},{8,12},{12,8},{9,1... | collective-permute-start | bytes 4423688 | tf_op jit(solution)/shard_map/ppermute | solution.py:163
  112.6 17.6 %collective-permute-start.5 = (bf16[640,1152]{1,0:T(8,128)(2,1)}, bf16[640,1152]{1,0:T(8,128)(2,1)}, u32[]{:S(2)}, u32[]{:S(2)}) collective-permute-start(bf16[640,1152]{1,0:T(8,128)(2,1)} %collective-permute-done.4.m1), channel_id=1, source_target_pairs={{0,4},{4,0},{1,5},{5,1},{2,6},{6,2},{3,7},{7,3},{8,12},{12,8},{9,1... | collective-permute-start | bytes 4423688 | tf_op jit(solution)/shard_map/ppermute | solution.py:163
  121.1 6.9 %copy-start.2 = (bf16[640,1152]{1,0:T(8,128)(2,1)}, bf16[640,1152]{1,0:T(8,128)(2,1)S(1)}, u32[]{:S(2)}) copy-start(bf16[640,1152]{1,0:T(8,128)(2,1)S(1)} %reshape.114.m2) | copy-start | bytes 4423684
  121.1 5.8 %copy-start.5 = (bf16[128,640]{1,0:T(8,128)(2,1)S(1)}, bf16[128,640]{1,0:T(8,128)(2,1)}, u32[]{:S(2)}) copy-start(bf16[128,640]{1,0:T(8,128)(2,1)} %fusion.69.tok_m) | copy-start | bytes 491524
  121.2 12.6 %collective-permute-start.8 = (bf16[640,1152]{1,0:T(8,128)(2,1)S(1)}, bf16[640,1152]{1,0:T(8,128)(2,1)}, u32[]{:S(2)}, u32[]{:S(2)}) collective-permute-start(bf16[640,1152]{1,0:T(8,128)(2,1)S(1)} %reshape.114.m2), channel_id=1, source_target_pairs={{0,4},{4,0},{1,5},{5,1},{2,6},{6,2},{3,7},{7,3},{8,12},{12,8},{9,1... | collective-permute-start | bytes 4423688 | tf_op jit(solution)/shard_map/ppermute | solution.py:163
  125.4 2.6 %copy-start.6 = (f32[128,640]{1,0:T(8,128)S(1)}, f32[128,640]{1,0:T(8,128)}, u32[]{:S(2)}) copy-start(f32[128,640]{1,0:T(8,128)} %fusion.76) | copy-start | bytes 983044
  155.6 23.9 %copy-start.16 = (bf16[2,128,640]{2,1,0:T(8,128)(2,1)S(1)}, bf16[2,128,640]{2,1,0:T(8,128)(2,1)}, u32[]{:S(2)}) copy-start(bf16[2,128,640]{2,1,0:T(8,128)(2,1)} %backward.1) | copy-start | bytes 983044
  167.5 22.5 %all-to-all-start.2 = ((f32[64,1,128]{2,1,0:T(1,128)}), f32[64,1,128]{2,1,0:T(1,128)S(1)}, u32[]{:S(2)}, u32[]{:S(2)}) async-start(f32[64,1,128]{2,1,0:T(1,128)} %broadcast_in_dim.36), calls=%async_computation.2 | async-start | bytes 65536 | tf_op jit(solution)/shard_map/all_to_all | solution.py:219

commit v3 on v2

--- a/solution.py
+++ b/solution.py
@@ -45,23 +45,40 @@
     return 0.5 * (1.0 + t) + 0.5 * v * (1.0 - t * t) * (c * (1.0 + 3.0 * 0.044715 * (v * v)))
 
 
+def copies(refs, lo, hi, buf, sems, first=0):
+    return [
+        pltpu.make_async_copy(ref.at[:, pl.ds(lo, hi - lo)], buf.at[i], sems.at[first + i])
+        for i, ref in enumerate(refs)
+    ]
+
+
 def forward_kernel(
-    where, tok_m, tok_o, pre0, pre1, pre3, goal, tt, live,
+    where, tok_o, pre0, half1, half2, half3, goal, tt, live,
     m0, o0, m1, o1, m2, o2, m3, o3,
-    pred, pre2, score, part, act,
+    pred, pre, score, part, act, w_in, w_out, sems,
 ):
     x, core = where[0], where[1]
-    pre2[...] = dot(tok_m[...], m2[:, :HALF]) + dot(tok_o[...], o2[:, :HALF])
-    for j, ref in enumerate((pre0, pre1, pre2, pre3)):
-        act[lax.rem(x + j, 4)] = jax.nn.gelu(ref[...]).astype(BF16)
+    got_in = copies((o1, o3, o2), 0, HALF, w_in, sems)
+    got_out = copies((m0, o0, m1, o1, m3, o3, m2, o2), HALF, COLS, w_out, sems, 3)
+    for copy in got_in + got_out:
+        copy.start()
+    for i, (j, ref) in enumerate(((0, pre0), (1, half1), (3, half3), (2, half2))):
+        value = ref[...]
+        if i > 0:
+            got_in[i - 1].wait()
+            value += dot(tok_o[...], w_in[i - 1])
+        at = lax.rem(x + j, 4)
+        pre[at] = value
+        act[at] = jax.nn.gelu(value).astype(BF16)
     sm, so = act[core], act[1 - core]
     dm, do = act[2 + core], act[3 - core]
-    slots = ((m0, o0), (m1, o1), (m2, o2), (m3, o3))
     pp = [0.0, 0.0]
     pt = [0.0, 0.0]
-    for j, (m, o) in enumerate(slots):
+    for i, j in enumerate((0, 1, 3, 2)):
+        got_out[2 * i].wait()
+        got_out[2 * i + 1].wait()
         for head, (am, ao, lo, hi) in enumerate(((sm, so, DINO_Q, OUT_Q), (dm, do, 0, DINO_Q))):
-            value = dot(am, m[:, HALF + lo:HALF + hi]) + dot(ao, o[:, HALF + lo:HALF + hi])
+            value = dot(am, w_out[2 * i, :, lo:hi]) + dot(ao, w_out[2 * i + 1, :, lo:hi])
             pred[j, :, lo:hi] = value
             aim = goal[j, :, lo:hi].astype(F32)
             pp[head] += jnp.sum(value * value, axis=1, keepdims=True)
@@ -74,36 +91,49 @@
         score[:, 2 * head:2 * head + 1] = inv_root
         score[:, 2 * head + 1:2 * head + 2] = cosine / mean
         total += cosine
-    part[...] = jnp.sum(live[...] * (2.0 - total), axis=0, keepdims=True) + jnp.zeros((1, 128), F32)
-
-
-def backward_kernel(
-    where, pred, goal, score, scale, pre0, pre1, pre2, pre3,
+    loss = jnp.sum(live[...] * (2.0 - total), axis=0, keepdims=True)
+    part[...] = loss[:, :, None] + jnp.zeros(part.shape, F32)
+
+
+def hidden_kernel(
+    where, pred, goal, score, scale, pre,
     m0, o0, m1, o1, m2, o2, m3, o3,
-    grad, pre, hid,
+    hid, w_out, sems,
 ):
-    x, core = where[0], where[1]
-    for j, ref in enumerate((pre0, pre1, pre2, pre3)):
-        pre[lax.rem(x + j, 4)] = ref[...]
-    slots = ((m0, o0), (m1, o1), (m2, o2), (m3, o3))
+    core = where[1]
+    got = copies((m0, o0, m1, o1, m2, o2, m3, o3), HALF, COLS, w_out, sems)
+    for copy in got:
+        copy.start()
     sums = [[0.0, 0.0], [0.0, 0.0]]
-    for j, (m, o) in enumerate(slots):
+    for j in range(4):
+        got[2 * j].wait()
+        got[2 * j + 1].wait()
         for head, (lo, hi, chans) in enumerate(((DINO_Q, OUT_Q, 4 * SAM_Q), (0, DINO_Q, 4 * DINO_Q))):
             aim = goal[j, :, lo:hi].astype(F32)
             inv_root = score[:, 2 * head:2 * head + 1]
             ratio = score[:, 2 * head + 1:2 * head + 2]
             back = (-scale[...] * (aim * inv_root - ratio * pred[j, :, lo:hi]) / chans).astype(BF16)
-            sums[head][0] += dot_t(back, m[:, HALF + lo:HALF + hi])
-            sums[head][1] += dot_t(back, o[:, HALF + lo:HALF + hi])
+            sums[head][0] += dot_t(back, w_out[2 * j, :, lo:hi])
+            sums[head][1] += dot_t(back, w_out[2 * j + 1, :, lo:hi])
     for head in range(2):
         for side in range(2):
             at = 2 * head + (core if side == 0 else 1 - core)
             hid[at] = (sums[head][side] * gelu_slope(pre[at])).astype(BF16)
-    for side in range(2):
-        total = 0.0
-        for j, pair in enumerate(slots):
-            total += dot_t(hid[lax.rem(x + j, 4)], pair[side][:, :HALF])
-        grad[core if side == 0 else 1 - core] = total.astype(BF16)
+
+
+def grad_kernel(where, hid, m0, o0, m1, o1, m2, o2, m3, o3, grad, w_in, sems):
+    x, core = where[0], where[1]
+    got = copies((m0, o0, m1, o1, m2, o2, m3, o3), 0, HALF, w_in, sems)
+    for copy in got:
+        copy.start()
+    total = [0.0, 0.0]
+    for j in range(4):
+        h = hid[lax.rem(x + j, 4)]
+        for side in range(2):
+            got[2 * j + side].wait()
+            total[side] += dot_t(h, w_in[2 * j + side])
+    grad[core] = total[0].astype(BF16)
+    grad[1 - core] = total[1].astype(BF16)
 
 
 def shards(
@@ -139,9 +169,10 @@
         got = lax.all_to_all(many, PLANE, split_axis=0, concat_axis=0, tiled=True)
         return got
 
-    own_b, opp_b, feats = lax.optimization_barrier(
-        (payload(x), payload((x + 2) % 4), jnp.concatenate(
-            [dino_maps, sam_maps, jnp.zeros((4, rows, OUT_Q - DINO_Q - SAM_Q), BF16)], axis=2)))
+    own_b = payload(x)
+    opp_b, dino_maps, sam_maps = lax.optimization_barrier((payload((x + 2) % 4), dino_maps, sam_maps))
+    feats = jnp.concatenate(
+        [dino_maps, sam_maps, jnp.zeros((4, rows, OUT_Q - DINO_Q - SAM_Q), BF16)], axis=2)
 
     def feat_for(slot):
         return lax.dynamic_index_in_dim(feats, (x - slot) % 4, axis=0, keepdims=False)
@@ -151,19 +182,11 @@
     tok_o = dot(student_tokens, pick_cols(1 - core)).astype(BF16)
 
     own_g = gather_plane(own_b)
-    own_g, got, tok_m, tok_o = lax.optimization_barrier((own_g, got, tok_m, tok_o))
-    opp_b, own_g = lax.optimization_barrier((opp_b, own_g))
+    own_g, opp_b, got, tok_m, tok_o = lax.optimization_barrier((own_g, opp_b, got, tok_m, tok_o))
     opp_g = gather_plane(opp_b)
-
-    own = own_g.reshape(HALF, COLS)
-    next_m = lax.ppermute(own, "x", ring(4, -1))
-    prev_m = lax.ppermute(own, "x", ring(4, 1))
 
     def swap(value):
         return lax.ppermute(value, "core", ring(2, 1))
-
-    opp = opp_g.reshape(HALF, COLS)
-    slots = [(w, swap(w)) for w in (own, next_m, opp, prev_m)]
 
     def gain_of(slot):
         q = (x + slot) % 4
@@ -193,41 +216,71 @@
     live = (slot_at < limit).astype(F32)[:, None]
     count = jnp.sum(jnp.clip(patch_counts, 0, IMG_TOK)).astype(F32)
 
-    pre = {j: dot(tok_m, slots[j][0][:, :HALF]) + dot(tok_o, slots[j][1][:, :HALF]) for j in (0, 1, 3)}
-    goal, tt, live, pre = lax.optimization_barrier((goal, tt, live, pre))
     place = jnp.stack([x, core]).astype(jnp.int32)
+    scale = live / count
+    own = own_g.reshape(HALF, COLS)
+    next_m = lax.ppermute(own, "x", ring(4, -1))
+    prev_m = lax.ppermute(own, "x", ring(4, 1))
+    opp = opp_g.reshape(HALF, COLS)
+    pre0 = dot(tok_m, own[:, :HALF])
+    own, pre0 = lax.optimization_barrier((own, pre0))
+    own_o = swap(own)
+    pre0 += dot(tok_o, own_o[:, :HALF])
+    next_m, prev_m, opp, pre0, goal, tt, live, scale, place = lax.optimization_barrier(
+        (next_m, prev_m, opp, pre0, goal, tt, live, scale, place))
+    slots = [(own, own_o)] + [(w, swap(w)) for w in (next_m, opp, prev_m)]
+
+    part = [dot(tok_m, w[:, :HALF]) for w in (next_m, opp, prev_m)]
     flat = [w for pair in slots for w in pair]
     in_vmem = pl.BlockSpec(memory_space=pltpu.VMEM)
+    anywhere = pl.BlockSpec(memory_space=pl.ANY)
     in_smem = pl.BlockSpec(memory_space=pltpu.SMEM)
-    pred, pre2, score, part = pl.pallas_call(
+    params = pltpu.CompilerParams(vmem_limit_bytes=VMEM_LIMIT)
+    pred, pre, score, loss = pl.pallas_call(
         forward_kernel,
         out_shape=(
             jax.ShapeDtypeStruct((4, rows, OUT_Q), F32),
-            jax.ShapeDtypeStruct((rows, HALF), F32),
+            jax.ShapeDtypeStruct((4, rows, HALF), F32),
             jax.ShapeDtypeStruct((rows, 4), F32),
-            jax.ShapeDtypeStruct((1, 128), F32),
+            jax.ShapeDtypeStruct((8, 1, 128), F32),
         ),
-        in_specs=[in_smem] + [in_vmem] * 16,
+        in_specs=[in_smem] + [in_vmem] * 8 + [anywhere] * 8,
         out_specs=(in_vmem,) * 4,
-        scratch_shapes=[pltpu.VMEM((4, rows, HALF), BF16)],
-        compiler_params=pltpu.CompilerParams(vmem_limit_bytes=VMEM_LIMIT),
+        scratch_shapes=[
+            pltpu.VMEM((4, rows, HALF), BF16),
+            pltpu.VMEM((3, HALF, HALF), BF16),
+            pltpu.VMEM((8, HALF, OUT_Q), BF16),
+            pltpu.SemaphoreType.DMA((11,)),
+        ],
+        compiler_params=params,
         name="forward",
-    )(place, tok_m, tok_o, pre[0], pre[1], pre[3], goal, tt, live, *flat)
-
-    local = lax.psum(lax.psum(part[0, 0], "core"), "x")
-    spread_out = jnp.broadcast_to(local, (64, 1, 128))
-    all_parts = lax.all_to_all(spread_out, PLANE, split_axis=0, concat_axis=0, tiled=True)
-    loss = jnp.sum(all_parts[:, 0, 0]) / count
+    )(place, tok_o, pre0, *part, goal, tt, live, *flat)
+
+    loss = lax.all_to_all(loss, ("x", "core"), split_axis=0, concat_axis=0, tiled=True)
+    hid = pl.pallas_call(
+        hidden_kernel,
+        out_shape=jax.ShapeDtypeStruct((4, rows, HALF), BF16),
+        in_specs=[in_smem] + [in_vmem] * 5 + [anywhere] * 8,
+        out_specs=in_vmem,
+        scratch_shapes=[pltpu.VMEM((8, HALF, OUT_Q), BF16), pltpu.SemaphoreType.DMA((8,))],
+        compiler_params=params,
+        name="hidden",
+    )(place, pred, goal, score, scale, pre, *flat)
+
+    loss = jnp.broadcast_to(jnp.sum(loss, axis=0, keepdims=True), (64, 1, 128))
+    loss, hid = lax.optimization_barrier((loss, hid))
+    loss = lax.all_to_all(loss, PLANE, split_axis=0, concat_axis=0, tiled=True)
+    loss = jnp.sum(loss[:, 0, 0]) / count
 
     grad = pl.pallas_call(
-        backward_kernel,
+        grad_kernel,
         out_shape=jax.ShapeDtypeStruct((2, rows, HALF), BF16),
-        in_specs=[in_smem] + [in_vmem] * 16,
+        in_specs=[in_smem, in_vmem] + [anywhere] * 8,
         out_specs=in_vmem,
-        scratch_shapes=[pltpu.VMEM((4, rows, HALF), F32), pltpu.VMEM((4, rows, HALF), BF16)],
-        compiler_params=pltpu.CompilerParams(vmem_limit_bytes=VMEM_LIMIT),
-        name="backward",
-    )(place, pred, goal, score, live / count, pre[0], pre[1], pre2, pre[3], *flat)
+        scratch_shapes=[pltpu.VMEM((8, HALF, HALF), BF16), pltpu.SemaphoreType.DMA((8,))],
+        compiler_params=params,
+        name="grad",
+    )(place, hid, *flat)
     grad = dot_t(grad[0], pick_cols(0)) + dot_t(grad[1], pick_cols(1))
     return (grad.astype(BF16), loss)
 

time: 195 us -> 171 us (0.88)
  waiting for transfers between devices: 52 us -> 34.9 us
  blocking collectives: 12.1 us -> 0 us
  starting transfers between devices: 68.2 us -> 74 us
  matrix products: 17.5 us -> 13.6 us
  Pallas kernels: 18.7 us -> 20.8 us
    ppermute x1, waiting for transfers between devices: 22.7 us -> 0.49 us  [shards(): prev_m = lax.ppermute(own, 'x', ring(4, 1))]
    all_to_all x2, waiting for transfers between devices: 18.8 us -> 31.7 us  [gather_plane(): got = lax.all_to_all(many, PLANE, split_axis=0, concat_axis=0, tiled=True)]
    psum x2 -> x0, blocking collectives: 12.1 us -> none  [shards(): local = lax.psum(lax.psum(part[0, 0], 'core'), 'x')]
    all_to_all x1 -> x2, waiting for transfers between devices: 9.03 us -> 0.87 us  [the longest x1 0.87 us: shards(): loss = lax.all_to_all(loss, PLANE, split_axis=0, concat_axis=0, tiled=True)]
    all_to_all x1 -> x2, starting transfers between devices: 12 us -> 16.3 us  [the longest x1 12 us: shards(): loss = lax.all_to_all(loss, PLANE, split_axis=0, concat_axis=0, tiled=True)]
    dot_general x9 -> x8, matrix products: 14.3 us -> 10.4 us  [dot(): return jnp.dot(a, b, preferred_element_type=F32)]
    pallas_call x1 -> x2, Pallas kernels: 10.5 us -> 13.8 us  [the longest x1 7.29 us: shards(): pl.pallas_call(hidden_kernel, out_shape=jax.ShapeDtypeStruct((4, rows, HA...]
    unnamed x43 -> x38, local copies, waits for them, and re-layouts: 0.23 us -> 2.32 us
  transfers between devices with their start and end apart: 12 -> 13, of which waited for: 4 -> 6; matrix products, arithmetic and copies ran while one was open for 14% -> 16% of each run, Pallas kernels for 0% -> 8%
where the time goes in v3:
time: 171 us; the launch traced here: 169 us
  starting transfers between devices  74 us (43%)
  waiting for transfers between devices  34.9 us (20%)
  Pallas kernels  20.8 us (12%)
  local copies, waits for them, and re-layouts  15.1 us (9%)
  matrix products  13.6 us (8%)
  other arithmetic  7.15 us (4%)
  between operations  3.85 us (2%)
    all_to_all x2, waiting for transfers between devices, gather_plane(): got = lax.all_to_all(many, PLANE, split_axis=0, concat_axis=0, tiled=True)  31.7 us
    all_to_all x2, starting transfers between devices, gather_plane(): got = lax.all_to_all(many, PLANE, split_axis=0, concat_axis=0, tiled=True)  27.3 us
    ppermute x4, starting transfers between devices, swap(): return lax.ppermute(value, 'core', ring(2, 1))  13.2 us
    all_to_all x1, starting transfers between devices, shards(): loss = lax.all_to_all(loss, PLANE, split_axis=0, concat_axis=0, tiled=True)  12 us
    ppermute x3, starting transfers between devices, shards(): lax.ppermute(feat_for(s), 'x', ring(4, -s))  10.5 us
    dot_general x8, matrix products, dot(): return jnp.dot(a, b, preferred_element_type=F32)  10.4 us
    pallas_call x1, Pallas kernels, shards(): pl.pallas_call(hidden_kernel, out_shape=jax.ShapeDtypeStruct((4, rows, HA...  7.29 us
    pallas_call x1, Pallas kernels, shards(): pl.pallas_call(forward_kernel, out_shape=(jax.ShapeDtypeStruct((4, rows,...  7.03 us
  transfers between devices with their start and end apart: 13, of which 6 were waited for; matrix products, arithmetic and copies ran while one was open for 16% of the time, Pallas kernels for 8%

profile of v3, /device:TPU:1, one launch (start us, length us, event | category | flops | bytes accessed | tf_op | source)
XLA Modules:
  0.0 169.4 jit_solution(4736760684717933157)
XLA Ops:
  0.8 0.8 reshape.122
  1.5 0.1 dynamic-slice_reduce_fusion
  1.6 0.7 constant_dynamic-slice_fusion
  2.4 1.5 fusion.67
  3.9 0.1 concatenate.51
  4.0 1.9 %broadcast_in_dim.15 = bf16[64,5,2,1152]{3,2,1,0:T(2,128)(2,1)} broadcast(bf16[5,2,1152]{2,1,0:T(2,128)(2,1)S(1)} %bitcast.57), dimensions={1,2,3} | broadcast | bytes 1497600 | tf_op jit(solution)/shard_map/broadcast_in_dim | solution.py:166
  5.9 17.1 %all-to-all-start = ((bf16[64,5,2,1152]{3,2,1,0:T(2,128)(2,1)}), bf16[64,5,2,1152]{3,2,1,0:T(2,128)(2,1)S(1)}, u32[]{:S(2)}, u32[]{:S(2)}) async-start(bf16[64,5,2,1152]{3,2,1,0:T(2,128)(2,1)} %broadcast_in_dim.15), calls=%async_computation | async-start | bytes 2949120 | tf_op jit(solution)/shard_map/all_to_all | solution.py:169
  23.3 0.1 concatenate.55
  23.4 1.9 %broadcast_in_dim.17 = bf16[64,5,2,1152]{3,2,1,0:T(2,128)(2,1)} broadcast(bf16[5,2,1152]{2,1,0:T(2,128)(2,1)S(1)} %bitcast.56), dimensions={1,2,3} | broadcast | bytes 1497600 | tf_op jit(solution)/shard_map/broadcast_in_dim | solution.py:166
  25.3 0.1 copy.34
  25.4 0.1 pad.28.clone
  25.5 0.1 maximum_maximum_fusion
  25.6 0.7 dynamic-slice_bitcast_fusion
  26.3 3.1 %collective-permute-start.2 = (bf16[128,512]{1,0:T(8,128)(2,1)S(1)}, bf16[128,512]{1,0:T(8,128)(2,1)S(1)}, u32[]{:S(2)}, u32[]{:S(2)}) collective-permute-start(bf16[128,512]{1,0:T(8,128)(2,1)S(1)} %get-tuple-element.69), channel_id=1, source_target_pairs={{0,128},{128,256},{256,384},{384,0},{1,129},{129,257},{257,385},{3... | collective-permute-start | bytes 393224 | tf_op jit(solution)/shard_map/ppermute | solution.py:180
  29.4 4.4 %collective-permute-start.1 = (bf16[128,512]{1,0:T(8,128)(2,1)S(1)}, bf16[128,512]{1,0:T(8,128)(2,1)S(1)}, u32[]{:S(2)}, u32[]{:S(2)}) collective-permute-start(bf16[128,512]{1,0:T(8,128)(2,1)S(1)} %get-tuple-element.70), channel_id=1, source_target_pairs={{0,256},{128,384},{256,0},{384,128},{1,257},{129,385},{257,1},{385... | collective-permute-start | bytes 393224 | tf_op jit(solution)/shard_map/ppermute | solution.py:180
  33.8 3.1 %collective-permute-start = (bf16[128,512]{1,0:T(8,128)(2,1)S(1)}, bf16[128,512]{1,0:T(8,128)(2,1)S(1)}, u32[]{:S(2)}, u32[]{:S(2)}) collective-permute-start(bf16[128,512]{1,0:T(8,128)(2,1)S(1)} %get-tuple-element.71), channel_id=1, source_target_pairs={{0,384},{128,0},{256,128},{384,256},{1,385},{129,1},{257,129},{385... | collective-permute-start | bytes 393224 | tf_op jit(solution)/shard_map/ppermute | solution.py:180
  36.9 0.1 fusion.103
  37.0 0.1 fusion.102
  37.1 0.1 pad_maximum_fusion.5
  37.2 1.5 fusion.61.tok_o
  38.7 0.6 fusion.64
  39.4 0.6 clamp_reduce_fusion
  40.0 0.6 dynamic_slice.79
  40.6 1.2 fusion.84.live
  41.8 16.3 %all-to-all-done = bf16[64,5,2,1152]{3,2,1,0:T(2,128)(2,1)S(1)} async-done(((bf16[64,5,2,1152]{3,2,1,0:T(2,128)(2,1)}), bf16[64,5,2,1152]{3,2,1,0:T(2,128)(2,1)S(1)}, u32[]{:S(2)}, u32[]{:S(2)}) %all-to-all-start) | async-done | bytes 1474592 | tf_op jit(solution)/shard_map/all_to_all | solution.py:169
  58.1 10.1 %all-to-all-start.1 = ((bf16[64,5,2,1152]{3,2,1,0:T(2,128)(2,1)}), bf16[64,5,2,1152]{3,2,1,0:T(2,128)(2,1)}, u32[]{:S(2)}, u32[]{:S(2)}) async-start(bf16[64,5,2,1152]{3,2,1,0:T(2,128)(2,1)} %broadcast_in_dim.17), calls=%async_computation.1 | async-start | bytes 2949120 | tf_op jit(solution)/shard_map/all_to_all | solution.py:169
  68.2 0.6 pad_add_fusion.where
  69.5 1.2 fusion.83.scale
  70.7 0.6 reshape.123.m0
  71.3 3.3 %collective-permute-start.4 = (bf16[640,1152]{1,0:T(8,128)(2,1)S(1)}, bf16[640,1152]{1,0:T(8,128)(2,1)}, u32[]{:S(2)}, u32[]{:S(2)}) collective-permute-start(bf16[640,1152]{1,0:T(8,128)(2,1)S(1)} %reshape.123.m0), channel_id=1, source_target_pairs={{0,128},{128,256},{256,384},{384,0},{1,129},{129,257},{257,385},{3... | collective-permute-start | bytes 4423688 | tf_op jit(solution)/shard_map/ppermute | solution.py:223
  74.6 3.4 %collective-permute-start.3 = (bf16[640,1152]{1,0:T(8,128)(2,1)S(1)}, bf16[640,1152]{1,0:T(8,128)(2,1)}, u32[]{:S(2)}, u32[]{:S(2)}) collective-permute-start(bf16[640,1152]{1,0:T(8,128)(2,1)S(1)} %reshape.123.m0), channel_id=1, source_target_pairs={{0,384},{128,0},{256,128},{384,256},{1,385},{129,1},{257,129},{385... | collective-permute-start | bytes 4423688 | tf_op jit(solution)/shard_map/ppermute | solution.py:222
  78.0 0.3 fusion.71
  78.3 4.1 %collective-permute-start.5 = (bf16[640,1152]{1,0:T(8,128)(2,1)S(1)}, bf16[640,1152]{1,0:T(8,128)(2,1)S(1)}, u32[]{:S(2)}, u32[]{:S(2)}) collective-permute-start(bf16[640,1152]{1,0:T(8,128)(2,1)S(1)} %reshape.123.m0), channel_id=1, source_target_pairs={{0,4},{4,0},{1,5},{5,1},{2,6},{6,2},{3,7},{7,3},{8,12},{12,8},{9,1... | collective-permute-start | bytes 4423688 | tf_op jit(solution)/shard_map/ppermute | solution.py:189
  82.4 0.9 convert_reduce_fusion
  83.3 0.2 multiply_reduce_fusion.2
  83.6 0.1 maximum_convert_fusion
  83.7 0.2 slice_reduce_fusion
  83.9 0.3 multiply_reduce_fusion
  84.2 0.9 pad_maximum_fusion.goal
  85.1 0.2 collective-permute-done.5.o0
  85.3 1.1 copy-done.3
  86.4 1.0 convolution_add_fusion.pre0
  87.4 15.5 %all-to-all-done.1 = bf16[64,5,2,1152]{3,2,1,0:T(2,128)(2,1)} async-done(((bf16[64,5,2,1152]{3,2,1,0:T(2,128)(2,1)}), bf16[64,5,2,1152]{3,2,1,0:T(2,128)(2,1)}, u32[]{:S(2)}, u32[]{:S(2)}) %all-to-all-start.1) | async-done | bytes 1474592 | tf_op jit(solution)/shard_map/all_to_all | solution.py:169
  102.9 3.5 %reshape.124.m2 = bf16[640,1152]{1,0:T(8,128)(2,1)S(1)} reshape(bf16[64,5,2,1152]{3,2,1,0:T(2,128)(2,1)} %all-to-all-done.1) | data formatting | bytes 2949120 | tf_op jit(solution)/shard_map/reshape | solution.py:224
  106.4 0.5 collective-permute-done.4.m3
  106.9 1.6 collective-permute-done.3.m1
  108.5 4.7 %collective-permute-start.6 = (bf16[640,1152]{1,0:T(8,128)(2,1)}, bf16[640,1152]{1,0:T(8,128)(2,1)S(1)}, u32[]{:S(2)}, u32[]{:S(2)}) collective-permute-start(bf16[640,1152]{1,0:T(8,128)(2,1)} %collective-permute-done.3.m1), channel_id=1, source_target_pairs={{0,4},{4,0},{1,5},{5,1},{2,6},{6,2},{3,7},{7,3},{8,12},{12,8},{9,1... | collective-permute-start | bytes 4423688 | tf_op jit(solution)/shard_map/ppermute | solution.py:189
  113.2 1.9 %collective-permute-start.7 = (bf16[640,1152]{1,0:T(8,128)(2,1)S(1)}, bf16[640,1152]{1,0:T(8,128)(2,1)}, u32[]{:S(2)}, u32[]{:S(2)}) collective-permute-start(bf16[640,1152]{1,0:T(8,128)(2,1)S(1)} %reshape.124.m2), channel_id=1, source_target_pairs={{0,4},{4,0},{1,5},{5,1},{2,6},{6,2},{3,7},{7,3},{8,12},{12,8},{9,1... | collective-permute-start | bytes 4423688 | tf_op jit(solution)/shard_map/ppermute | solution.py:189
  115.1 2.6 %collective-permute-start.8 = (bf16[640,1152]{1,0:T(8,128)(2,1)}, bf16[640,1152]{1,0:T(8,128)(2,1)}, u32[]{:S(2)}, u32[]{:S(2)}) collective-permute-start(bf16[640,1152]{1,0:T(8,128)(2,1)} %collective-permute-done.4.m3), channel_id=1, source_target_pairs={{0,4},{4,0},{1,5},{5,1},{2,6},{6,2},{3,7},{7,3},{8,12},{12,8},{9,1... | collective-permute-start | bytes 4423688 | tf_op jit(solution)/shard_map/ppermute | solution.py:189
  117.7 0.7 copy.36.tt
  118.5 2.2 %fusion.77.half1 = f32[128,640]{1,0:T(8,128)} fusion(bf16[128,640]{0,1:T(8,128)(2,1)S(1)} %fusion.64, bf16[640,1152]{1,0:T(8,128)(2,1)} %collective-permute-done.3.m1), kind=kOutput, calls=%fused_computation.65 | convolution fusion | flops 104857600 | bytes 1310720 | tf_op jit(solution)/shard_map/dot_general | solution.py:29
  120.7 1.1 fusion.75.half2
  121.7 2.2 %fusion.73.half3 = f32[128,640]{1,0:T(8,128)} fusion(bf16[128,640]{0,1:T(8,128)(2,1)S(1)} %fusion.64, bf16[640,1152]{1,0:T(8,128)(2,1)} %collective-permute-done.4.m3), kind=kOutput, calls=%fused_computation.61 | convolution fusion | flops 104857600 | bytes 1310720 | tf_op jit(solution)/shard_map/dot_general | solution.py:29
  124.0 1.1 copy-done.4
  125.1 7.0 %forward.1 = (f32[4,128,512]{2,1,0:T(8,128)}, f32[4,128,640]{2,1,0:T(8,128)}, f32[128,4]{1,0:T(8,128)}, f32[8,1,128]{2,1,0:T(1,128)}) custom-call(s32[2]{0:T(128)} %pad_add_fusion.where, bf16[128,640]{1,0:T(8,128)(2,1)} %fusion.61.tok_o, f32[128,640]{1,0:T(8,128)} %convolution_add_fusion.pre0, f32[128,640]{1,0:T(8,128)} %fusion.77.half1, ...), custom_call_target="tpu_custom_call" | custom-call | tf_op jit(solution)/shard_map/forward/pallas_call | solution.py:239
  132.1 4.4 %all-to-all-start.2 = ((f32[8,1,128]{2,1,0:T(1,128)}), f32[8,1,128]{2,1,0:T(1,128)S(1)}, u32[]{:S(2)}, u32[]{:S(2)}) async-start(f32[8,1,128]{2,1,0:T(1,128)} %get-tuple-element.51), calls=%async_computation.2 | async-start | bytes 8192 | tf_op jit(solution)/shard_map/all_to_all | solution.py:259
  136.5 7.3 %hidden.1.hid = bf16[4,128,640]{2,1,0:T(8,128)(2,1)} custom-call(s32[2]{0:T(128)} %pad_add_fusion.where, f32[4,128,512]{2,1,0:T(8,128)} %get-tuple-element.52.pred, bf16[4,128,512]{2,1,0:T(8,128)(2,1)} %pad_maximum_fusion.goal, f32[128,4]{1,0:T(8,128)} %get-tuple-element.53.score, f32[128,1]{1,0:T(8,128)} %fusion.83.scale, ...), custom_call_target="tpu_custom_call" | custom-call | tf_op jit(solution)/shard_map/hidden/pallas_call | solution.py:260
  143.8 0.6 broadcast_in_dim.39
  144.4 12.0 %all-to-all-start.3 = ((f32[64,1,128]{2,1,0:T(1,128)}), f32[64,1,128]{2,1,0:T(1,128)S(1)}, u32[]{:S(2)}, u32[]{:S(2)}) async-start(f32[64,1,128]{2,1,0:T(1,128)} %broadcast_in_dim.39), calls=%async_computation.3 | async-start | bytes 65536 | tf_op jit(solution)/shard_map/all_to_all | solution.py:272
  156.4 6.5 %grad.1 = bf16[2,128,640]{2,1,0:T(8,128)(2,1)} custom-call(s32[2]{0:T(128)} %pad_add_fusion.where, bf16[4,128,640]{2,1,0:T(8,128)(2,1)} %hidden.1.hid, bf16[640,1152]{1,0:T(8,128)(2,1)} %copy-done.1, bf16[640,1152]{1,0:T(8,128)(2,1)} %copy-done.3, bf16[640,1152]{1,0:T(8,128)(2,1)} %collective-permute-done.3.m1, bf16[640,1152]{1,0:T(8,128)(2,1)} %copy-done.4, ...), custom_call_target="tpu_custom_call" | custom-call | tf_op jit(solution)/shard_map/grad/pallas_call | solution.py:275
  162.9 1.7 %fusion.6 = f32[128,1280]{1,0:T(8,128)S(1)} fusion(s32[640]{0:T(1024)S(1)} %get-tuple-element.96, s32[640]{0:T(1024)S(1)} %get-tuple-element.97, s32[640]{0:T(1024)S(1)} %get-tuple-element.95, s32[640]{0:T(1024)S(1)} %get-tuple-element.98, pred[640]{0:T(1024)(128)(4,1)S(1)} %get-tuple-element.93, pred[640]{0:T(1024)(128)(4,1)S(1)} %get-tuple-element.94, ...), kind=kOutput, calls=%fused_computation.12 | convolution fusion | flops 214630400 | bytes 830720 | tf_op jit(solution)/shard_map/dot_general | solution.py:33
  164.6 1.5 fusion.17
  166.1 0.9 all-to-all-done.3
  166.9 0.7 slice_reduce_fusion.1
  (66 shorter events, 0.4 us)
Async XLA Ops:
  0.6 36.6 %copy-start = (bf16[128,1280]{1,0:T(8,128)(2,1)S(1)}, bf16[128,1280]{1,0:T(8,128)(2,1)}, u32[]{:S(2)}) copy-start(bf16[128,1280]{1,0:T(8,128)(2,1)} %param.10) | copy-start | bytes 983044
  5.9 52.1 %all-to-all-start = ((bf16[64,5,2,1152]{3,2,1,0:T(2,128)(2,1)}), bf16[64,5,2,1152]{3,2,1,0:T(2,128)(2,1)S(1)}, u32[]{:S(2)}, u32[]{:S(2)}) async-start(bf16[64,5,2,1152]{3,2,1,0:T(2,128)(2,1)} %broadcast_in_dim.15), calls=%async_computation | async-start | bytes 2949120 | tf_op jit(solution)/shard_map/all_to_all | solution.py:169
  23.1 2.2 %copy-start.15 = (bf16[4,128,64]{1,2,0:T(8,128)(2,1)S(1)}, bf16[4,128,64]{1,2,0:T(8,128)(2,1)}, u32[]{:S(2)}) copy-start(bf16[4,128,64]{1,2,0:T(8,128)(2,1)} %param.11) | copy-start | bytes 196612
  23.1 2.4 %copy-start.13 = (bf16[4,128,384]{2,1,0:T(8,128)(2,1)S(1)}, bf16[4,128,384]{2,1,0:T(8,128)(2,1)}, u32[]{:S(2)}) copy-start(bf16[4,128,384]{2,1,0:T(8,128)(2,1)} %param.12) | copy-start | bytes 1179652
  25.2 11.7 %copy-start.17 = (f32[256]{0:T(256)S(1)}, f32[256]{0:T(256)}, u32[]{:S(2)}) copy-start(f32[256]{0:T(256)} %param.13) | copy-start | bytes 3076
  25.3 11.8 %copy-start.16 = (f32[1536]{0:T(1024)S(1)}, f32[1536]{0:T(1024)}, u32[]{:S(2)}) copy-start(f32[1536]{0:T(1024)} %param.14) | copy-start | bytes 18436
  26.3 15.5 %collective-permute-start.2 = (bf16[128,512]{1,0:T(8,128)(2,1)S(1)}, bf16[128,512]{1,0:T(8,128)(2,1)S(1)}, u32[]{:S(2)}, u32[]{:S(2)}) collective-permute-start(bf16[128,512]{1,0:T(8,128)(2,1)S(1)} %get-tuple-element.69), channel_id=1, source_target_pairs={{0,128},{128,256},{256,384},{384,0},{1,129},{129,257},{257,385},{3... | collective-permute-start | bytes 393224 | tf_op jit(solution)/shard_map/ppermute | solution.py:180
  29.4 12.3 %collective-permute-start.1 = (bf16[128,512]{1,0:T(8,128)(2,1)S(1)}, bf16[128,512]{1,0:T(8,128)(2,1)S(1)}, u32[]{:S(2)}, u32[]{:S(2)}) collective-permute-start(bf16[128,512]{1,0:T(8,128)(2,1)S(1)} %get-tuple-element.70), channel_id=1, source_target_pairs={{0,256},{128,384},{256,0},{384,128},{1,257},{129,385},{257,1},{385... | collective-permute-start | bytes 393224 | tf_op jit(solution)/shard_map/ppermute | solution.py:180
  33.8 8.0 %collective-permute-start = (bf16[128,512]{1,0:T(8,128)(2,1)S(1)}, bf16[128,512]{1,0:T(8,128)(2,1)S(1)}, u32[]{:S(2)}, u32[]{:S(2)}) collective-permute-start(bf16[128,512]{1,0:T(8,128)(2,1)S(1)} %get-tuple-element.71), channel_id=1, source_target_pairs={{0,384},{128,0},{256,128},{384,256},{1,385},{129,1},{257,129},{385... | collective-permute-start | bytes 393224 | tf_op jit(solution)/shard_map/ppermute | solution.py:180
  38.7 0.7 copy-start.18
  41.8 16.3 %copy-start.7 = (bf16[128,512]{1,0:T(8,128)(2,1)}, bf16[128,512]{1,0:T(8,128)(2,1)S(1)}, u32[]{:S(2)}) copy-start(bf16[128,512]{1,0:T(8,128)(2,1)S(1)} %collective-permute-done.2) | copy-start | bytes 393220
  41.8 28.9 %copy-start.9 = (bf16[128,512]{1,0:T(8,128)(2,1)}, bf16[128,512]{1,0:T(8,128)(2,1)S(1)}, u32[]{:S(2)}) copy-start(bf16[128,512]{1,0:T(8,128)(2,1)S(1)} %collective-permute-done.1) | copy-start | bytes 393220
  41.8 28.9 %copy-start.11 = (bf16[128,512]{1,0:T(8,128)(2,1)}, bf16[128,512]{1,0:T(8,128)(2,1)S(1)}, u32[]{:S(2)}) copy-start(bf16[128,512]{1,0:T(8,128)(2,1)S(1)} %collective-permute-done) | copy-start | bytes 393220
  58.1 44.8 %all-to-all-start.1 = ((bf16[64,5,2,1152]{3,2,1,0:T(2,128)(2,1)}), bf16[64,5,2,1152]{3,2,1,0:T(2,128)(2,1)}, u32[]{:S(2)}, u32[]{:S(2)}) async-start(bf16[64,5,2,1152]{3,2,1,0:T(2,128)(2,1)} %broadcast_in_dim.17), calls=%async_computation.1 | async-start | bytes 2949120 | tf_op jit(solution)/shard_map/all_to_all | solution.py:169
  71.3 12.4 %copy-start.1 = (bf16[640,1152]{1,0:T(8,128)(2,1)}, bf16[640,1152]{1,0:T(8,128)(2,1)S(1)}, u32[]{:S(2)}) copy-start(bf16[640,1152]{1,0:T(8,128)(2,1)S(1)} %reshape.123.m0) | copy-start | bytes 4423684
  71.3 12.2 %copy-start.5 = (bf16[128,512]{1,0:T(8,128)(2,1)S(1)}, bf16[128,512]{1,0:T(8,128)(2,1)}, u32[]{:S(2)}) copy-start(bf16[128,512]{1,0:T(8,128)(2,1)} %get-tuple-element.39) | copy-start | bytes 393220
  71.3 12.2 %copy-start.8 = (bf16[128,512]{1,0:T(8,128)(2,1)S(1)}, bf16[128,512]{1,0:T(8,128)(2,1)}, u32[]{:S(2)}) copy-start(bf16[128,512]{1,0:T(8,128)(2,1)} %copy-done.7) | copy-start | bytes 393220
  71.3 12.2 %copy-start.10 = (bf16[128,512]{1,0:T(8,128)(2,1)S(1)}, bf16[128,512]{1,0:T(8,128)(2,1)}, u32[]{:S(2)}) copy-start(bf16[128,512]{1,0:T(8,128)(2,1)} %copy-done.9) | copy-start | bytes 393220
  71.3 12.2 %copy-start.12 = (bf16[128,512]{1,0:T(8,128)(2,1)S(1)}, bf16[128,512]{1,0:T(8,128)(2,1)}, u32[]{:S(2)}) copy-start(bf16[128,512]{1,0:T(8,128)(2,1)} %copy-done.11) | copy-start | bytes 393220
  71.3 35.5 %collective-permute-start.4 = (bf16[640,1152]{1,0:T(8,128)(2,1)S(1)}, bf16[640,1152]{1,0:T(8,128)(2,1)}, u32[]{:S(2)}, u32[]{:S(2)}) collective-permute-start(bf16[640,1152]{1,0:T(8,128)(2,1)S(1)} %reshape.123.m0), channel_id=1, source_target_pairs={{0,128},{128,256},{256,384},{384,0},{1,129},{129,257},{257,385},{3... | collective-permute-start | bytes 4423688 | tf_op jit(solution)/shard_map/ppermute | solution.py:223
  74.6 33.9 %collective-permute-start.3 = (bf16[640,1152]{1,0:T(8,128)(2,1)S(1)}, bf16[640,1152]{1,0:T(8,128)(2,1)}, u32[]{:S(2)}, u32[]{:S(2)}) collective-permute-start(bf16[640,1152]{1,0:T(8,128)(2,1)S(1)} %reshape.123.m0), channel_id=1, source_target_pairs={{0,384},{128,0},{256,128},{384,256},{1,385},{129,1},{257,129},{385... | collective-permute-start | bytes 4423688 | tf_op jit(solution)/shard_map/ppermute | solution.py:222
  78.3 6.9 %collective-permute-start.5 = (bf16[640,1152]{1,0:T(8,128)(2,1)S(1)}, bf16[640,1152]{1,0:T(8,128)(2,1)S(1)}, u32[]{:S(2)}, u32[]{:S(2)}) collective-permute-start(bf16[640,1152]{1,0:T(8,128)(2,1)S(1)} %reshape.123.m0), channel_id=1, source_target_pairs={{0,4},{4,0},{1,5},{5,1},{2,6},{6,2},{3,7},{7,3},{8,12},{12,8},{9,1... | collective-permute-start | bytes 4423688 | tf_op jit(solution)/shard_map/ppermute | solution.py:189
  83.7 2.7 %copy-start.6 = (bf16[128,640]{1,0:T(8,128)(2,1)S(1)}, bf16[128,640]{1,0:T(8,128)(2,1)}, u32[]{:S(2)}) copy-start(bf16[128,640]{1,0:T(8,128)(2,1)} %fusion.61.tok_o) | copy-start | bytes 491524
  85.3 1.1 copy-start.3
  106.4 17.6 %copy-start.2 = (bf16[640,1152]{1,0:T(8,128)(2,1)}, bf16[640,1152]{1,0:T(8,128)(2,1)S(1)}, u32[]{:S(2)}) copy-start(bf16[640,1152]{1,0:T(8,128)(2,1)S(1)} %reshape.124.m2) | copy-start | bytes 4423684
  108.5 15.4 %collective-permute-start.6 = (bf16[640,1152]{1,0:T(8,128)(2,1)}, bf16[640,1152]{1,0:T(8,128)(2,1)S(1)}, u32[]{:S(2)}, u32[]{:S(2)}) collective-permute-start(bf16[640,1152]{1,0:T(8,128)(2,1)} %collective-permute-done.3.m1), channel_id=1, source_target_pairs={{0,4},{4,0},{1,5},{5,1},{2,6},{6,2},{3,7},{7,3},{8,12},{12,8},{9,1... | collective-permute-start | bytes 4423688 | tf_op jit(solution)/shard_map/ppermute | solution.py:189
  113.2 10.8 %collective-permute-start.7 = (bf16[640,1152]{1,0:T(8,128)(2,1)S(1)}, bf16[640,1152]{1,0:T(8,128)(2,1)}, u32[]{:S(2)}, u32[]{:S(2)}) collective-permute-start(bf16[640,1152]{1,0:T(8,128)(2,1)S(1)} %reshape.124.m2), channel_id=1, source_target_pairs={{0,4},{4,0},{1,5},{5,1},{2,6},{6,2},{3,7},{7,3},{8,12},{12,8},{9,1... | collective-permute-start | bytes 4423688 | tf_op jit(solution)/shard_map/ppermute | solution.py:189
  115.1 8.8 %collective-permute-start.8 = (bf16[640,1152]{1,0:T(8,128)(2,1)}, bf16[640,1152]{1,0:T(8,128)(2,1)}, u32[]{:S(2)}, u32[]{:S(2)}) collective-permute-start(bf16[640,1152]{1,0:T(8,128)(2,1)} %collective-permute-done.4.m3), channel_id=1, source_target_pairs={{0,4},{4,0},{1,5},{5,1},{2,6},{6,2},{3,7},{7,3},{8,12},{12,8},{9,1... | collective-permute-start | bytes 4423688 | tf_op jit(solution)/shard_map/ppermute | solution.py:189
  124.0 1.1 copy-start.4
  132.1 11.7 %all-to-all-start.2 = ((f32[8,1,128]{2,1,0:T(1,128)}), f32[8,1,128]{2,1,0:T(1,128)S(1)}, u32[]{:S(2)}, u32[]{:S(2)}) async-start(f32[8,1,128]{2,1,0:T(1,128)} %get-tuple-element.51), calls=%async_computation.2 | async-start | bytes 8192 | tf_op jit(solution)/shard_map/all_to_all | solution.py:259
  144.4 22.5 %all-to-all-start.3 = ((f32[64,1,128]{2,1,0:T(1,128)}), f32[64,1,128]{2,1,0:T(1,128)S(1)}, u32[]{:S(2)}, u32[]{:S(2)}) async-start(f32[64,1,128]{2,1,0:T(1,128)} %broadcast_in_dim.39), calls=%async_computation.3 | async-start | bytes 65536 | tf_op jit(solution)/shard_map/all_to_all | solution.py:272
  162.9 1.7 %copy-start.14 = (bf16[2,128,640]{2,1,0:T(8,128)(2,1)S(1)}, bf16[2,128,640]{2,1,0:T(8,128)(2,1)}, u32[]{:S(2)}) copy-start(bf16[2,128,640]{2,1,0:T(8,128)(2,1)} %grad.1) | copy-start | bytes 983044

commit v4 on v3

v4 whole, which is shorter than its diff:
```python
import functools

import jax
import jax.numpy as jnp
from jax import lax
from jax.experimental import pallas as pl
from jax.experimental.pallas import tpu as pltpu
from jax.sharding import Mesh, PartitionSpec as P

IMG_TOK = 1024
AXES = ("x", "ylo", "z", "core", "yhi")
PLANE = ("ylo", "z", "yhi")
HALF = 640
DINO_Q = 384
SAM_Q = 64
SAM = 256
FEAT_Q = 512
FAR = 256
COLS = HALF + DINO_Q
OPP_COLS = COLS - FAR + SAM
F32 = jnp.float32
BF16 = jnp.bfloat16
VMEM_LIMIT = 56 * 1024 * 1024


def ring(n, shift):
    return [(i, (i + shift) % n) for i in range(n)]


def dot(a, b):
    return jnp.dot(a, b, preferred_element_type=F32)


def dot_t(a, b):
    return lax.dot_general(a, b, (((1,), (1,)), ((), ())), preferred_element_type=F32)


def pick_cols(half):
    source = lax.broadcasted_iota(jnp.int32, (2 * HALF, HALF), 0)
    at = lax.broadcasted_iota(jnp.int32, (2 * HALF, HALF), 1)
    return (source == (at // 40) * 80 + half * 40 + at % 40).astype(BF16)


def gelu_slope(v):
    c = 0.7978845608028654
    t = jnp.tanh(c * (v + 0.044715 * (v * v * v)))
    return 0.5 * (1.0 + t) + 0.5 * v * (1.0 - t * t) * (c * (1.0 + 3.0 * 0.044715 * (v * v)))


def copies(refs, lo, hi, buf, sems, first=0):
    return [
        pltpu.make_async_copy(ref.at[:, pl.ds(lo, hi - lo)], buf.at[i], sems.at[first + i])
        for i, ref in enumerate(refs)
    ]


def far_copies(opp, far, buf, at, sems, first):
    low, high = pl.ds(0, FAR), pl.ds(FAR, DINO_Q - FAR)
    out = []
    for i, (a, b) in enumerate(zip(opp, far)):
        out.append(pltpu.make_async_copy(b, buf.at[at + i, :, low], sems.at[first + 2 * i]))
        source = a.at[:, pl.ds(HALF, DINO_Q - FAR)]
        out.append(pltpu.make_async_copy(source, buf.at[at + i, :, high], sems.at[first + 2 * i + 1]))
    return out


def forward_kernel(
    where, tok_m, tok_o, pre0, goal_s, goal_d, live,
    m0, o0, m1, o1, m2, o2, m3, o3, mf, of,
    pred_s, pred_d, pre, score, part, act, w_in, w_out, w_sam, sems,
):
    x, core = where[0], where[1]
    got_in = copies((m1, o1, m3, o3, m2, o2), 0, HALF, w_in, sems)
    got_out = copies((m0, o0, m1, o1, m3, o3), HALF, COLS, w_out, sems, 6)
    got_far = far_copies((m2, o2), (mf, of), w_out, 6, sems, 12)
    got_sam = copies((m2, o2), OPP_COLS - SAM, OPP_COLS, w_sam, sems, 16)
    for copy in got_in + got_out + got_far + got_sam:
        copy.start()
    for i, j in enumerate((0, 1, 3, 2)):
        if i == 0:
            value = pre0[...]
        else:
            got_in[2 * i - 2].wait()
            got_in[2 * i - 1].wait()
            value = dot(tok_m[...], w_in[2 * i - 2]) + dot(tok_o[...], w_in[2 * i - 1])
        at = lax.rem(x + j, 4)
        pre[at] = value
        act[at] = jax.nn.gelu(value).astype(BF16)

    def sums(value, aim):
        return [jnp.sum(v, axis=1, keepdims=True) for v in (value * value, aim * aim, value * aim)]

    found = [0.0, 0.0, 0.0]
    dm, do = act[2 + core], act[3 - core]
    for i, j in enumerate((0, 1, 3, 2)):
        for copy in got_out[2 * i:2 * i + 2] or got_far:
            copy.wait()
        value = dot(dm, w_out[2 * i]) + dot(do, w_out[2 * i + 1])
        pred_d[j] = value
        found = [a + b for a, b in zip(found, sums(value, goal_d[j].astype(F32)))]
    for copy in got_sam:
        copy.wait()
    value = dot(act[core], w_sam[0]) + dot(act[1 - core], w_sam[1])
    pred_s[...] = value
    total = 0.0
    heads = ((SAM, sums(value, goal_s[...].astype(F32))), (4 * DINO_Q, found))
    for head, (chans, (pp, tt, pt)) in enumerate(heads):
        mean = pp / chans + 1e-05
        inv_root = lax.rsqrt(mean * (tt / chans + 1e-05))
        cosine = pt / chans * inv_root
        score[:, 2 * head:2 * head + 1] = inv_root
        score[:, 2 * head + 1:2 * head + 2] = cosine / mean
        total += cosine
    loss = jnp.sum(live[...] * (2.0 - total), axis=0, keepdims=True)
    part[...] = loss[:, :, None] + jnp.zeros(part.shape, F32)


def hidden_kernel(
    where, pred_s, pred_d, goal_s, goal_d, score, scale, pre,
    m0, o0, m1, o1, m2, o2, m3, o3, mf, of,
    hid, w_out, w_sam, sems,
):
    core = where[1]
    got_sam = copies((m2, o2), OPP_COLS - SAM, OPP_COLS, w_sam, sems)
    got_out = copies((m0, o0, m1, o1, m3, o3), HALF, COLS, w_out, sems, 2)
    got_far = far_copies((m2, o2), (mf, of), w_out, 6, sems, 8)
    for copy in got_sam + got_out + got_far:
        copy.start()

    def back(head, pred, goal, chans):
        inv_root = score[:, 2 * head:2 * head + 1]
        ratio = score[:, 2 * head + 1:2 * head + 2]
        return (-scale[...] * (goal.astype(F32) * inv_root - ratio * pred) / chans).astype(BF16)

    def finish(head, found):
        for side, value in enumerate(found):
            at = 2 * head + (core if side == 0 else 1 - core)
            hid[at] = (value * gelu_slope(pre[at])).astype(BF16)

    value = back(0, pred_s[...], goal_s[...], SAM)
    for copy in got_sam:
        copy.wait()
    finish(0, [dot_t(value, w_sam[side]) for side in range(2)])
    found = [0.0, 0.0]
    for i, j in enumerate((0, 1, 3, 2)):
        value = back(1, pred_d[j], goal_d[j], 4 * DINO_Q)
        for copy in got_out[2 * i:2 * i + 2] or got_far:
            copy.wait()
        for side in range(2):
            found[side] += dot_t(value, w_out[2 * i + side])
    finish(1, found)


def grad_kernel(where, hid, m0, o0, m1, o1, m2, o2, m3, o3, grad, w_in, sems):
    x, core = where[0], where[1]
    got = copies((m0, o0, m1, o1, m2, o2, m3, o3), 0, HALF, w_in, sems)
    for copy in got:
        copy.start()
    total = [0.0, 0.0]
    for j in range(4):
        h = hid[lax.rem(x + j, 4)]
        for side in range(2):
            got[2 * j + side].wait()
            total[side] += dot_t(h, w_in[2 * j + side])
    at = lax.broadcasted_iota(jnp.int32, (1, HALF), 1)
    block = (at * 1639) >> 16
    row = lax.broadcasted_iota(jnp.int32, (2 * HALF, HALF), 0)
    whole = 0.0
    for side, half in enumerate((core, 1 - core)):
        source = at + block * 40 + half * 40
        whole += dot_t(total[side].astype(BF16), (row == source).astype(BF16))
    grad[...] = whole.astype(BF16)


def shards(
    student_tokens,
    sam_maps,
    dino_maps,
    sam_gain,
    dino_gain,
    patch_counts,
    sam_in,
    sam_out,
    dino_in,
    dino_out,
):
    rows = student_tokens.shape[0]
    x = lax.axis_index("x")
    core = lax.axis_index("core")
    shard = sam_in.shape[0]

    both = jnp.concatenate([sam_in, dino_in], axis=0)
    picked = dot(both, pick_cols(x % 2)).astype(BF16).reshape(2, shard, HALF)

    def payload(q, first, extra):
        part_in = lax.dynamic_index_in_dim(picked, q // 2, axis=0, keepdims=False)
        part_d = lax.dynamic_slice(dino_out, (0, q * DINO_Q + first), (shard, DINO_Q - first))
        part = jnp.concatenate([part_in, part_d] + extra, axis=1)
        cols = part.shape[1]
        return jnp.broadcast_to(part.reshape(1, shard // 2, 2, cols), (64, shard // 2, 2, cols))

    def gather_plane(many):
        return lax.all_to_all(many, PLANE, split_axis=0, concat_axis=0, tiled=True)

    own_b = payload(x, 0, [])
    sam4 = sam_out.reshape(shard, 4, SAM_Q)
    sam_parts = [lax.dynamic_index_in_dim(sam4, (x + j) % 4, axis=1, keepdims=False) for j in range(4)]
    opp_b, dino_maps, sam_maps = lax.optimization_barrier(
        (payload((x + 2) % 4, FAR, sam_parts), dino_maps, sam_maps))
    feats = jnp.concatenate(
        [dino_maps, sam_maps, jnp.zeros((4, rows, FEAT_Q - DINO_Q - SAM_Q), BF16)], axis=2)

    def feat_for(slot):
        return lax.dynamic_index_in_dim(feats, (x - slot) % 4, axis=0, keepdims=False)

    got = [feat_for(0)] + [lax.ppermute(feat_for(s), "x", ring(4, -s)) for s in (1, 2, 3)]
    tok_m = dot(student_tokens, pick_cols(core)).astype(BF16)
    tok_o = dot(student_tokens, pick_cols(1 - core)).astype(BF16)

    own_g = gather_plane(own_b)
    start = lax.axis_index(AXES) * rows
    limit = lax.dynamic_index_in_dim(patch_counts, start // IMG_TOK, keepdims=False)
    slot_at = start % IMG_TOK + jnp.arange(rows, dtype=jnp.int32)
    live = (slot_at < limit).astype(F32)[:, None]
    count = jnp.sum(jnp.clip(patch_counts, 0, IMG_TOK)).astype(F32)

    place = jnp.stack([x, core]).astype(jnp.int32)
    scale = live / count
    own, opp_b, got, tok_m, tok_o, live, scale, place = lax.optimization_barrier(
        (own_g.reshape(HALF, COLS), opp_b, got, tok_m, tok_o, live, scale, place))
    opp_g = gather_plane(opp_b)

    def swap(value):
        return lax.ppermute(value, "core", ring(2, 1))

    def gains(gain, width):
        return [lax.dynamic_slice(gain, ((x + j) % 4 * width,), (width,)) for j in range(4)]

    def targets(part, gain):
        chans = 4 * part.shape[2] if part.shape[0] == 4 else part.shape[2]
        center = jnp.sum(part, axis=(0, 2), keepdims=True) / chans
        spread = jnp.sum(part * part, axis=(0, 2), keepdims=True) / chans - center * center
        return ((part - center) * lax.rsqrt(spread + 1e-06) * gain).astype(BF16)

    next_m = lax.ppermute(own, "x", ring(4, -1))
    prev_m = lax.ppermute(own, "x", ring(4, 1))
    far_m = lax.ppermute(own[:, HALF:HALF + FAR], "x", ring(4, 2))
    pre0 = dot(tok_m, own[:, :HALF])
    own, pre0 = lax.optimization_barrier((own, pre0))
    own_o = swap(own)
    own_o, got = lax.optimization_barrier((own_o, got))
    pre0 += dot(tok_o, own_o[:, :HALF])
    feat_d = jnp.stack([g[:, :DINO_Q] for g in got]).astype(F32)
    feat_s = jnp.concatenate([g[:, DINO_Q:DINO_Q + SAM_Q] for g in got], axis=1).astype(F32)
    goal_d = targets(feat_d, jnp.stack(gains(dino_gain, DINO_Q))[:, None, :])
    goal_s = targets(feat_s[None], jnp.concatenate(gains(sam_gain, SAM_Q))[None, None, :])[0]

    next_m, prev_m, far_m, pre0, goal_s, goal_d = lax.optimization_barrier(
        (next_m, prev_m, far_m, pre0, goal_s, goal_d))
    next_o, prev_o, far_o = swap(next_m), swap(prev_m), swap(far_m)
    opp = opp_g.reshape(HALF, OPP_COLS)
    slots = [(own, own_o), (next_m, next_o), (opp, swap(opp)), (prev_m, prev_o)]
    flat = [w for pair in slots for w in pair]
    in_vmem = pl.BlockSpec(memory_space=pltpu.VMEM)
    anywhere = pl.BlockSpec(memory_space=pl.ANY)
    in_smem = pl.BlockSpec(memory_space=pltpu.SMEM)
    params = pltpu.CompilerParams(vmem_limit_bytes=VMEM_LIMIT)
    pred_s, pred_d, pre, score, loss = pl.pallas_call(
        forward_kernel,
        out_shape=(
            jax.ShapeDtypeStruct((rows, SAM), F32),
            jax.ShapeDtypeStruct((4, rows, DINO_Q), F32),
            jax.ShapeDtypeStruct((4, rows, HALF), F32),
            jax.ShapeDtypeStruct((rows, 4), F32),
            jax.ShapeDtypeStruct((16, 1, 128), F32),
        ),
        in_specs=[in_smem] + [in_vmem] * 6 + [anywhere] * 10,
        out_specs=(in_vmem,) * 5,
        scratch_shapes=[
            pltpu.VMEM((4, rows, HALF), BF16),
            pltpu.VMEM((6, HALF, HALF), BF16),
            pltpu.VMEM((8, HALF, DINO_Q), BF16),
            pltpu.VMEM((2, HALF, SAM), BF16),
            pltpu.SemaphoreType.DMA((18,)),
        ],
        compiler_params=params,
        name="forward",
    )(place, tok_m, tok_o, pre0, goal_s, goal_d, live, *flat, far_m, far_o)

    loss = lax.all_to_all(loss, ("x", "ylo", "core"), split_axis=0, concat_axis=0, tiled=True)
    hid = pl.pallas_call(
        hidden_kernel,
        out_shape=jax.ShapeDtypeStruct((4, rows, HALF), BF16),
        in_specs=[in_smem] + [in_vmem] * 7 + [anywhere] * 10,
        out_specs=in_vmem,
        scratch_shapes=[
            pltpu.VMEM((8, HALF, DINO_Q), BF16),
            pltpu.VMEM((2, HALF, SAM), BF16),
            pltpu.SemaphoreType.DMA((12,)),
        ],
        compiler_params=params,
        name="hidden",
    )(place, pred_s, pred_d, goal_s, goal_d, score, scale, pre, *flat, far_m, far_o)

    loss = jnp.broadcast_to(jnp.sum(loss, axis=0, keepdims=True), (32, 1, 128))
    loss, hid = lax.optimization_barrier((loss, hid))
    loss = lax.all_to_all(loss, ("z", "yhi"), split_axis=0, concat_axis=0, tiled=True)
    loss = jnp.sum(loss[:, 0, 0]) / count

    grad = pl.pallas_call(
        grad_kernel,
        out_shape=jax.ShapeDtypeStruct((rows, 2 * HALF), BF16),
        in_specs=[in_smem, in_vmem] + [anywhere] * 8,
        out_specs=in_vmem,
        scratch_shapes=[pltpu.VMEM((8, HALF, HALF), BF16), pltpu.SemaphoreType.DMA((8,))],
        compiler_params=params,
        name="grad",
    )(place, hid, *flat)
    return (grad, loss)


def solution(mesh):
    fine = Mesh(mesh.devices.reshape(4, 2, 8, 2, 4), AXES)
    tokens = P(AXES, None)
    rest = ("ylo", "z", "core", "yhi")
    return jax.shard_map(
        shards,
        mesh=fine,
        in_specs=(
            tokens,
            P(None, rest, "x"),
            P(None, rest, "x"),
            P(),
            P(),
            P(),
            P(rest, None),
            P(rest, None),
            P(rest, None),
            P(rest, None),
        ),
        out_specs=(tokens, P()),
        check_vma=False,
    )
```

time: 171 us -> 164 us (0.959)
  matrix products: 13.6 us -> 5.02 us
  local copies, waits for them, and re-layouts: 15.1 us -> 23.4 us
  waiting for transfers between devices: 34.9 us -> 29.4 us
  starting transfers between devices: 74 us -> 71.5 us
    all_to_all x4, waiting for transfers between devices: 32.6 us -> 13 us  [the longest x2 9.61 us: gather_plane(): return lax.all_to_all(many, PLANE, split_axis=0, concat_axis=0, tiled=True)]
    ppermute x0 -> x1, waiting for transfers between devices: none -> 15 us  [shards(): far_m = lax.ppermute(own[:, HALF:HALF + FAR], 'x', ring(4, 2))]
    all_to_all x4, starting transfers between devices: 43.6 us -> 33.7 us  [the longest x2 23.9 us: gather_plane(): return lax.all_to_all(many, PLANE, split_axis=0, concat_axis=0, tiled=True)]
    dot_general x8 -> x5, matrix products: 10.4 us -> 5.02 us  [dot(): return jnp.dot(a, b, preferred_element_type=F32)]
    ppermute x4 -> x5, starting transfers between devices: 13.2 us -> 17.3 us  [swap(): return lax.ppermute(value, 'core', ring(2, 1))]
    another operation x1 -> x8, local copies, waits for them, and re-layouts: 0.01 us -> 3.63 us  [the longest x4 3.62 us: shards(): feat_d = jnp.stack([g[:, :DINO_Q] for g in got]).astype(F32)]
    ppermute x0 -> x1, starting transfers between devices: none -> 3.44 us  [shards(): far_m = lax.ppermute(own[:, HALF:HALF + FAR], 'x', ring(4, 2))]
    dot_general x2 -> x0, matrix products: 3.18 us -> none  [dot_t(): lax.dot_general(a, b, (((1,), (1,)), ((), ())), preferred_element_type=F32)]
  transfers between devices with their start and end apart: 13 -> 15, of which waited for: 6 -> 4; matrix products, arithmetic and copies ran while one was open for 16% -> 16% of each run, Pallas kernels for 8% -> 9%
where the time goes in v4:
time: 164 us; the launch traced here: 162 us
  starting transfers between devices  71.5 us (44%)
  waiting for transfers between devices  29.4 us (18%)
  local copies, waits for them, and re-layouts  23.4 us (14%)
  Pallas kernels  21.9 us (13%)
  other arithmetic  6.8 us (4%)
  matrix products  5.02 us (3%)
  between operations  3.98 us (2%)
    all_to_all x2, starting transfers between devices, gather_plane(): return lax.all_to_all(many, PLANE, split_axis=0, concat_axis=0, tiled=True)  23.9 us
    ppermute x5, starting transfers between devices, swap(): return lax.ppermute(value, 'core', ring(2, 1))  17.3 us
    ppermute x1, waiting for transfers between devices, shards(): far_m = lax.ppermute(own[:, HALF:HALF + FAR], 'x', ring(4, 2))  15 us
    ppermute x3, starting transfers between devices, shards(): lax.ppermute(feat_for(s), 'x', ring(4, -s))  10.5 us
    all_to_all x2, waiting for transfers between devices, gather_plane(): return lax.all_to_all(many, PLANE, split_axis=0, concat_axis=0, tiled=True)  9.61 us
    pallas_call x1, Pallas kernels, shards(): pl.pallas_call(forward_kernel, out_shape=(jax.ShapeDtypeStruct((rows, SAM...  7.79 us
    pallas_call x1, Pallas kernels, shards(): pl.pallas_call(grad_kernel, out_shape=jax.ShapeDtypeStruct((rows, 2 * HAL...  7.64 us
    pallas_call x1, Pallas kernels, shards(): pl.pallas_call(hidden_kernel, out_shape=jax.ShapeDtypeStruct((4, rows, HA...  6.5 us
  transfers between devices with their start and end apart: 15, of which 4 were waited for; matrix products, arithmetic and copies ran while one was open for 16% of the time, Pallas kernels for 9%

profile of v4, /device:TPU:1, one launch (start us, length us, event | category | flops | bytes accessed | tf_op | source)
XLA Modules:
  0.0 162.0 jit_solution(2986533459500483705)
XLA Ops:
  0.8 0.7 constant_dynamic-slice_fusion.2
  1.5 1.5 fusion.45
  3.1 1.8 %broadcast_in_dim.13 = bf16[64,5,2,1024]{3,2,1,0:T(2,128)(2,1)} broadcast(bf16[5,2,1024]{2,1,0:T(2,128)(2,1)S(1)} %maximum_bitcast_fusion), dimensions={1,2,3} | broadcast | bytes 1331200 | tf_op jit(solution)/shard_map/broadcast_in_dim | solution.py:200
  4.8 17.3 %all-to-all-start = ((bf16[64,5,2,1024]{3,2,1,0:T(2,128)(2,1)}), bf16[64,5,2,1024]{3,2,1,0:T(2,128)(2,1)S(1)}, u32[]{:S(2)}, u32[]{:S(2)}) async-start(bf16[64,5,2,1024]{3,2,1,0:T(2,128)(2,1)} %broadcast_in_dim.13), calls=%async_computation | async-start | bytes 2621440 | tf_op jit(solution)/shard_map/all_to_all | solution.py:203
  22.2 0.7 constant_dynamic-slice_fusion
  23.2 0.1 concatenate.69
  23.4 1.8 %broadcast_in_dim.15 = bf16[64,5,2,1024]{3,2,1,0:T(2,128)(2,1)} broadcast(bf16[5,2,1024]{2,1,0:T(2,128)(2,1)S(1)} %bitcast.38), dimensions={1,2,3} | broadcast | bytes 1331200 | tf_op jit(solution)/shard_map/broadcast_in_dim | solution.py:200
  25.1 0.1 copy.33
  25.4 0.1 maximum_maximum_fusion
  25.5 0.8 dynamic-slice_bitcast_fusion
  26.3 3.1 %collective-permute-start.2 = (bf16[128,512]{1,0:T(8,128)(2,1)}, bf16[128,512]{1,0:T(8,128)(2,1)}, u32[]{:S(2)}, u32[]{:S(2)}) collective-permute-start(bf16[128,512]{1,0:T(8,128)(2,1)} %get-tuple-element.78), channel_id=1, source_target_pairs={{0,128},{128,256},{256,384},{384,0},{1,129},{129,257},{257,385},{3... | collective-permute-start | bytes 393224 | tf_op jit(solution)/shard_map/ppermute | solution.py:216
  29.4 4.4 %collective-permute-start.1 = (bf16[128,512]{1,0:T(8,128)(2,1)}, bf16[128,512]{1,0:T(8,128)(2,1)S(1)}, u32[]{:S(2)}, u32[]{:S(2)}) collective-permute-start(bf16[128,512]{1,0:T(8,128)(2,1)} %get-tuple-element.79), channel_id=1, source_target_pairs={{0,256},{128,384},{256,0},{384,128},{1,257},{129,385},{257,1},{385... | collective-permute-start | bytes 393224 | tf_op jit(solution)/shard_map/ppermute | solution.py:216
  33.8 3.1 %collective-permute-start = (bf16[128,512]{1,0:T(8,128)(2,1)}, bf16[128,512]{1,0:T(8,128)(2,1)S(1)}, u32[]{:S(2)}, u32[]{:S(2)}) collective-permute-start(bf16[128,512]{1,0:T(8,128)(2,1)} %get-tuple-element.80), channel_id=1, source_target_pairs={{0,384},{128,0},{256,128},{384,256},{1,385},{129,1},{257,129},{385... | collective-permute-start | bytes 393224 | tf_op jit(solution)/shard_map/ppermute | solution.py:216
  36.9 0.6 dynamic_slice.79
  37.5 0.7 clamp_reduce_fusion
  38.1 1.2 fusion.57.live
  39.3 0.7 fusion.42.tok_m
  40.1 1.4 fusion.39.tok_o
  41.5 0.6 pad_add_fusion.where
  42.9 1.2 fusion.56.scale
  44.1 9.6 %all-to-all-done = bf16[64,5,2,1024]{3,2,1,0:T(2,128)(2,1)S(1)} async-done(((bf16[64,5,2,1024]{3,2,1,0:T(2,128)(2,1)}), bf16[64,5,2,1024]{3,2,1,0:T(2,128)(2,1)S(1)}, u32[]{:S(2)}, u32[]{:S(2)}) %all-to-all-start) | async-done | bytes 1310752 | tf_op jit(solution)/shard_map/all_to_all | solution.py:203
  53.7 0.5 reshape.212.m0
  54.3 0.6 copy-done.12
  54.9 0.7 copy-done.13
  55.6 0.3 fusion.49
  55.9 6.5 %collective-permute-start.6 = (bf16[640,1024]{1,0:T(8,128)(2,1)S(1)}, bf16[640,1024]{1,0:T(8,128)(2,1)S(1)}, u32[]{:S(2)}, u32[]{:S(2)}) collective-permute-start(bf16[640,1024]{1,0:T(8,128)(2,1)S(1)} %reshape.212.m0), channel_id=1, source_target_pairs={{0,4},{4,0},{1,5},{5,1},{2,6},{6,2},{3,7},{7,3},{8,12},{12,8},{9,1... | collective-permute-start | bytes 3932168 | tf_op jit(solution)/shard_map/ppermute | solution.py:234
  62.5 0.1 fusion.71
  62.8 0.8 slice.36
  63.6 3.1 %collective-permute-start.4 = (bf16[640,1024]{1,0:T(8,128)(2,1)S(1)}, bf16[640,1024]{1,0:T(8,128)(2,1)}, u32[]{:S(2)}, u32[]{:S(2)}) collective-permute-start(bf16[640,1024]{1,0:T(8,128)(2,1)S(1)} %reshape.212.m0), channel_id=1, source_target_pairs={{0,128},{128,256},{256,384},{384,0},{1,129},{129,257},{257,385},{3... | collective-permute-start | bytes 3932168 | tf_op jit(solution)/shard_map/ppermute | solution.py:246
  66.7 3.4 %collective-permute-start.3 = (bf16[640,1024]{1,0:T(8,128)(2,1)S(1)}, bf16[640,1024]{1,0:T(8,128)(2,1)}, u32[]{:S(2)}, u32[]{:S(2)}) collective-permute-start(bf16[640,1024]{1,0:T(8,128)(2,1)S(1)} %reshape.212.m0), channel_id=1, source_target_pairs={{0,384},{128,0},{256,128},{384,256},{1,385},{129,1},{257,129},{385... | collective-permute-start | bytes 3932168 | tf_op jit(solution)/shard_map/ppermute | solution.py:245
  70.1 6.6 %all-to-all-start.1 = ((bf16[64,5,2,1024]{3,2,1,0:T(2,128)(2,1)}), bf16[64,5,2,1024]{3,2,1,0:T(2,128)(2,1)}, u32[]{:S(2)}, u32[]{:S(2)}) async-start(bf16[64,5,2,1024]{3,2,1,0:T(2,128)(2,1)} %broadcast_in_dim.15), calls=%async_computation.1 | async-start | bytes 2621440 | tf_op jit(solution)/shard_map/all_to_all | solution.py:203
  76.7 3.4 %collective-permute-start.5 = (bf16[640,256]{1,0:T(8,128)(2,1)}, bf16[640,256]{1,0:T(8,128)(2,1)S(1)}, u32[]{:S(2)}, u32[]{:S(2)}) collective-permute-start(bf16[640,256]{1,0:T(8,128)(2,1)} %slice.36), channel_id=1, source_target_pairs={{0,256},{128,384},{256,0},{384,128},{1,257},{129,385},{257,1},{385... | collective-permute-start | bytes 983048 | tf_op jit(solution)/shard_map/ppermute | solution.py:247
  80.2 0.8 slice_bitcast_fusion.7
  81.0 0.8 slice_bitcast_fusion.6
  81.8 0.8 slice_bitcast_fusion.5
  82.6 0.9 slice_bitcast_fusion.3
  83.5 0.9 slice_bitcast_fusion.2
  84.4 0.9 slice_bitcast_fusion.1
  85.3 0.9 slice_bitcast_fusion
  86.2 0.8 slice_bitcast_fusion.4
  87.0 0.2 convert_reduce_fusion.1
  87.2 0.2 convert_reduce_fusion
  87.4 1.0 fusion.53.goal_d
  88.4 0.8 multiply_convert_fusion.goal_s
  89.2 1.1 convolution_add_fusion.pre0
  90.3 15.0 %collective-permute-done.5.mf = bf16[640,256]{1,0:T(8,128)(2,1)S(1)} collective-permute-done((bf16[640,256]{1,0:T(8,128)(2,1)}, bf16[640,256]{1,0:T(8,128)(2,1)S(1)}, u32[]{:S(2)}, u32[]{:S(2)}) %collective-permute-start.5) | collective-permute-done | bytes 327712 | tf_op jit(solution)/shard_map/ppermute | solution.py:247
  105.2 0.7 copy-done.6
  106.0 2.6 %collective-permute-start.7 = (bf16[640,1024]{1,0:T(8,128)(2,1)}, bf16[640,1024]{1,0:T(8,128)(2,1)S(1)}, u32[]{:S(2)}, u32[]{:S(2)}) collective-permute-start(bf16[640,1024]{1,0:T(8,128)(2,1)} %collective-permute-done.3.m1), channel_id=1, source_target_pairs={{0,4},{4,0},{1,5},{5,1},{2,6},{6,2},{3,7},{7,3},{8,12},{12,8},{9,1... | collective-permute-start | bytes 3932168 | tf_op jit(solution)/shard_map/ppermute | solution.py:234
  108.6 2.1 %collective-permute-start.9 = (bf16[640,1024]{1,0:T(8,128)(2,1)}, bf16[640,1024]{1,0:T(8,128)(2,1)}, u32[]{:S(2)}, u32[]{:S(2)}) collective-permute-start(bf16[640,1024]{1,0:T(8,128)(2,1)} %collective-permute-done.4.m3), channel_id=1, source_target_pairs={{0,4},{4,0},{1,5},{5,1},{2,6},{6,2},{3,7},{7,3},{8,12},{12,8},{9,1... | collective-permute-start | bytes 3932168 | tf_op jit(solution)/shard_map/ppermute | solution.py:234
  110.6 3.2 %reshape.214.m2 = bf16[640,1024]{1,0:T(8,128)(2,1)S(1)} reshape(bf16[64,5,2,1024]{3,2,1,0:T(2,128)(2,1)} %all-to-all-done.1) | data formatting | bytes 2621440 | tf_op jit(solution)/shard_map/reshape | solution.py:261
  113.9 4.0 %collective-permute-start.8 = (bf16[640,1024]{1,0:T(8,128)(2,1)S(1)}, bf16[640,1024]{1,0:T(8,128)(2,1)S(1)}, u32[]{:S(2)}, u32[]{:S(2)}) collective-permute-start(bf16[640,1024]{1,0:T(8,128)(2,1)S(1)} %reshape.214.m2), channel_id=1, source_target_pairs={{0,4},{4,0},{1,5},{5,1},{2,6},{6,2},{3,7},{7,3},{8,12},{12,8},{9,1... | collective-permute-start | bytes 3932168 | tf_op jit(solution)/shard_map/ppermute | solution.py:234
  117.9 2.1 %collective-permute-start.10 = (bf16[640,256]{1,0:T(8,128)(2,1)S(1)}, bf16[640,256]{1,0:T(8,128)(2,1)S(1)}, u32[]{:S(2)}, u32[]{:S(2)}) collective-permute-start(bf16[640,256]{1,0:T(8,128)(2,1)S(1)} %copy-done.7), channel_id=1, source_target_pairs={{0,4},{4,0},{1,5},{5,1},{2,6},{6,2},{3,7},{7,3},{8,12},{12,8},{9,1... | collective-permute-start | bytes 983048 | tf_op jit(solution)/shard_map/ppermute | solution.py:234
  120.0 1.4 collective-permute-done.10.of
  121.4 0.7 copy-done.8
  122.1 0.5 copy-done.4
  122.6 1.1 copy-done.5
  123.7 7.8 %forward.1 = (f32[128,256]{1,0:T(8,128)}, f32[4,128,384]{2,1,0:T(8,128)}, f32[4,128,640]{2,1,0:T(8,128)}, f32[128,4]{1,0:T(8,128)}, f32[16,1,128]{2,1,0:T(1,128)}) custom-call(s32[2]{0:T(128)} %pad_add_fusion.where, bf16[128,640]{1,0:T(8,128)(2,1)} %copy-done.9, bf16[128,640]{1,0:T(8,128)(2,1)} %fusion.39.tok_o, f32[128,640]{1,0:T(8,128)} %convolution_add_fusion.pre0, ...), custom_call_target="tpu_custom_call" | custom-call | tf_op jit(solution)/shard_map/forward/pallas_call | solution.py:268
  131.5 3.9 %all-to-all-start.2 = ((f32[16,1,128]{2,1,0:T(1,128)}), f32[16,1,128]{2,1,0:T(1,128)S(1)}, u32[]{:S(2)}, u32[]{:S(2)}) async-start(f32[16,1,128]{2,1,0:T(1,128)} %get-tuple-element.62), calls=%async_computation.2 | async-start | bytes 16384 | tf_op jit(solution)/shard_map/all_to_all | solution.py:290
  135.4 6.5 %hidden.1.hid = bf16[4,128,640]{2,1,0:T(8,128)(2,1)} custom-call(s32[2]{0:T(128)} %pad_add_fusion.where, f32[128,256]{1,0:T(8,128)} %get-tuple-element.63.pred_s, f32[4,128,384]{2,1,0:T(8,128)} %get-tuple-element.64.pred_d, bf16[128,256]{1,0:T(8,128)(2,1)} %multiply_convert_fusion.goal_s, bf16[4,128,384]{2,1,0:T(8,128)(2,1)} %fusion.53.goal_d, ...), custom_call_target="tpu_custom_call" | custom-call | tf_op jit(solution)/shard_map/hidden/pallas_call | solution.py:291
  142.0 0.6 broadcast_in_dim.17
  142.6 5.9 %all-to-all-start.3 = ((f32[32,1,128]{2,1,0:T(1,128)}), f32[32,1,128]{2,1,0:T(1,128)S(1)}, u32[]{:S(2)}, u32[]{:S(2)}) async-start(f32[32,1,128]{2,1,0:T(1,128)} %broadcast_in_dim.17), calls=%async_computation.3 | async-start | bytes 32768 | tf_op jit(solution)/shard_map/all_to_all | solution.py:307
  148.5 7.6 %grad.1 = bf16[128,1280]{1,0:T(8,128)(2,1)} custom-call(s32[2]{0:T(128)} %pad_add_fusion.where, bf16[4,128,640]{2,1,0:T(8,128)(2,1)} %hidden.1.hid, bf16[640,1024]{1,0:T(8,128)(2,1)} %copy-done.1, bf16[640,1024]{1,0:T(8,128)(2,1)} %copy-done.3, bf16[640,1024]{1,0:T(8,128)(2,1)} %collective-permute-done.3.m1, bf16[640,1024]{1,0:T(8,128)(2,1)} %copy-done.4, ...), custom_call_target="tpu_custom_call" | custom-call | tf_op jit(solution)/shard_map/grad/pallas_call | solution.py:310
  156.2 3.4 %all-to-all-done.3 = f32[32,1,128]{2,1,0:T(1,128)S(1)} async-done(((f32[32,1,128]{2,1,0:T(1,128)}), f32[32,1,128]{2,1,0:T(1,128)S(1)}, u32[]{:S(2)}, u32[]{:S(2)}) %all-to-all-start.3) | async-done | bytes 16416 | tf_op jit(solution)/shard_map/all_to_all | solution.py:307
  159.5 0.6 slice_reduce_fusion
  (71 shorter events, 0.8 us)
Async XLA Ops:
  0.6 38.7 %copy-start = (bf16[128,1280]{1,0:T(8,128)(2,1)S(1)}, bf16[128,1280]{1,0:T(8,128)(2,1)}, u32[]{:S(2)}) copy-start(bf16[128,1280]{1,0:T(8,128)(2,1)} %param.10) | copy-start | bytes 983044
  4.8 18.2 %copy-start.15 = (bf16[10,256]{1,0:T(8,128)(2,1)S(1)}, bf16[10,256]{1,0:T(8,128)(2,1)}, u32[]{:S(2)}) copy-start(bf16[10,256]{1,0:T(8,128)(2,1)} %param.17) | copy-start | bytes 15364
  4.8 48.9 %all-to-all-start = ((bf16[64,5,2,1024]{3,2,1,0:T(2,128)(2,1)}), bf16[64,5,2,1024]{3,2,1,0:T(2,128)(2,1)S(1)}, u32[]{:S(2)}, u32[]{:S(2)}) async-start(bf16[64,5,2,1024]{3,2,1,0:T(2,128)(2,1)} %broadcast_in_dim.13), calls=%async_computation | async-start | bytes 2621440 | tf_op jit(solution)/shard_map/all_to_all | solution.py:203
  22.1 3.0 %copy-start.14 = (bf16[4,128,64]{1,2,0:T(8,128)(2,1)S(1)}, bf16[4,128,64]{1,2,0:T(8,128)(2,1)}, u32[]{:S(2)}) copy-start(bf16[4,128,64]{1,2,0:T(8,128)(2,1)} %param.11) | copy-start | bytes 196612
  22.1 3.3 %copy-start.11 = (bf16[4,128,384]{2,1,0:T(8,128)(2,1)S(1)}, bf16[4,128,384]{2,1,0:T(8,128)(2,1)}, u32[]{:S(2)}) copy-start(bf16[4,128,384]{2,1,0:T(8,128)(2,1)} %param.12) | copy-start | bytes 1179652
  25.1 11.8 %copy-start.18 = (s32[64]{0:T(128)S(1)}, s32[64]{0:T(128)}, u32[]{:S(2)}) copy-start(s32[64]{0:T(128)} %param.15) | copy-start | bytes 772
  26.3 28.0 %collective-permute-start.2 = (bf16[128,512]{1,0:T(8,128)(2,1)}, bf16[128,512]{1,0:T(8,128)(2,1)}, u32[]{:S(2)}, u32[]{:S(2)}) collective-permute-start(bf16[128,512]{1,0:T(8,128)(2,1)} %get-tuple-element.78), channel_id=1, source_target_pairs={{0,128},{128,256},{256,384},{384,0},{1,129},{129,257},{257,385},{3... | collective-permute-start | bytes 393224 | tf_op jit(solution)/shard_map/ppermute | solution.py:216
  29.4 24.8 %collective-permute-start.1 = (bf16[128,512]{1,0:T(8,128)(2,1)}, bf16[128,512]{1,0:T(8,128)(2,1)S(1)}, u32[]{:S(2)}, u32[]{:S(2)}) collective-permute-start(bf16[128,512]{1,0:T(8,128)(2,1)} %get-tuple-element.79), channel_id=1, source_target_pairs={{0,256},{128,384},{256,0},{384,128},{1,257},{129,385},{257,1},{385... | collective-permute-start | bytes 393224 | tf_op jit(solution)/shard_map/ppermute | solution.py:216
  33.8 20.5 %collective-permute-start = (bf16[128,512]{1,0:T(8,128)(2,1)}, bf16[128,512]{1,0:T(8,128)(2,1)S(1)}, u32[]{:S(2)}, u32[]{:S(2)}) collective-permute-start(bf16[128,512]{1,0:T(8,128)(2,1)} %get-tuple-element.80), channel_id=1, source_target_pairs={{0,384},{128,0},{256,128},{384,256},{1,385},{129,1},{257,129},{385... | collective-permute-start | bytes 393224 | tf_op jit(solution)/shard_map/ppermute | solution.py:216
  40.1 15.5 %copy-start.9 = (bf16[128,640]{1,0:T(8,128)(2,1)}, bf16[128,640]{1,0:T(8,128)(2,1)S(1)}, u32[]{:S(2)}) copy-start(bf16[128,640]{1,0:T(8,128)(2,1)S(1)} %fusion.42.tok_m) | copy-start | bytes 491524
  54.2 15.9 %copy-start.1 = (bf16[640,1024]{1,0:T(8,128)(2,1)}, bf16[640,1024]{1,0:T(8,128)(2,1)S(1)}, u32[]{:S(2)}) copy-start(bf16[640,1024]{1,0:T(8,128)(2,1)S(1)} %reshape.212.m0) | copy-start | bytes 3932164
  54.2 8.3 %copy-start.16 = (f32[1536]{0:T(1024)S(1)}, f32[1536]{0:T(1024)}, u32[]{:S(2)}) copy-start(f32[1536]{0:T(1024)} %param.14) | copy-start | bytes 18436
  54.2 8.4 %copy-start.17 = (f32[256]{0:T(256)S(1)}, f32[256]{0:T(256)}, u32[]{:S(2)}) copy-start(f32[256]{0:T(256)} %param.13) | copy-start | bytes 3076
  54.3 0.7 copy-start.12
  54.9 0.7 copy-start.13
  55.9 24.3 %collective-permute-start.6 = (bf16[640,1024]{1,0:T(8,128)(2,1)S(1)}, bf16[640,1024]{1,0:T(8,128)(2,1)S(1)}, u32[]{:S(2)}, u32[]{:S(2)}) collective-permute-start(bf16[640,1024]{1,0:T(8,128)(2,1)S(1)} %reshape.212.m0), channel_id=1, source_target_pairs={{0,4},{4,0},{1,5},{5,1},{2,6},{6,2},{3,7},{7,3},{8,12},{12,8},{9,1... | collective-permute-start | bytes 3932168 | tf_op jit(solution)/shard_map/ppermute | solution.py:234
  63.6 41.6 %collective-permute-start.4 = (bf16[640,1024]{1,0:T(8,128)(2,1)S(1)}, bf16[640,1024]{1,0:T(8,128)(2,1)}, u32[]{:S(2)}, u32[]{:S(2)}) collective-permute-start(bf16[640,1024]{1,0:T(8,128)(2,1)S(1)} %reshape.212.m0), channel_id=1, source_target_pairs={{0,128},{128,256},{256,384},{384,0},{1,129},{129,257},{257,385},{3... | collective-permute-start | bytes 3932168 | tf_op jit(solution)/shard_map/ppermute | solution.py:246
  66.7 38.5 %collective-permute-start.3 = (bf16[640,1024]{1,0:T(8,128)(2,1)S(1)}, bf16[640,1024]{1,0:T(8,128)(2,1)}, u32[]{:S(2)}, u32[]{:S(2)}) collective-permute-start(bf16[640,1024]{1,0:T(8,128)(2,1)S(1)} %reshape.212.m0), channel_id=1, source_target_pairs={{0,384},{128,0},{256,128},{384,256},{1,385},{129,1},{257,129},{385... | collective-permute-start | bytes 3932168 | tf_op jit(solution)/shard_map/ppermute | solution.py:245
  70.1 40.5 %all-to-all-start.1 = ((bf16[64,5,2,1024]{3,2,1,0:T(2,128)(2,1)}), bf16[64,5,2,1024]{3,2,1,0:T(2,128)(2,1)}, u32[]{:S(2)}, u32[]{:S(2)}) async-start(bf16[64,5,2,1024]{3,2,1,0:T(2,128)(2,1)} %broadcast_in_dim.15), calls=%async_computation.1 | async-start | bytes 2621440 | tf_op jit(solution)/shard_map/all_to_all | solution.py:203
  76.7 28.5 %collective-permute-start.5 = (bf16[640,256]{1,0:T(8,128)(2,1)}, bf16[640,256]{1,0:T(8,128)(2,1)S(1)}, u32[]{:S(2)}, u32[]{:S(2)}) collective-permute-start(bf16[640,256]{1,0:T(8,128)(2,1)} %slice.36), channel_id=1, source_target_pairs={{0,256},{128,384},{256,0},{384,128},{1,257},{129,385},{257,1},{385... | collective-permute-start | bytes 983048 | tf_op jit(solution)/shard_map/ppermute | solution.py:247
  80.2 9.0 %copy-start.3 = (bf16[640,1024]{1,0:T(8,128)(2,1)}, bf16[640,1024]{1,0:T(8,128)(2,1)S(1)}, u32[]{:S(2)}) copy-start(bf16[640,1024]{1,0:T(8,128)(2,1)S(1)} %collective-permute-done.6.o0) | copy-start | bytes 3932164
  81.0 8.2 %copy-start.10 = (bf16[128,640]{1,0:T(8,128)(2,1)S(1)}, bf16[128,640]{1,0:T(8,128)(2,1)}, u32[]{:S(2)}) copy-start(bf16[128,640]{1,0:T(8,128)(2,1)} %fusion.39.tok_o) | copy-start | bytes 491524
  105.2 0.7 copy-start.6
  106.0 15.4 %collective-permute-start.7 = (bf16[640,1024]{1,0:T(8,128)(2,1)}, bf16[640,1024]{1,0:T(8,128)(2,1)S(1)}, u32[]{:S(2)}, u32[]{:S(2)}) collective-permute-start(bf16[640,1024]{1,0:T(8,128)(2,1)} %collective-permute-done.3.m1), channel_id=1, source_target_pairs={{0,4},{4,0},{1,5},{5,1},{2,6},{6,2},{3,7},{7,3},{8,12},{12,8},{9,1... | collective-permute-start | bytes 3932168 | tf_op jit(solution)/shard_map/ppermute | solution.py:234
  108.6 9.3 %copy-start.7 = (bf16[640,256]{1,0:T(8,128)(2,1)S(1)}, bf16[640,256]{1,0:T(8,128)(2,1)}, u32[]{:S(2)}) copy-start(bf16[640,256]{1,0:T(8,128)(2,1)} %copy-done.6) | copy-start | bytes 983044
  108.6 12.8 %collective-permute-start.9 = (bf16[640,1024]{1,0:T(8,128)(2,1)}, bf16[640,1024]{1,0:T(8,128)(2,1)}, u32[]{:S(2)}, u32[]{:S(2)}) collective-permute-start(bf16[640,1024]{1,0:T(8,128)(2,1)} %collective-permute-done.4.m3), channel_id=1, source_target_pairs={{0,4},{4,0},{1,5},{5,1},{2,6},{6,2},{3,7},{7,3},{8,12},{12,8},{9,1... | collective-permute-start | bytes 3932168 | tf_op jit(solution)/shard_map/ppermute | solution.py:234
  113.8 7.6 %copy-start.2 = (bf16[640,1024]{1,0:T(8,128)(2,1)}, bf16[640,1024]{1,0:T(8,128)(2,1)S(1)}, u32[]{:S(2)}) copy-start(bf16[640,1024]{1,0:T(8,128)(2,1)S(1)} %reshape.214.m2) | copy-start | bytes 3932164
  113.9 7.5 %collective-permute-start.8 = (bf16[640,1024]{1,0:T(8,128)(2,1)S(1)}, bf16[640,1024]{1,0:T(8,128)(2,1)S(1)}, u32[]{:S(2)}, u32[]{:S(2)}) collective-permute-start(bf16[640,1024]{1,0:T(8,128)(2,1)S(1)} %reshape.214.m2), channel_id=1, source_target_pairs={{0,4},{4,0},{1,5},{5,1},{2,6},{6,2},{3,7},{7,3},{8,12},{12,8},{9,1... | collective-permute-start | bytes 3932168 | tf_op jit(solution)/shard_map/ppermute | solution.py:234
  117.9 3.5 %collective-permute-start.10 = (bf16[640,256]{1,0:T(8,128)(2,1)S(1)}, bf16[640,256]{1,0:T(8,128)(2,1)S(1)}, u32[]{:S(2)}, u32[]{:S(2)}) collective-permute-start(bf16[640,256]{1,0:T(8,128)(2,1)S(1)} %copy-done.7), channel_id=1, source_target_pairs={{0,4},{4,0},{1,5},{5,1},{2,6},{6,2},{3,7},{7,3},{8,12},{12,8},{9,1... | collective-permute-start | bytes 983048 | tf_op jit(solution)/shard_map/ppermute | solution.py:234
  121.4 0.7 copy-start.8
  121.4 1.2 copy-start.4
  122.6 1.1 copy-start.5
  131.5 10.5 %all-to-all-start.2 = ((f32[16,1,128]{2,1,0:T(1,128)}), f32[16,1,128]{2,1,0:T(1,128)S(1)}, u32[]{:S(2)}, u32[]{:S(2)}) async-start(f32[16,1,128]{2,1,0:T(1,128)} %get-tuple-element.62), calls=%async_computation.2 | async-start | bytes 16384 | tf_op jit(solution)/shard_map/all_to_all | solution.py:290
  142.6 16.9 %all-to-all-start.3 = ((f32[32,1,128]{2,1,0:T(1,128)}), f32[32,1,128]{2,1,0:T(1,128)S(1)}, u32[]{:S(2)}, u32[]{:S(2)}) async-start(f32[32,1,128]{2,1,0:T(1,128)} %broadcast_in_dim.17), calls=%async_computation.3 | async-start | bytes 32768 | tf_op jit(solution)/shard_map/all_to_all | solution.py:307

commit v5 on v4

--- a/solution.py
+++ b/solution.py
@@ -15,9 +15,7 @@
 SAM_Q = 64
 SAM = 256
 FEAT_Q = 512
-FAR = 256
 COLS = HALF + DINO_Q
-OPP_COLS = COLS - FAR + SAM
 F32 = jnp.float32
 BF16 = jnp.bfloat16
 VMEM_LIMIT = 56 * 1024 * 1024
@@ -54,27 +52,35 @@
     ]
 
 
-def far_copies(opp, far, buf, at, sems, first):
-    low, high = pl.ds(0, FAR), pl.ds(FAR, DINO_Q - FAR)
-    out = []
-    for i, (a, b) in enumerate(zip(opp, far)):
-        out.append(pltpu.make_async_copy(b, buf.at[at + i, :, low], sems.at[first + 2 * i]))
-        source = a.at[:, pl.ds(HALF, DINO_Q - FAR)]
-        out.append(pltpu.make_async_copy(source, buf.at[at + i, :, high], sems.at[first + 2 * i + 1]))
-    return out
+def target_kernel(f0, f1, f2, f3, gain_s, gain_d, goal_s, goal_d):
+    parts = [f[...].astype(F32) for f in (f0, f1, f2, f3)]
+
+    def center_of(lo, hi):
+        cut = [p[:, lo:hi] for p in parts]
+        chans = 4 * (hi - lo)
+        center = sum(jnp.sum(p, axis=1, keepdims=True) for p in cut) / chans
+        square = sum(jnp.sum(p * p, axis=1, keepdims=True) for p in cut) / chans
+        return cut, center, lax.rsqrt(square - center * center + 1e-06)
+
+    cut, center, root = center_of(0, DINO_Q)
+    for j, part in enumerate(cut):
+        goal_d[j] = ((part - center) * root * gain_d[j]).astype(BF16)
+    cut, center, root = center_of(DINO_Q, DINO_Q + SAM_Q)
+    for j, part in enumerate(cut):
+        at = slice(j * SAM_Q, (j + 1) * SAM_Q)
+        goal_s[:, at] = ((part - center) * root * gain_s[:, at]).astype(BF16)
 
 
 def forward_kernel(
     where, tok_m, tok_o, pre0, goal_s, goal_d, live,
-    m0, o0, m1, o1, m2, o2, m3, o3, mf, of,
+    m0, o0, m1, o1, m2, o2, m3, o3,
     pred_s, pred_d, pre, score, part, act, w_in, w_out, w_sam, sems,
 ):
     x, core = where[0], where[1]
     got_in = copies((m1, o1, m3, o3, m2, o2), 0, HALF, w_in, sems)
-    got_out = copies((m0, o0, m1, o1, m3, o3), HALF, COLS, w_out, sems, 6)
-    got_far = far_copies((m2, o2), (mf, of), w_out, 6, sems, 12)
-    got_sam = copies((m2, o2), OPP_COLS - SAM, OPP_COLS, w_sam, sems, 16)
-    for copy in got_in + got_out + got_far + got_sam:
+    got_out = copies((m0, o0, m1, o1, m3, o3, m2, o2), HALF, COLS, w_out, sems, 6)
+    got_sam = copies((m2, o2), COLS, COLS + SAM, w_sam, sems, 14)
+    for copy in got_in + got_out + got_sam:
         copy.start()
     for i, j in enumerate((0, 1, 3, 2)):
         if i == 0:
@@ -93,8 +99,8 @@
     found = [0.0, 0.0, 0.0]
     dm, do = act[2 + core], act[3 - core]
     for i, j in enumerate((0, 1, 3, 2)):
-        for copy in got_out[2 * i:2 * i + 2] or got_far:
-            copy.wait()
+        got_out[2 * i].wait()
+        got_out[2 * i + 1].wait()
         value = dot(dm, w_out[2 * i]) + dot(do, w_out[2 * i + 1])
         pred_d[j] = value
         found = [a + b for a, b in zip(found, sums(value, goal_d[j].astype(F32)))]
@@ -117,14 +123,13 @@
 
 def hidden_kernel(
     where, pred_s, pred_d, goal_s, goal_d, score, scale, pre,
-    m0, o0, m1, o1, m2, o2, m3, o3, mf, of,
+    m0, o0, m1, o1, m2, o2, m3, o3,
     hid, w_out, w_sam, sems,
 ):
     core = where[1]
-    got_sam = copies((m2, o2), OPP_COLS - SAM, OPP_COLS, w_sam, sems)
-    got_out = copies((m0, o0, m1, o1, m3, o3), HALF, COLS, w_out, sems, 2)
-    got_far = far_copies((m2, o2), (mf, of), w_out, 6, sems, 8)
-    for copy in got_sam + got_out + got_far:
+    got_sam = copies((m2, o2), COLS, COLS + SAM, w_sam, sems)
+    got_out = copies((m0, o0, m1, o1, m2, o2, m3, o3), HALF, COLS, w_out, sems, 2)
+    for copy in got_sam + got_out:
         copy.start()
 
     def back(head, pred, goal, chans):
@@ -142,12 +147,11 @@
         copy.wait()
     finish(0, [dot_t(value, w_sam[side]) for side in range(2)])
     found = [0.0, 0.0]
-    for i, j in enumerate((0, 1, 3, 2)):
+    for j in range(4):
         value = back(1, pred_d[j], goal_d[j], 4 * DINO_Q)
-        for copy in got_out[2 * i:2 * i + 2] or got_far:
-            copy.wait()
         for side in range(2):
-            found[side] += dot_t(value, w_out[2 * i + side])
+            got_out[2 * j + side].wait()
+            found[side] += dot_t(value, w_out[2 * j + side])
     finish(1, found)
 
 
@@ -192,9 +196,9 @@
     both = jnp.concatenate([sam_in, dino_in], axis=0)
     picked = dot(both, pick_cols(x % 2)).astype(BF16).reshape(2, shard, HALF)
 
-    def payload(q, first, extra):
+    def payload(q, extra):
         part_in = lax.dynamic_index_in_dim(picked, q // 2, axis=0, keepdims=False)
-        part_d = lax.dynamic_slice(dino_out, (0, q * DINO_Q + first), (shard, DINO_Q - first))
+        part_d = lax.dynamic_slice(dino_out, (0, q * DINO_Q), (shard, DINO_Q))
         part = jnp.concatenate([part_in, part_d] + extra, axis=1)
         cols = part.shape[1]
         return jnp.broadcast_to(part.reshape(1, shard // 2, 2, cols), (64, shard // 2, 2, cols))
@@ -202,11 +206,11 @@
     def gather_plane(many):
         return lax.all_to_all(many, PLANE, split_axis=0, concat_axis=0, tiled=True)
 
-    own_b = payload(x, 0, [])
+    own_b = payload(x, [])
     sam4 = sam_out.reshape(shard, 4, SAM_Q)
     sam_parts = [lax.dynamic_index_in_dim(sam4, (x + j) % 4, axis=1, keepdims=False) for j in range(4)]
     opp_b, dino_maps, sam_maps = lax.optimization_barrier(
-        (payload((x + 2) % 4, FAR, sam_parts), dino_maps, sam_maps))
+        (payload((x + 2) % 4, sam_parts), dino_maps, sam_maps))
     feats = jnp.concatenate(
         [dino_maps, sam_maps, jnp.zeros((4, rows, FEAT_Q - DINO_Q - SAM_Q), BF16)], axis=2)
 
@@ -226,42 +230,39 @@
 
     place = jnp.stack([x, core]).astype(jnp.int32)
     scale = live / count
-    own, opp_b, got, tok_m, tok_o, live, scale, place = lax.optimization_barrier(
-        (own_g.reshape(HALF, COLS), opp_b, got, tok_m, tok_o, live, scale, place))
+    def gains(gain, width):
+        return [lax.dynamic_slice(gain, ((x + j) % 4 * width,), (width,)) for j in range(4)]
+
+    in_vmem = pl.BlockSpec(memory_space=pltpu.VMEM)
+    goal_s, goal_d = pl.pallas_call(
+        target_kernel,
+        out_shape=(
+            jax.ShapeDtypeStruct((rows, SAM), BF16),
+            jax.ShapeDtypeStruct((4, rows, DINO_Q), BF16),
+        ),
+        in_specs=[in_vmem] * 6,
+        out_specs=(in_vmem,) * 2,
+        name="target",
+    )(*got, jnp.concatenate(gains(sam_gain, SAM_Q))[None, :], jnp.stack(gains(dino_gain, DINO_Q))[:, None, :])
+    own, opp_b, goal_s, goal_d, tok_m, tok_o, live, scale, place = lax.optimization_barrier(
+        (own_g.reshape(HALF, COLS), opp_b, goal_s, goal_d, tok_m, tok_o, live, scale, place))
     opp_g = gather_plane(opp_b)
 
     def swap(value):
         return lax.ppermute(value, "core", ring(2, 1))
 
-    def gains(gain, width):
-        return [lax.dynamic_slice(gain, ((x + j) % 4 * width,), (width,)) for j in range(4)]
-
-    def targets(part, gain):
-        chans = 4 * part.shape[2] if part.shape[0] == 4 else part.shape[2]
-        center = jnp.sum(part, axis=(0, 2), keepdims=True) / chans
-        spread = jnp.sum(part * part, axis=(0, 2), keepdims=True) / chans - center * center
-        return ((part - center) * lax.rsqrt(spread + 1e-06) * gain).astype(BF16)
 
     next_m = lax.ppermute(own, "x", ring(4, -1))
     prev_m = lax.ppermute(own, "x", ring(4, 1))
-    far_m = lax.ppermute(own[:, HALF:HALF + FAR], "x", ring(4, 2))
-    pre0 = dot(tok_m, own[:, :HALF])
-    own, pre0 = lax.optimization_barrier((own, pre0))
     own_o = swap(own)
-    own_o, got = lax.optimization_barrier((own_o, got))
-    pre0 += dot(tok_o, own_o[:, :HALF])
-    feat_d = jnp.stack([g[:, :DINO_Q] for g in got]).astype(F32)
-    feat_s = jnp.concatenate([g[:, DINO_Q:DINO_Q + SAM_Q] for g in got], axis=1).astype(F32)
-    goal_d = targets(feat_d, jnp.stack(gains(dino_gain, DINO_Q))[:, None, :])
-    goal_s = targets(feat_s[None], jnp.concatenate(gains(sam_gain, SAM_Q))[None, None, :])[0]
-
-    next_m, prev_m, far_m, pre0, goal_s, goal_d = lax.optimization_barrier(
-        (next_m, prev_m, far_m, pre0, goal_s, goal_d))
-    next_o, prev_o, far_o = swap(next_m), swap(prev_m), swap(far_m)
-    opp = opp_g.reshape(HALF, OPP_COLS)
+    pre0 = dot(tok_m, own[:, :HALF]) + dot(tok_o, own_o[:, :HALF])
+    next_m, prev_m = lax.optimization_barrier((next_m, prev_m))
+    next_o, prev_o = swap(next_m), swap(prev_m)
+    opp_g, pre0 = lax.optimization_barrier((opp_g, pre0))
+    opp = opp_g.reshape(HALF, COLS + SAM)
+    opp, next_o, prev_o = lax.optimization_barrier((opp, next_o, prev_o))
     slots = [(own, own_o), (next_m, next_o), (opp, swap(opp)), (prev_m, prev_o)]
     flat = [w for pair in slots for w in pair]
-    in_vmem = pl.BlockSpec(memory_space=pltpu.VMEM)
     anywhere = pl.BlockSpec(memory_space=pl.ANY)
     in_smem = pl.BlockSpec(memory_space=pltpu.SMEM)
     params = pltpu.CompilerParams(vmem_limit_bytes=VMEM_LIMIT)
@@ -274,37 +275,37 @@
             jax.ShapeDtypeStruct((rows, 4), F32),
             jax.ShapeDtypeStruct((16, 1, 128), F32),
         ),
-        in_specs=[in_smem] + [in_vmem] * 6 + [anywhere] * 10,
+        in_specs=[in_smem] + [in_vmem] * 6 + [anywhere] * 8,
         out_specs=(in_vmem,) * 5,
         scratch_shapes=[
             pltpu.VMEM((4, rows, HALF), BF16),
             pltpu.VMEM((6, HALF, HALF), BF16),
             pltpu.VMEM((8, HALF, DINO_Q), BF16),
             pltpu.VMEM((2, HALF, SAM), BF16),
-            pltpu.SemaphoreType.DMA((18,)),
+            pltpu.SemaphoreType.DMA((16,)),
         ],
         compiler_params=params,
         name="forward",
-    )(place, tok_m, tok_o, pre0, goal_s, goal_d, live, *flat, far_m, far_o)
-
-    loss = lax.all_to_all(loss, ("x", "ylo", "core"), split_axis=0, concat_axis=0, tiled=True)
+    )(place, tok_m, tok_o, pre0, goal_s, goal_d, live, *flat)
+
+    loss = lax.all_to_all(loss, ("z", "core"), split_axis=0, concat_axis=0, tiled=True)
     hid = pl.pallas_call(
         hidden_kernel,
         out_shape=jax.ShapeDtypeStruct((4, rows, HALF), BF16),
-        in_specs=[in_smem] + [in_vmem] * 7 + [anywhere] * 10,
+        in_specs=[in_smem] + [in_vmem] * 7 + [anywhere] * 8,
         out_specs=in_vmem,
         scratch_shapes=[
             pltpu.VMEM((8, HALF, DINO_Q), BF16),
             pltpu.VMEM((2, HALF, SAM), BF16),
-            pltpu.SemaphoreType.DMA((12,)),
+            pltpu.SemaphoreType.DMA((10,)),
         ],
         compiler_params=params,
         name="hidden",
-    )(place, pred_s, pred_d, goal_s, goal_d, score, scale, pre, *flat, far_m, far_o)
+    )(place, pred_s, pred_d, goal_s, goal_d, score, scale, pre, *flat)
 
     loss = jnp.broadcast_to(jnp.sum(loss, axis=0, keepdims=True), (32, 1, 128))
     loss, hid = lax.optimization_barrier((loss, hid))
-    loss = lax.all_to_all(loss, ("z", "yhi"), split_axis=0, concat_axis=0, tiled=True)
+    loss = lax.all_to_all(loss, ("x", "ylo", "yhi"), split_axis=0, concat_axis=0, tiled=True)
     loss = jnp.sum(loss[:, 0, 0]) / count
 
     grad = pl.pallas_call(

time: 164 us -> 160 us (0.976)
  local copies, waits for them, and re-layouts: 23.4 us -> 14.1 us
  waiting for transfers between devices: 29.4 us -> 32.8 us
  Pallas kernels: 21.9 us -> 24.8 us
  starting transfers between devices: 71.5 us -> 73.5 us
    ppermute x1, waiting for transfers between devices: 0.01 us -> 21.3 us  [shards(): prev_m = lax.ppermute(own, 'x', ring(4, 1))]
    ppermute x1 -> x0, waiting for transfers between devices: 15 us -> none  [shards(): far_m = lax.ppermute(own[:, HALF:HALF + FAR], 'x', ring(4, 2))]
    all_to_all x2, starting transfers between devices: 9.86 us -> 15.3 us  [the longest x1 9.15 us: shards(): lax.all_to_all(loss, ('x', 'ylo', 'yhi'), split_axis=0, concat_axis=0, ti...]
    another operation x8 -> x4, local copies, waits for them, and re-layouts: 3.63 us -> 0.01 us  [shards(): jnp.stack(gains(dino_gain, DINO_Q))[:, None, :]]
    all_to_all x2, waiting for transfers between devices: 9.61 us -> 6.05 us  [gather_plane(): return lax.all_to_all(many, PLANE, split_axis=0, concat_axis=0, tiled=True)]
    ppermute x1 -> x0, starting transfers between devices: 3.44 us -> none  [shards(): far_m = lax.ppermute(own[:, HALF:HALF + FAR], 'x', ring(4, 2))]
    ppermute x5 -> x4, starting transfers between devices: 17.3 us -> 13.9 us  [swap(): return lax.ppermute(value, 'core', ring(2, 1))]
    all_to_all x2, starting transfers between devices: 23.9 us -> 27.2 us  [gather_plane(): return lax.all_to_all(many, PLANE, split_axis=0, concat_axis=0, tiled=True)]
  transfers between devices with their start and end apart: 15 -> 13, of which waited for: 4 -> 5; matrix products, arithmetic and copies ran while one was open for 16% -> 10% of each run, Pallas kernels for 9% -> 11%
where the time goes in v5:
time: 160 us; the launch traced here: 159 us
  starting transfers between devices  73.5 us (46%)
  waiting for transfers between devices  32.8 us (20%)
  Pallas kernels  24.8 us (16%)
  local copies, waits for them, and re-layouts  14.1 us (9%)
  other arithmetic  5.38 us (3%)
  matrix products  4.44 us (3%)
  between operations  3.87 us (2%)
    all_to_all x2, starting transfers between devices, gather_plane(): return lax.all_to_all(many, PLANE, split_axis=0, concat_axis=0, tiled=True)  27.2 us
    ppermute x1, waiting for transfers between devices, shards(): prev_m = lax.ppermute(own, 'x', ring(4, 1))  21.3 us
    ppermute x4, starting transfers between devices, swap(): return lax.ppermute(value, 'core', ring(2, 1))  13.9 us
    ppermute x3, starting transfers between devices, shards(): lax.ppermute(feat_for(s), 'x', ring(4, -s))  10.5 us
    all_to_all x1, starting transfers between devices, shards(): lax.all_to_all(loss, ('x', 'ylo', 'yhi'), split_axis=0, concat_axis=0, ti...  9.15 us
    pallas_call x1, Pallas kernels, shards(): pl.pallas_call(forward_kernel, out_shape=(jax.ShapeDtypeStruct((rows, SAM...  7.84 us
    pallas_call x1, Pallas kernels, shards(): pl.pallas_call(grad_kernel, out_shape=jax.ShapeDtypeStruct((rows, 2 * HAL...  7.64 us
    pallas_call x1, Pallas kernels, shards(): pl.pallas_call(hidden_kernel, out_shape=jax.ShapeDtypeStruct((4, rows, HA...  7.08 us
  transfers between devices with their start and end apart: 13, of which 5 were waited for; matrix products, arithmetic and copies ran while one was open for 10% of the time, Pallas kernels for 11%

profile of v5, /device:TPU:1, one launch (start us, length us, event | category | flops | bytes accessed | tf_op | source)
XLA Modules:
  0.0 159.0 jit_solution(17584535909518573586)
XLA Ops:
  0.6 0.0 copy-start
  0.8 0.7 constant_dynamic-slice_fusion
  1.5 1.5 fusion.45
  3.1 1.8 %broadcast_in_dim.31 = bf16[64,5,2,1024]{3,2,1,0:T(2,128)(2,1)} broadcast(bf16[5,2,1024]{2,1,0:T(2,128)(2,1)S(1)} %maximum_bitcast_fusion), dimensions={1,2,3} | broadcast | bytes 1331200 | tf_op jit(solution)/shard_map/broadcast_in_dim | solution.py:204
  4.9 17.3 %all-to-all-start = ((bf16[64,5,2,1024]{3,2,1,0:T(2,128)(2,1)}), bf16[64,5,2,1024]{3,2,1,0:T(2,128)(2,1)S(1)}, u32[]{:S(2)}, u32[]{:S(2)}) async-start(bf16[64,5,2,1024]{3,2,1,0:T(2,128)(2,1)} %broadcast_in_dim.31), calls=%async_computation | async-start | bytes 2621440 | tf_op jit(solution)/shard_map/all_to_all | solution.py:207
  22.1 0.0 copy-start.11
  22.1 0.0 copy-start.7
  22.3 0.1 reshape.57
  22.4 0.1 dynamic-slice_reduce_fusion
  22.6 0.1 concatenate.43
  22.7 0.0 copy-start.13
  22.7 2.0 %broadcast_in_dim.33 = bf16[64,5,2,1280]{3,2,1,0:T(2,128)(2,1)} broadcast(bf16[5,2,1280]{2,1,0:T(2,128)(2,1)S(1)} %bitcast.23), dimensions={1,2,3} | broadcast | bytes 1664000 | tf_op jit(solution)/shard_map/broadcast_in_dim | solution.py:204
  24.7 0.1 copy.33
  24.9 0.1 pad.12.clone
  25.0 0.1 maximum_maximum_fusion
  25.1 0.7 dynamic-slice_bitcast_fusion
  25.8 3.1 %collective-permute-start.2 = (bf16[128,512]{1,0:T(8,128)(2,1)S(1)}, bf16[128,512]{1,0:T(8,128)(2,1)S(1)}, u32[]{:S(2)}, u32[]{:S(2)}) collective-permute-start(bf16[128,512]{1,0:T(8,128)(2,1)S(1)} %get-tuple-element.62), channel_id=1, source_target_pairs={{0,128},{128,256},{256,384},{384,0},{1,129},{129,257},{257,385},{3... | collective-permute-start | bytes 393224 | tf_op jit(solution)/shard_map/ppermute | solution.py:220
  28.9 4.4 %collective-permute-start.1 = (bf16[128,512]{1,0:T(8,128)(2,1)S(1)}, bf16[128,512]{1,0:T(8,128)(2,1)S(1)}, u32[]{:S(2)}, u32[]{:S(2)}) collective-permute-start(bf16[128,512]{1,0:T(8,128)(2,1)S(1)} %get-tuple-element.63), channel_id=1, source_target_pairs={{0,256},{128,384},{256,0},{384,128},{1,257},{129,385},{257,1},{385... | collective-permute-start | bytes 393224 | tf_op jit(solution)/shard_map/ppermute | solution.py:220
  33.3 3.1 %collective-permute-start = (bf16[128,512]{1,0:T(8,128)(2,1)S(1)}, bf16[128,512]{1,0:T(8,128)(2,1)S(1)}, u32[]{:S(2)}, u32[]{:S(2)}) collective-permute-start(bf16[128,512]{1,0:T(8,128)(2,1)S(1)} %get-tuple-element.64), channel_id=1, source_target_pairs={{0,384},{128,0},{256,128},{384,256},{1,385},{129,1},{257,129},{385... | collective-permute-start | bytes 393224 | tf_op jit(solution)/shard_map/ppermute | solution.py:220
  36.4 0.1 fusion.66
  36.6 0.6 dynamic_slice.87
  37.2 0.1 fusion.67
  37.3 0.7 pad_maximum_fusion.1
  37.9 0.7 clamp_reduce_fusion
  38.6 1.3 fusion.52.live
  39.9 0.7 fusion.42.tok_m
  40.7 0.8 fusion.39.tok_o
  41.4 0.7 pad_add_fusion.where
  42.7 0.6 broadcast_in_dim.36.gain_d
  43.4 1.3 fusion.51.scale
  44.6 0.0 collective-permute-done.2.f3
  44.6 0.0 collective-permute-done.1.f2
  44.7 0.6 copy-done.8
  45.3 0.1 copy-done.9
  45.3 0.0 copy-done.10
  45.4 2.3 %target.1 = (bf16[128,256]{1,0:T(8,128)(2,1)}, bf16[4,128,384]{2,1,0:T(8,128)(2,1)}) custom-call(bf16[128,512]{1,0:T(8,128)(2,1)} %get-tuple-element.65.f0, bf16[128,512]{1,0:T(8,128)(2,1)} %copy-done.10, bf16[128,512]{1,0:T(8,128)(2,1)} %copy-done.9, bf16[128,512]{1,0:T(8,128)(2,1)} %copy-done.8, f32[1,256]{1,0:T(1,128)} %bitcast.24, ...), custom_call_target="tpu_custom_call" | custom-call | tf_op jit(solution)/shard_map/target/pallas_call | solution.py:237
  47.7 6.0 %all-to-all-done = bf16[64,5,2,1024]{3,2,1,0:T(2,128)(2,1)S(1)} async-done(((bf16[64,5,2,1024]{3,2,1,0:T(2,128)(2,1)}), bf16[64,5,2,1024]{3,2,1,0:T(2,128)(2,1)S(1)}, u32[]{:S(2)}, u32[]{:S(2)}) %all-to-all-start) | async-done | bytes 1310752 | tf_op jit(solution)/shard_map/all_to_all | solution.py:207
  53.7 0.5 reshape.56.m0
  54.2 9.9 %all-to-all-start.1 = ((bf16[64,5,2,1280]{3,2,1,0:T(2,128)(2,1)}), bf16[64,5,2,1280]{3,2,1,0:T(2,128)(2,1)}, u32[]{:S(2)}, u32[]{:S(2)}) async-start(bf16[64,5,2,1280]{3,2,1,0:T(2,128)(2,1)} %broadcast_in_dim.33), calls=%async_computation.1 | async-start | bytes 3276800 | tf_op jit(solution)/shard_map/all_to_all | solution.py:207
  64.2 3.1 %collective-permute-start.5 = (bf16[640,1024]{1,0:T(8,128)(2,1)S(1)}, bf16[640,1024]{1,0:T(8,128)(2,1)}, u32[]{:S(2)}, u32[]{:S(2)}) collective-permute-start(bf16[640,1024]{1,0:T(8,128)(2,1)S(1)} %reshape.56.m0), channel_id=1, source_target_pairs={{0,128},{128,256},{256,384},{384,0},{1,129},{129,257},{257,385},{3... | collective-permute-start | bytes 3932168 | tf_op jit(solution)/shard_map/ppermute | solution.py:256
  67.3 3.4 %collective-permute-start.4 = (bf16[640,1024]{1,0:T(8,128)(2,1)S(1)}, bf16[640,1024]{1,0:T(8,128)(2,1)}, u32[]{:S(2)}, u32[]{:S(2)}) collective-permute-start(bf16[640,1024]{1,0:T(8,128)(2,1)S(1)} %reshape.56.m0), channel_id=1, source_target_pairs={{0,384},{128,0},{256,128},{384,256},{1,385},{129,1},{257,129},{385... | collective-permute-start | bytes 3932168 | tf_op jit(solution)/shard_map/ppermute | solution.py:255
  70.7 4.1 %collective-permute-start.3 = (bf16[640,1024]{1,0:T(8,128)(2,1)S(1)}, bf16[640,1024]{1,0:T(8,128)(2,1)S(1)}, u32[]{:S(2)}, u32[]{:S(2)}) collective-permute-start(bf16[640,1024]{1,0:T(8,128)(2,1)S(1)} %reshape.56.m0), channel_id=1, source_target_pairs={{0,4},{4,0},{1,5},{5,1},{2,6},{6,2},{3,7},{7,3},{8,12},{12,8},{9,1... | collective-permute-start | bytes 3932168 | tf_op jit(solution)/shard_map/ppermute | solution.py:252
  74.8 21.3 %collective-permute-done.5.m3 = bf16[640,1024]{1,0:T(8,128)(2,1)} collective-permute-done((bf16[640,1024]{1,0:T(8,128)(2,1)S(1)}, bf16[640,1024]{1,0:T(8,128)(2,1)}, u32[]{:S(2)}, u32[]{:S(2)}) %collective-permute-start.5) | collective-permute-done | bytes 1310752 | tf_op jit(solution)/shard_map/ppermute | solution.py:256
  96.0 1.6 %collective-permute-done.4.m1 = bf16[640,1024]{1,0:T(8,128)(2,1)} collective-permute-done((bf16[640,1024]{1,0:T(8,128)(2,1)S(1)}, bf16[640,1024]{1,0:T(8,128)(2,1)}, u32[]{:S(2)}, u32[]{:S(2)}) %collective-permute-start.4) | collective-permute-done | bytes 1310752 | tf_op jit(solution)/shard_map/ppermute | solution.py:255
  97.7 4.7 %collective-permute-start.6 = (bf16[640,1024]{1,0:T(8,128)(2,1)}, bf16[640,1024]{1,0:T(8,128)(2,1)}, u32[]{:S(2)}, u32[]{:S(2)}) collective-permute-start(bf16[640,1024]{1,0:T(8,128)(2,1)} %collective-permute-done.4.m1), channel_id=1, source_target_pairs={{0,4},{4,0},{1,5},{5,1},{2,6},{6,2},{3,7},{7,3},{8,12},{12,8},{9,1... | collective-permute-start | bytes 3932168 | tf_op jit(solution)/shard_map/ppermute | solution.py:252
  102.4 1.9 %collective-permute-start.7 = (bf16[640,1024]{1,0:T(8,128)(2,1)}, bf16[640,1024]{1,0:T(8,128)(2,1)}, u32[]{:S(2)}, u32[]{:S(2)}) collective-permute-start(bf16[640,1024]{1,0:T(8,128)(2,1)} %collective-permute-done.5.m3), channel_id=1, source_target_pairs={{0,4},{4,0},{1,5},{5,1},{2,6},{6,2},{3,7},{7,3},{8,12},{12,8},{9,1... | collective-permute-start | bytes 3932168 | tf_op jit(solution)/shard_map/ppermute | solution.py:252
  104.3 0.3 fusion.49
  104.7 0.0 collective-permute-done.3.o0
  104.7 1.1 convolution_add_fusion.pre0
  105.8 0.0 all-to-all-done.1
  105.8 3.8 %reshape.58.m2 = bf16[640,1280]{1,0:T(8,128)(2,1)S(1)} reshape(bf16[64,5,2,1280]{3,2,1,0:T(2,128)(2,1)} %all-to-all-done.1) | data formatting | bytes 3276800 | tf_op jit(solution)/shard_map/reshape | solution.py:262
  109.7 0.0 collective-permute-done.6.o1
  109.7 0.0 collective-permute-done.7.o3
  109.7 3.2 %collective-permute-start.8 = (bf16[640,1280]{1,0:T(8,128)(2,1)S(1)}, bf16[640,1280]{1,0:T(8,128)(2,1)S(1)}, u32[]{:S(2)}, u32[]{:S(2)}) collective-permute-start(bf16[640,1280]{1,0:T(8,128)(2,1)S(1)} %reshape.58.m2), channel_id=1, source_target_pairs={{0,4},{4,0},{1,5},{5,1},{2,6},{6,2},{3,7},{7,3},{8,12},{12,8},{9,1... | collective-permute-start | bytes 4915208 | tf_op jit(solution)/shard_map/ppermute | solution.py:252
  112.9 2.9 %collective-permute-done.8.o2 = bf16[640,1280]{1,0:T(8,128)(2,1)S(1)} collective-permute-done((bf16[640,1280]{1,0:T(8,128)(2,1)S(1)}, bf16[640,1280]{1,0:T(8,128)(2,1)S(1)}, u32[]{:S(2)}, u32[]{:S(2)}) %collective-permute-start.8) | collective-permute-done | bytes 1638432 | tf_op jit(solution)/shard_map/ppermute | solution.py:252
  115.8 1.2 copy-done.4
  117.0 7.8 %forward.1 = (f32[128,256]{1,0:T(8,128)}, f32[4,128,384]{2,1,0:T(8,128)}, f32[4,128,640]{2,1,0:T(8,128)}, f32[128,4]{1,0:T(8,128)}, f32[16,1,128]{2,1,0:T(1,128)}) custom-call(s32[2]{0:T(128)} %pad_add_fusion.where, bf16[128,640]{1,0:T(8,128)(2,1)} %copy-done.5, bf16[128,640]{1,0:T(8,128)(2,1)} %copy-done.6, f32[128,640]{1,0:T(8,128)} %convolution_add_fusion.pre0, ...), custom_call_target="tpu_custom_call" | custom-call | tf_op jit(solution)/shard_map/forward/pallas_call | solution.py:269
  124.9 6.2 %all-to-all-start.2 = ((f32[16,1,128]{2,1,0:T(1,128)}), f32[16,1,128]{2,1,0:T(1,128)S(1)}, u32[]{:S(2)}, u32[]{:S(2)}) async-start(f32[16,1,128]{2,1,0:T(1,128)} %get-tuple-element.50), calls=%async_computation.2 | async-start | bytes 16384 | tf_op jit(solution)/shard_map/all_to_all | solution.py:291
  131.1 7.1 %hidden.1.hid = bf16[4,128,640]{2,1,0:T(8,128)(2,1)} custom-call(s32[2]{0:T(128)} %pad_add_fusion.where, f32[128,256]{1,0:T(8,128)} %get-tuple-element.51.pred_s, f32[4,128,384]{2,1,0:T(8,128)} %get-tuple-element.52.pred_d, bf16[128,256]{1,0:T(8,128)(2,1)} %get-tuple-element.41.goal_s, bf16[4,128,384]{2,1,0:T(8,128)(2,1)} %get-tuple-element.42.goal_d, ...), custom_call_target="tpu_custom_call" | custom-call | tf_op jit(solution)/shard_map/hidden/pallas_call | solution.py:292
  138.2 0.6 broadcast_in_dim.37
  138.8 9.2 %all-to-all-start.3 = ((f32[32,1,128]{2,1,0:T(1,128)}), f32[32,1,128]{2,1,0:T(1,128)S(1)}, u32[]{:S(2)}, u32[]{:S(2)}) async-start(f32[32,1,128]{2,1,0:T(1,128)} %broadcast_in_dim.37), calls=%async_computation.3 | async-start | bytes 32768 | tf_op jit(solution)/shard_map/all_to_all | solution.py:308
  148.0 7.6 %grad.1 = bf16[128,1280]{1,0:T(8,128)(2,1)} custom-call(s32[2]{0:T(128)} %pad_add_fusion.where, bf16[4,128,640]{2,1,0:T(8,128)(2,1)} %hidden.1.hid, bf16[640,1024]{1,0:T(8,128)(2,1)} %copy-done.1, bf16[640,1024]{1,0:T(8,128)(2,1)} %copy-done.3, bf16[640,1024]{1,0:T(8,128)(2,1)} %collective-permute-done.4.m1, bf16[640,1024]{1,0:T(8,128)(2,1)} %collective-permute-done.6.o1, ...), custom_call_target="tpu_custom_call" | custom-call | tf_op jit(solution)/shard_map/grad/pallas_call | solution.py:311
  155.6 0.9 all-to-all-done.3
  156.5 0.6 slice_reduce_fusion
  (47 shorter events, 0.3 us)
Async XLA Ops:
  0.6 39.3 %copy-start = (bf16[128,1280]{1,0:T(8,128)(2,1)S(1)}, bf16[128,1280]{1,0:T(8,128)(2,1)}, u32[]{:S(2)}) copy-start(bf16[128,1280]{1,0:T(8,128)(2,1)} %param.10) | copy-start | bytes 983044
  4.9 17.4 %copy-start.12 = (bf16[10,256]{1,0:T(8,128)(2,1)S(1)}, bf16[10,256]{1,0:T(8,128)(2,1)}, u32[]{:S(2)}) copy-start(bf16[10,256]{1,0:T(8,128)(2,1)} %param.17) | copy-start | bytes 15364
  4.9 48.9 %all-to-all-start = ((bf16[64,5,2,1024]{3,2,1,0:T(2,128)(2,1)}), bf16[64,5,2,1024]{3,2,1,0:T(2,128)(2,1)S(1)}, u32[]{:S(2)}, u32[]{:S(2)}) async-start(bf16[64,5,2,1024]{3,2,1,0:T(2,128)(2,1)} %broadcast_in_dim.31), calls=%async_computation | async-start | bytes 2621440 | tf_op jit(solution)/shard_map/all_to_all | solution.py:207
  22.1 2.6 %copy-start.11 = (bf16[4,128,64]{1,2,0:T(8,128)(2,1)S(1)}, bf16[4,128,64]{1,2,0:T(8,128)(2,1)}, u32[]{:S(2)}) copy-start(bf16[4,128,64]{1,2,0:T(8,128)(2,1)} %param.11) | copy-start | bytes 196612
  22.1 2.8 %copy-start.7 = (bf16[4,128,384]{2,1,0:T(8,128)(2,1)S(1)}, bf16[4,128,384]{2,1,0:T(8,128)(2,1)}, u32[]{:S(2)}) copy-start(bf16[4,128,384]{2,1,0:T(8,128)(2,1)} %param.12) | copy-start | bytes 1179652
  22.7 13.8 %copy-start.13 = (f32[1536]{0:T(1024)S(1)}, f32[1536]{0:T(1024)}, u32[]{:S(2)}) copy-start(f32[1536]{0:T(1024)} %param.14) | copy-start | bytes 18436
  24.7 11.9 %copy-start.15 = (s32[64]{0:T(128)S(1)}, s32[64]{0:T(128)}, u32[]{:S(2)}) copy-start(s32[64]{0:T(128)} %param.15) | copy-start | bytes 772
  24.7 12.5 %copy-start.14 = (f32[256]{0:T(256)S(1)}, f32[256]{0:T(256)}, u32[]{:S(2)}) copy-start(f32[256]{0:T(256)} %param.13) | copy-start | bytes 3076
  25.8 18.9 %collective-permute-start.2 = (bf16[128,512]{1,0:T(8,128)(2,1)S(1)}, bf16[128,512]{1,0:T(8,128)(2,1)S(1)}, u32[]{:S(2)}, u32[]{:S(2)}) collective-permute-start(bf16[128,512]{1,0:T(8,128)(2,1)S(1)} %get-tuple-element.62), channel_id=1, source_target_pairs={{0,128},{128,256},{256,384},{384,0},{1,129},{129,257},{257,385},{3... | collective-permute-start | bytes 393224 | tf_op jit(solution)/shard_map/ppermute | solution.py:220
  28.9 15.8 %collective-permute-start.1 = (bf16[128,512]{1,0:T(8,128)(2,1)S(1)}, bf16[128,512]{1,0:T(8,128)(2,1)S(1)}, u32[]{:S(2)}, u32[]{:S(2)}) collective-permute-start(bf16[128,512]{1,0:T(8,128)(2,1)S(1)} %get-tuple-element.63), channel_id=1, source_target_pairs={{0,256},{128,384},{256,0},{384,128},{1,257},{129,385},{257,1},{385... | collective-permute-start | bytes 393224 | tf_op jit(solution)/shard_map/ppermute | solution.py:220
  33.3 11.4 %collective-permute-start = (bf16[128,512]{1,0:T(8,128)(2,1)S(1)}, bf16[128,512]{1,0:T(8,128)(2,1)S(1)}, u32[]{:S(2)}, u32[]{:S(2)}) collective-permute-start(bf16[128,512]{1,0:T(8,128)(2,1)S(1)} %get-tuple-element.64), channel_id=1, source_target_pairs={{0,384},{128,0},{256,128},{384,256},{1,385},{129,1},{257,129},{385... | collective-permute-start | bytes 393224 | tf_op jit(solution)/shard_map/ppermute | solution.py:220
  40.7 63.7 %copy-start.5 = (bf16[128,640]{1,0:T(8,128)(2,1)}, bf16[128,640]{1,0:T(8,128)(2,1)S(1)}, u32[]{:S(2)}) copy-start(bf16[128,640]{1,0:T(8,128)(2,1)S(1)} %fusion.42.tok_m) | copy-start | bytes 491524
  41.4 63.2 %copy-start.6 = (bf16[128,640]{1,0:T(8,128)(2,1)}, bf16[128,640]{1,0:T(8,128)(2,1)S(1)}, u32[]{:S(2)}) copy-start(bf16[128,640]{1,0:T(8,128)(2,1)S(1)} %fusion.39.tok_o) | copy-start | bytes 491524
  44.6 0.6 copy-start.8
  44.7 0.7 copy-start.9
  44.7 0.7 copy-start.10
  54.2 50.1 %copy-start.1 = (bf16[640,1024]{1,0:T(8,128)(2,1)}, bf16[640,1024]{1,0:T(8,128)(2,1)S(1)}, u32[]{:S(2)}) copy-start(bf16[640,1024]{1,0:T(8,128)(2,1)S(1)} %reshape.56.m0) | copy-start | bytes 3932164
  54.2 51.6 %all-to-all-start.1 = ((bf16[64,5,2,1280]{3,2,1,0:T(2,128)(2,1)}), bf16[64,5,2,1280]{3,2,1,0:T(2,128)(2,1)}, u32[]{:S(2)}, u32[]{:S(2)}) async-start(bf16[64,5,2,1280]{3,2,1,0:T(2,128)(2,1)} %broadcast_in_dim.33), calls=%async_computation.1 | async-start | bytes 3276800 | tf_op jit(solution)/shard_map/all_to_all | solution.py:207
  64.2 31.9 %collective-permute-start.5 = (bf16[640,1024]{1,0:T(8,128)(2,1)S(1)}, bf16[640,1024]{1,0:T(8,128)(2,1)}, u32[]{:S(2)}, u32[]{:S(2)}) collective-permute-start(bf16[640,1024]{1,0:T(8,128)(2,1)S(1)} %reshape.56.m0), channel_id=1, source_target_pairs={{0,128},{128,256},{256,384},{384,0},{1,129},{129,257},{257,385},{3... | collective-permute-start | bytes 3932168 | tf_op jit(solution)/shard_map/ppermute | solution.py:256
  67.3 30.4 %collective-permute-start.4 = (bf16[640,1024]{1,0:T(8,128)(2,1)S(1)}, bf16[640,1024]{1,0:T(8,128)(2,1)}, u32[]{:S(2)}, u32[]{:S(2)}) collective-permute-start(bf16[640,1024]{1,0:T(8,128)(2,1)S(1)} %reshape.56.m0), channel_id=1, source_target_pairs={{0,384},{128,0},{256,128},{384,256},{1,385},{129,1},{257,129},{385... | collective-permute-start | bytes 3932168 | tf_op jit(solution)/shard_map/ppermute | solution.py:255
  70.7 34.0 %collective-permute-start.3 = (bf16[640,1024]{1,0:T(8,128)(2,1)S(1)}, bf16[640,1024]{1,0:T(8,128)(2,1)S(1)}, u32[]{:S(2)}, u32[]{:S(2)}) collective-permute-start(bf16[640,1024]{1,0:T(8,128)(2,1)S(1)} %reshape.56.m0), channel_id=1, source_target_pairs={{0,4},{4,0},{1,5},{5,1},{2,6},{6,2},{3,7},{7,3},{8,12},{12,8},{9,1... | collective-permute-start | bytes 3932168 | tf_op jit(solution)/shard_map/ppermute | solution.py:252
  97.7 12.0 %collective-permute-start.6 = (bf16[640,1024]{1,0:T(8,128)(2,1)}, bf16[640,1024]{1,0:T(8,128)(2,1)}, u32[]{:S(2)}, u32[]{:S(2)}) collective-permute-start(bf16[640,1024]{1,0:T(8,128)(2,1)} %collective-permute-done.4.m1), channel_id=1, source_target_pairs={{0,4},{4,0},{1,5},{5,1},{2,6},{6,2},{3,7},{7,3},{8,12},{12,8},{9,1... | collective-permute-start | bytes 3932168 | tf_op jit(solution)/shard_map/ppermute | solution.py:252
  102.4 7.3 %collective-permute-start.7 = (bf16[640,1024]{1,0:T(8,128)(2,1)}, bf16[640,1024]{1,0:T(8,128)(2,1)}, u32[]{:S(2)}, u32[]{:S(2)}) collective-permute-start(bf16[640,1024]{1,0:T(8,128)(2,1)} %collective-permute-done.5.m3), channel_id=1, source_target_pairs={{0,4},{4,0},{1,5},{5,1},{2,6},{6,2},{3,7},{7,3},{8,12},{12,8},{9,1... | collective-permute-start | bytes 3932168 | tf_op jit(solution)/shard_map/ppermute | solution.py:252
  104.7 5.0 %copy-start.3 = (bf16[640,1024]{1,0:T(8,128)(2,1)}, bf16[640,1024]{1,0:T(8,128)(2,1)S(1)}, u32[]{:S(2)}) copy-start(bf16[640,1024]{1,0:T(8,128)(2,1)S(1)} %collective-permute-done.3.o0) | copy-start | bytes 3932164
  109.7 6.2 %copy-start.2 = (bf16[640,1280]{1,0:T(8,128)(2,1)}, bf16[640,1280]{1,0:T(8,128)(2,1)S(1)}, u32[]{:S(2)}) copy-start(bf16[640,1280]{1,0:T(8,128)(2,1)S(1)} %reshape.58.m2) | copy-start | bytes 4915204
  109.7 6.1 %collective-permute-start.8 = (bf16[640,1280]{1,0:T(8,128)(2,1)S(1)}, bf16[640,1280]{1,0:T(8,128)(2,1)S(1)}, u32[]{:S(2)}, u32[]{:S(2)}) collective-permute-start(bf16[640,1280]{1,0:T(8,128)(2,1)S(1)} %reshape.58.m2), channel_id=1, source_target_pairs={{0,4},{4,0},{1,5},{5,1},{2,6},{6,2},{3,7},{7,3},{8,12},{12,8},{9,1... | collective-permute-start | bytes 4915208 | tf_op jit(solution)/shard_map/ppermute | solution.py:252
  115.8 1.2 copy-start.4
  124.9 13.3 %all-to-all-start.2 = ((f32[16,1,128]{2,1,0:T(1,128)}), f32[16,1,128]{2,1,0:T(1,128)S(1)}, u32[]{:S(2)}, u32[]{:S(2)}) async-start(f32[16,1,128]{2,1,0:T(1,128)} %get-tuple-element.50), calls=%async_computation.2 | async-start | bytes 16384 | tf_op jit(solution)/shard_map/all_to_all | solution.py:291
  138.8 17.7 %all-to-all-start.3 = ((f32[32,1,128]{2,1,0:T(1,128)}), f32[32,1,128]{2,1,0:T(1,128)S(1)}, u32[]{:S(2)}, u32[]{:S(2)}) async-start(f32[32,1,128]{2,1,0:T(1,128)} %broadcast_in_dim.37), calls=%async_computation.3 | async-start | bytes 32768 | tf_op jit(solution)/shard_map/all_to_all | solution.py:308

commit v6 on v5

--- a/solution.py
+++ b/solution.py
@@ -16,6 +16,7 @@
 SAM = 256
 FEAT_Q = 512
 COLS = HALF + DINO_Q
+DINO = 4 * DINO_Q
 F32 = jnp.float32
 BF16 = jnp.bfloat16
 VMEM_LIMIT = 56 * 1024 * 1024
@@ -50,6 +51,28 @@
         pltpu.make_async_copy(ref.at[:, pl.ds(lo, hi - lo)], buf.at[i], sems.at[first + i])
         for i, ref in enumerate(refs)
     ]
+
+
+def side_by_side(mine, other, lo, hi, buf, sems, first=0):
+    width = hi - lo
+    return [
+        pltpu.make_async_copy(
+            ref.at[:, pl.ds(lo, width)],
+            buf.at[side, :, pl.ds(j * width, width)],
+            sems.at[first + 4 * side + j],
+        )
+        for side, refs in enumerate((mine, other))
+        for j, ref in enumerate(refs)
+    ]
+
+
+def dots(product, left, got, right):
+    out = []
+    for side in range(2):
+        for copy in got[4 * side:4 * side + 4]:
+            copy.wait()
+        out.append(product(left[side], right[side]))
+    return out
 
 
 def target_kernel(f0, f1, f2, f3, gain_s, gain_d, goal_s, goal_d):
@@ -64,7 +87,8 @@
 
     cut, center, root = center_of(0, DINO_Q)
     for j, part in enumerate(cut):
-        goal_d[j] = ((part - center) * root * gain_d[j]).astype(BF16)
+        at = slice(j * DINO_Q, (j + 1) * DINO_Q)
+        goal_d[:, at] = ((part - center) * root * gain_d[:, at]).astype(BF16)
     cut, center, root = center_of(DINO_Q, DINO_Q + SAM_Q)
     for j, part in enumerate(cut):
         at = slice(j * SAM_Q, (j + 1) * SAM_Q)
@@ -78,7 +102,7 @@
 ):
     x, core = where[0], where[1]
     got_in = copies((m1, o1, m3, o3, m2, o2), 0, HALF, w_in, sems)
-    got_out = copies((m0, o0, m1, o1, m3, o3, m2, o2), HALF, COLS, w_out, sems, 6)
+    got_out = side_by_side((m0, m1, m2, m3), (o0, o1, o2, o3), HALF, COLS, w_out, sems, 6)
     got_sam = copies((m2, o2), COLS, COLS + SAM, w_sam, sems, 14)
     for copy in got_in + got_out + got_sam:
         copy.start()
@@ -96,20 +120,15 @@
     def sums(value, aim):
         return [jnp.sum(v, axis=1, keepdims=True) for v in (value * value, aim * aim, value * aim)]
 
-    found = [0.0, 0.0, 0.0]
-    dm, do = act[2 + core], act[3 - core]
-    for i, j in enumerate((0, 1, 3, 2)):
-        got_out[2 * i].wait()
-        got_out[2 * i + 1].wait()
-        value = dot(dm, w_out[2 * i]) + dot(do, w_out[2 * i + 1])
-        pred_d[j] = value
-        found = [a + b for a, b in zip(found, sums(value, goal_d[j].astype(F32)))]
+    value = sum(dots(dot, (act[2 + core], act[3 - core]), got_out, w_out))
+    pred_d[...] = value
+    found = sums(value, goal_d[...].astype(F32))
     for copy in got_sam:
         copy.wait()
     value = dot(act[core], w_sam[0]) + dot(act[1 - core], w_sam[1])
     pred_s[...] = value
     total = 0.0
-    heads = ((SAM, sums(value, goal_s[...].astype(F32))), (4 * DINO_Q, found))
+    heads = ((SAM, sums(value, goal_s[...].astype(F32))), (DINO, found))
     for head, (chans, (pp, tt, pt)) in enumerate(heads):
         mean = pp / chans + 1e-05
         inv_root = lax.rsqrt(mean * (tt / chans + 1e-05))
@@ -128,7 +147,7 @@
 ):
     core = where[1]
     got_sam = copies((m2, o2), COLS, COLS + SAM, w_sam, sems)
-    got_out = copies((m0, o0, m1, o1, m2, o2, m3, o3), HALF, COLS, w_out, sems, 2)
+    got_out = side_by_side((m0, m1, m2, m3), (o0, o1, o2, o3), HALF, COLS, w_out, sems, 2)
     for copy in got_sam + got_out:
         copy.start()
 
@@ -146,26 +165,18 @@
     for copy in got_sam:
         copy.wait()
     finish(0, [dot_t(value, w_sam[side]) for side in range(2)])
-    found = [0.0, 0.0]
-    for j in range(4):
-        value = back(1, pred_d[j], goal_d[j], 4 * DINO_Q)
-        for side in range(2):
-            got_out[2 * j + side].wait()
-            found[side] += dot_t(value, w_out[2 * j + side])
-    finish(1, found)
-
-
-def grad_kernel(where, hid, m0, o0, m1, o1, m2, o2, m3, o3, grad, w_in, sems):
+    value = back(1, pred_d[...], goal_d[...], DINO)
+    finish(1, dots(dot_t, (value, value), got_out, w_out))
+
+
+def grad_kernel(where, hid, m0, o0, m1, o1, m2, o2, m3, o3, grad, slots, w_in, sems):
     x, core = where[0], where[1]
-    got = copies((m0, o0, m1, o1, m2, o2, m3, o3), 0, HALF, w_in, sems)
+    got = side_by_side((m0, m1, m2, m3), (o0, o1, o2, o3), 0, HALF, w_in, sems)
     for copy in got:
         copy.start()
-    total = [0.0, 0.0]
     for j in range(4):
-        h = hid[lax.rem(x + j, 4)]
-        for side in range(2):
-            got[2 * j + side].wait()
-            total[side] += dot_t(h, w_in[2 * j + side])
+        slots[:, j * HALF:(j + 1) * HALF] = hid[lax.rem(x + j, 4)]
+    total = dots(dot_t, (slots[...], slots[...]), got, w_in)
     at = lax.broadcasted_iota(jnp.int32, (1, HALF), 1)
     block = (at * 1639) >> 16
     row = lax.broadcasted_iota(jnp.int32, (2 * HALF, HALF), 0)
@@ -174,6 +185,24 @@
         source = at + block * 40 + half * 40
         whole += dot_t(total[side].astype(BF16), (row == source).astype(BF16))
     grad[...] = whole.astype(BF16)
+
+
+def rows_kernel(pairs, rows):
+    rows[...] = pairs[...].reshape(rows.shape)
+
+
+def full_rows(got):
+    pairs = got.reshape(HALF // 2, 2, got.shape[3])
+    cols = got.shape[3]
+    return pl.pallas_call(
+        rows_kernel,
+        out_shape=jax.ShapeDtypeStruct((HALF, cols), BF16),
+        grid=(2,),
+        in_specs=[pl.BlockSpec((HALF // 4, 2, cols), lambda i: (i, 0, 0))],
+        out_specs=pl.BlockSpec((HALF // 2, cols), lambda i: (i, 0)),
+        compiler_params=pltpu.CompilerParams(vmem_limit_bytes=VMEM_LIMIT),
+        name="rows",
+    )(pairs)
 
 
 def shards(
@@ -238,12 +267,12 @@
         target_kernel,
         out_shape=(
             jax.ShapeDtypeStruct((rows, SAM), BF16),
-            jax.ShapeDtypeStruct((4, rows, DINO_Q), BF16),
+            jax.ShapeDtypeStruct((rows, DINO), BF16),
         ),
         in_specs=[in_vmem] * 6,
         out_specs=(in_vmem,) * 2,
         name="target",
-    )(*got, jnp.concatenate(gains(sam_gain, SAM_Q))[None, :], jnp.stack(gains(dino_gain, DINO_Q))[:, None, :])
+    )(*got, jnp.concatenate(gains(sam_gain, SAM_Q))[None, :], jnp.concatenate(gains(dino_gain, DINO_Q))[None, :])
     own, opp_b, goal_s, goal_d, tok_m, tok_o, live, scale, place = lax.optimization_barrier(
         (own_g.reshape(HALF, COLS), opp_b, goal_s, goal_d, tok_m, tok_o, live, scale, place))
     opp_g = gather_plane(opp_b)
@@ -259,7 +288,7 @@
     next_m, prev_m = lax.optimization_barrier((next_m, prev_m))
     next_o, prev_o = swap(next_m), swap(prev_m)
     opp_g, pre0 = lax.optimization_barrier((opp_g, pre0))
-    opp = opp_g.reshape(HALF, COLS + SAM)
+    opp = full_rows(opp_g)
     opp, next_o, prev_o = lax.optimization_barrier((opp, next_o, prev_o))
     slots = [(own, own_o), (next_m, next_o), (opp, swap(opp)), (prev_m, prev_o)]
     flat = [w for pair in slots for w in pair]
@@ -270,7 +299,7 @@
         forward_kernel,
         out_shape=(
             jax.ShapeDtypeStruct((rows, SAM), F32),
-            jax.ShapeDtypeStruct((4, rows, DINO_Q), F32),
+            jax.ShapeDtypeStruct((rows, DINO), F32),
             jax.ShapeDtypeStruct((4, rows, HALF), F32),
             jax.ShapeDtypeStruct((rows, 4), F32),
             jax.ShapeDtypeStruct((16, 1, 128), F32),
@@ -280,7 +309,7 @@
         scratch_shapes=[
             pltpu.VMEM((4, rows, HALF), BF16),
             pltpu.VMEM((6, HALF, HALF), BF16),
-            pltpu.VMEM((8, HALF, DINO_Q), BF16),
+            pltpu.VMEM((2, HALF, DINO), BF16),
             pltpu.VMEM((2, HALF, SAM), BF16),
             pltpu.SemaphoreType.DMA((16,)),
         ],
@@ -295,7 +324,7 @@
         in_specs=[in_smem] + [in_vmem] * 7 + [anywhere] * 8,
         out_specs=in_vmem,
         scratch_shapes=[
-            pltpu.VMEM((8, HALF, DINO_Q), BF16),
+            pltpu.VMEM((2, HALF, DINO), BF16),
             pltpu.VMEM((2, HALF, SAM), BF16),
             pltpu.SemaphoreType.DMA((10,)),
         ],
@@ -313,7 +342,11 @@
         out_shape=jax.ShapeDtypeStruct((rows, 2 * HALF), BF16),
         in_specs=[in_smem, in_vmem] + [anywhere] * 8,
         out_specs=in_vmem,
-        scratch_shapes=[pltpu.VMEM((8, HALF, HALF), BF16), pltpu.SemaphoreType.DMA((8,))],
+        scratch_shapes=[
+            pltpu.VMEM((rows, 4 * HALF), BF16),
+            pltpu.VMEM((2, HALF, 4 * HALF), BF16),
+            pltpu.SemaphoreType.DMA((8,)),
+        ],
         compiler_params=params,
         name="grad",
     )(place, hid, *flat)

time: 160 us -> 158 us (0.988)
  local copies, waits for them, and re-layouts: 14.1 us -> 10.4 us
    reshape x1 -> x0, local copies, waits for them, and re-layouts: 3.8 us -> none  [shards(): opp = opp_g.reshape(HALF, COLS + SAM)]
    pallas_call x0 -> x1, Pallas kernels: none -> 2.45 us  [full_rows(): pl.pallas_call(rows_kernel, out_shape=jax.ShapeDtypeStruct((HALF, cols),...]
  transfers between devices with their start and end apart: 13 -> 13, of which waited for: 5 -> 6; matrix products, arithmetic and copies ran while one was open for 10% -> 8% of each run, Pallas kernels for 11% -> 12%
where the time goes in v6:
time: 158 us; the launch traced here: 157 us
  starting transfers between devices  73.5 us (47%)
  waiting for transfers between devices  34 us (22%)
  Pallas kernels  25.9 us (16%)
  local copies, waits for them, and re-layouts  10.4 us (7%)
  other arithmetic  5.44 us (3%)
  matrix products  4.44 us (3%)
  between operations  3.78 us (2%)
    all_to_all x2, starting transfers between devices, gather_plane(): return lax.all_to_all(many, PLANE, split_axis=0, concat_axis=0, tiled=True)  27.2 us
    ppermute x1, waiting for transfers between devices, shards(): prev_m = lax.ppermute(own, 'x', ring(4, 1))  21.3 us
    ppermute x4, starting transfers between devices, swap(): return lax.ppermute(value, 'core', ring(2, 1))  13.7 us
    ppermute x3, starting transfers between devices, shards(): lax.ppermute(feat_for(s), 'x', ring(4, -s))  10.5 us
    all_to_all x1, starting transfers between devices, shards(): lax.all_to_all(loss, ('x', 'ylo', 'yhi'), split_axis=0, concat_axis=0, ti...  9.15 us
    pallas_call x1, Pallas kernels, shards(): pl.pallas_call(forward_kernel, out_shape=(jax.ShapeDtypeStruct((rows, SAM...  7.36 us
    pallas_call x1, Pallas kernels, shards(): pl.pallas_call(grad_kernel, out_shape=jax.ShapeDtypeStruct((rows, 2 * HAL...  7.25 us
    pallas_call x1, Pallas kernels, shards(): pl.pallas_call(hidden_kernel, out_shape=jax.ShapeDtypeStruct((4, rows, HA...  6.58 us
  transfers between devices with their start and end apart: 13, of which 6 were waited for; matrix products, arithmetic and copies ran while one was open for 8% of the time, Pallas kernels for 12%

profile of v6, /device:TPU:1, one launch (start us, length us, event | category | flops | bytes accessed | tf_op | source)
XLA Modules:
  0.0 157.4 jit_solution(15652540174253048713)
XLA Ops:
  0.6 0.0 copy-start
  0.8 0.7 constant_dynamic-slice_fusion
  1.5 1.5 fusion.45
  3.1 1.8 %broadcast_in_dim.31 = bf16[64,5,2,1024]{3,2,1,0:T(2,128)(2,1)} broadcast(bf16[5,2,1024]{2,1,0:T(2,128)(2,1)S(1)} %maximum_bitcast_fusion), dimensions={1,2,3} | broadcast | bytes 1331200 | tf_op jit(solution)/shard_map/broadcast_in_dim | solution.py:233
  4.9 17.3 %all-to-all-start = ((bf16[64,5,2,1024]{3,2,1,0:T(2,128)(2,1)}), bf16[64,5,2,1024]{3,2,1,0:T(2,128)(2,1)S(1)}, u32[]{:S(2)}, u32[]{:S(2)}) async-start(bf16[64,5,2,1024]{3,2,1,0:T(2,128)(2,1)} %broadcast_in_dim.31), calls=%async_computation | async-start | bytes 2621440 | tf_op jit(solution)/shard_map/all_to_all | solution.py:236
  22.1 0.0 copy-start.10
  22.1 0.0 copy-start.6
  22.3 0.1 reshape.57
  22.4 0.1 dynamic-slice_reduce_fusion
  22.6 0.1 concatenate.46
  22.7 2.0 %broadcast_in_dim.33 = bf16[64,5,2,1280]{3,2,1,0:T(2,128)(2,1)} broadcast(bf16[5,2,1280]{2,1,0:T(2,128)(2,1)S(1)} %bitcast.24), dimensions={1,2,3} | broadcast | bytes 1664000 | tf_op jit(solution)/shard_map/broadcast_in_dim | solution.py:233
  24.7 0.1 copy.33
  24.9 0.1 pad.12.clone
  25.0 0.1 maximum_maximum_fusion
  25.1 0.7 dynamic-slice_bitcast_fusion
  25.8 3.1 %collective-permute-start.2 = (bf16[128,512]{1,0:T(8,128)(2,1)S(1)}, bf16[128,512]{1,0:T(8,128)(2,1)S(1)}, u32[]{:S(2)}, u32[]{:S(2)}) collective-permute-start(bf16[128,512]{1,0:T(8,128)(2,1)S(1)} %get-tuple-element.62), channel_id=1, source_target_pairs={{0,128},{128,256},{256,384},{384,0},{1,129},{129,257},{257,385},{3... | collective-permute-start | bytes 393224 | tf_op jit(solution)/shard_map/ppermute | solution.py:249
  28.9 4.4 %collective-permute-start.1 = (bf16[128,512]{1,0:T(8,128)(2,1)S(1)}, bf16[128,512]{1,0:T(8,128)(2,1)S(1)}, u32[]{:S(2)}, u32[]{:S(2)}) collective-permute-start(bf16[128,512]{1,0:T(8,128)(2,1)S(1)} %get-tuple-element.63), channel_id=1, source_target_pairs={{0,256},{128,384},{256,0},{384,128},{1,257},{129,385},{257,1},{385... | collective-permute-start | bytes 393224 | tf_op jit(solution)/shard_map/ppermute | solution.py:249
  33.3 3.1 %collective-permute-start = (bf16[128,512]{1,0:T(8,128)(2,1)S(1)}, bf16[128,512]{1,0:T(8,128)(2,1)S(1)}, u32[]{:S(2)}, u32[]{:S(2)}) collective-permute-start(bf16[128,512]{1,0:T(8,128)(2,1)S(1)} %get-tuple-element.64), channel_id=1, source_target_pairs={{0,384},{128,0},{256,128},{384,256},{1,385},{129,1},{257,129},{385... | collective-permute-start | bytes 393224 | tf_op jit(solution)/shard_map/ppermute | solution.py:249
  36.4 0.7 dynamic_slice.87
  37.1 0.1 fusion.67
  37.2 0.7 pad_maximum_fusion.1
  37.8 0.7 clamp_reduce_fusion
  38.5 0.1 fusion.66
  38.6 1.3 fusion.52.live
  39.9 0.8 fusion.42.tok_m
  40.7 0.8 fusion.39.tok_o
  41.5 0.6 pad_add_fusion.where
  42.8 0.6 broadcast_in_dim.36.gain_d
  43.4 1.3 fusion.51.scale
  44.7 0.0 collective-permute-done.2.f3
  44.7 0.0 collective-permute-done.1.f2
  44.8 0.0 collective-permute-done.f1
  44.8 0.6 copy-done.7
  45.4 0.0 copy-done.8
  45.4 0.1 copy-done.9
  45.5 2.3 %target.1 = (bf16[128,256]{1,0:T(8,128)(2,1)}, bf16[128,1536]{1,0:T(8,128)(2,1)}) custom-call(bf16[128,512]{1,0:T(8,128)(2,1)} %get-tuple-element.65.f0, bf16[128,512]{1,0:T(8,128)(2,1)} %copy-done.9, bf16[128,512]{1,0:T(8,128)(2,1)} %copy-done.8, bf16[128,512]{1,0:T(8,128)(2,1)} %copy-done.7, f32[1,256]{1,0:T(1,128)} %bitcast.25, ...), custom_call_target="tpu_custom_call" | custom-call | tf_op jit(solution)/shard_map/target/pallas_call | solution.py:266
  47.8 5.9 %all-to-all-done = bf16[64,5,2,1024]{3,2,1,0:T(2,128)(2,1)S(1)} async-done(((bf16[64,5,2,1024]{3,2,1,0:T(2,128)(2,1)}), bf16[64,5,2,1024]{3,2,1,0:T(2,128)(2,1)S(1)}, u32[]{:S(2)}, u32[]{:S(2)}) %all-to-all-start) | async-done | bytes 1310752 | tf_op jit(solution)/shard_map/all_to_all | solution.py:236
  53.7 0.5 reshape.56.m0
  54.2 9.9 %all-to-all-start.1 = ((bf16[64,5,2,1280]{3,2,1,0:T(2,128)(2,1)}), bf16[64,5,2,1280]{3,2,1,0:T(2,128)(2,1)}, u32[]{:S(2)}, u32[]{:S(2)}) async-start(bf16[64,5,2,1280]{3,2,1,0:T(2,128)(2,1)} %broadcast_in_dim.33), calls=%async_computation.1 | async-start | bytes 3276800 | tf_op jit(solution)/shard_map/all_to_all | solution.py:236
  64.2 3.1 %collective-permute-start.5 = (bf16[640,1024]{1,0:T(8,128)(2,1)S(1)}, bf16[640,1024]{1,0:T(8,128)(2,1)}, u32[]{:S(2)}, u32[]{:S(2)}) collective-permute-start(bf16[640,1024]{1,0:T(8,128)(2,1)S(1)} %reshape.56.m0), channel_id=1, source_target_pairs={{0,128},{128,256},{256,384},{384,0},{1,129},{129,257},{257,385},{3... | collective-permute-start | bytes 3932168 | tf_op jit(solution)/shard_map/ppermute | solution.py:285
  67.3 3.4 %collective-permute-start.4 = (bf16[640,1024]{1,0:T(8,128)(2,1)S(1)}, bf16[640,1024]{1,0:T(8,128)(2,1)}, u32[]{:S(2)}, u32[]{:S(2)}) collective-permute-start(bf16[640,1024]{1,0:T(8,128)(2,1)S(1)} %reshape.56.m0), channel_id=1, source_target_pairs={{0,384},{128,0},{256,128},{384,256},{1,385},{129,1},{257,129},{385... | collective-permute-start | bytes 3932168 | tf_op jit(solution)/shard_map/ppermute | solution.py:284
  70.7 4.1 %collective-permute-start.3 = (bf16[640,1024]{1,0:T(8,128)(2,1)S(1)}, bf16[640,1024]{1,0:T(8,128)(2,1)S(1)}, u32[]{:S(2)}, u32[]{:S(2)}) collective-permute-start(bf16[640,1024]{1,0:T(8,128)(2,1)S(1)} %reshape.56.m0), channel_id=1, source_target_pairs={{0,4},{4,0},{1,5},{5,1},{2,6},{6,2},{3,7},{7,3},{8,12},{12,8},{9,1... | collective-permute-start | bytes 3932168 | tf_op jit(solution)/shard_map/ppermute | solution.py:281
  74.8 21.3 %collective-permute-done.5.m3 = bf16[640,1024]{1,0:T(8,128)(2,1)} collective-permute-done((bf16[640,1024]{1,0:T(8,128)(2,1)S(1)}, bf16[640,1024]{1,0:T(8,128)(2,1)}, u32[]{:S(2)}, u32[]{:S(2)}) %collective-permute-start.5) | collective-permute-done | bytes 1310752 | tf_op jit(solution)/shard_map/ppermute | solution.py:285
  96.0 1.6 %collective-permute-done.4.m1 = bf16[640,1024]{1,0:T(8,128)(2,1)} collective-permute-done((bf16[640,1024]{1,0:T(8,128)(2,1)S(1)}, bf16[640,1024]{1,0:T(8,128)(2,1)}, u32[]{:S(2)}, u32[]{:S(2)}) %collective-permute-start.4) | collective-permute-done | bytes 1310752 | tf_op jit(solution)/shard_map/ppermute | solution.py:284
  97.7 4.7 %collective-permute-start.6 = (bf16[640,1024]{1,0:T(8,128)(2,1)}, bf16[640,1024]{1,0:T(8,128)(2,1)}, u32[]{:S(2)}, u32[]{:S(2)}) collective-permute-start(bf16[640,1024]{1,0:T(8,128)(2,1)} %collective-permute-done.4.m1), channel_id=1, source_target_pairs={{0,4},{4,0},{1,5},{5,1},{2,6},{6,2},{3,7},{7,3},{8,12},{12,8},{9,1... | collective-permute-start | bytes 3932168 | tf_op jit(solution)/shard_map/ppermute | solution.py:281
  102.4 1.9 %collective-permute-start.7 = (bf16[640,1024]{1,0:T(8,128)(2,1)}, bf16[640,1024]{1,0:T(8,128)(2,1)}, u32[]{:S(2)}, u32[]{:S(2)}) collective-permute-start(bf16[640,1024]{1,0:T(8,128)(2,1)} %collective-permute-done.5.m3), channel_id=1, source_target_pairs={{0,4},{4,0},{1,5},{5,1},{2,6},{6,2},{3,7},{7,3},{8,12},{12,8},{9,1... | collective-permute-start | bytes 3932168 | tf_op jit(solution)/shard_map/ppermute | solution.py:281
  104.3 0.3 fusion.49
  104.7 0.0 collective-permute-done.3.o0
  104.7 1.1 convolution_add_fusion.pre0
  105.8 0.0 all-to-all-done.1
  105.8 2.5 %rows.1.m2 = bf16[640,1280]{1,0:T(8,128)(2,1)} custom-call(bf16[320,2,1280]{2,1,0:T(2,128)(2,1)} %bitcast.12.pairs), custom_call_target="tpu_custom_call" | custom-call | tf_op jit(solution)/shard_map/rows/pallas_call | solution.py:197
  108.3 0.0 collective-permute-done.7.o3
  108.3 3.0 %collective-permute-start.8 = (bf16[640,1280]{1,0:T(8,128)(2,1)}, bf16[640,1280]{1,0:T(8,128)(2,1)S(1)}, u32[]{:S(2)}, u32[]{:S(2)}) collective-permute-start(bf16[640,1280]{1,0:T(8,128)(2,1)} %rows.1.m2), channel_id=1, source_target_pairs={{0,4},{4,0},{1,5},{5,1},{2,6},{6,2},{3,7},{7,3},{8,12},{12,8},{9,1... | collective-permute-start | bytes 4915208 | tf_op jit(solution)/shard_map/ppermute | solution.py:281
  111.3 3.3 %collective-permute-done.8.o2 = bf16[640,1280]{1,0:T(8,128)(2,1)S(1)} collective-permute-done((bf16[640,1280]{1,0:T(8,128)(2,1)}, bf16[640,1280]{1,0:T(8,128)(2,1)S(1)}, u32[]{:S(2)}, u32[]{:S(2)}) %collective-permute-start.8) | collective-permute-done | bytes 1638432 | tf_op jit(solution)/shard_map/ppermute | solution.py:281
  114.7 1.2 copy-done.3
  115.8 7.4 %forward.1 = (f32[128,256]{1,0:T(8,128)}, f32[128,1536]{1,0:T(8,128)}, f32[4,128,640]{2,1,0:T(8,128)}, f32[128,4]{1,0:T(8,128)}, f32[16,1,128]{2,1,0:T(1,128)}) custom-call(s32[2]{0:T(128)} %pad_add_fusion.where, bf16[128,640]{1,0:T(8,128)(2,1)} %copy-done.4, bf16[128,640]{1,0:T(8,128)(2,1)} %copy-done.5, f32[128,640]{1,0:T(8,128)} %convolution_add_fusion.pre0, ...), custom_call_target="tpu_custom_call" | custom-call | tf_op jit(solution)/shard_map/forward/pallas_call | solution.py:298
  123.2 6.4 %all-to-all-start.2 = ((f32[16,1,128]{2,1,0:T(1,128)}), f32[16,1,128]{2,1,0:T(1,128)S(1)}, u32[]{:S(2)}, u32[]{:S(2)}) async-start(f32[16,1,128]{2,1,0:T(1,128)} %get-tuple-element.50), calls=%async_computation.2 | async-start | bytes 16384 | tf_op jit(solution)/shard_map/all_to_all | solution.py:320
  129.6 6.6 %hidden.1.hid = bf16[4,128,640]{2,1,0:T(8,128)(2,1)} custom-call(s32[2]{0:T(128)} %pad_add_fusion.where, f32[128,256]{1,0:T(8,128)} %get-tuple-element.51.pred_s, f32[128,1536]{1,0:T(8,128)} %get-tuple-element.52.pred_d, bf16[128,256]{1,0:T(8,128)(2,1)} %get-tuple-element.41.goal_s, bf16[128,1536]{1,0:T(8,128)(2,1)} %get-tuple-element.42.goal_d, ...), custom_call_target="tpu_custom_call" | custom-call | tf_op jit(solution)/shard_map/hidden/pallas_call | solution.py:321
  136.2 0.4 all-to-all-done.2
  136.6 0.6 broadcast_in_dim.37
  137.2 9.1 %all-to-all-start.3 = ((f32[32,1,128]{2,1,0:T(1,128)}), f32[32,1,128]{2,1,0:T(1,128)S(1)}, u32[]{:S(2)}, u32[]{:S(2)}) async-start(f32[32,1,128]{2,1,0:T(1,128)} %broadcast_in_dim.37), calls=%async_computation.3 | async-start | bytes 32768 | tf_op jit(solution)/shard_map/all_to_all | solution.py:337
  146.4 7.2 %grad.1 = bf16[128,1280]{1,0:T(8,128)(2,1)} custom-call(s32[2]{0:T(128)} %pad_add_fusion.where, bf16[4,128,640]{2,1,0:T(8,128)(2,1)} %hidden.1.hid, bf16[640,1024]{1,0:T(8,128)(2,1)} %copy-done.1, bf16[640,1024]{1,0:T(8,128)(2,1)} %copy-done.2, bf16[640,1024]{1,0:T(8,128)(2,1)} %collective-permute-done.4.m1, bf16[640,1024]{1,0:T(8,128)(2,1)} %collective-permute-done.6.o1, ...), custom_call_target="tpu_custom_call" | custom-call | tf_op jit(solution)/shard_map/grad/pallas_call | solution.py:340
  153.7 1.3 all-to-all-done.3
  155.0 0.6 slice_reduce_fusion
  (41 shorter events, 0.3 us)
Async XLA Ops:
  0.6 39.3 %copy-start = (bf16[128,1280]{1,0:T(8,128)(2,1)S(1)}, bf16[128,1280]{1,0:T(8,128)(2,1)}, u32[]{:S(2)}) copy-start(bf16[128,1280]{1,0:T(8,128)(2,1)} %param.10) | copy-start | bytes 983044
  4.9 17.4 %copy-start.11 = (bf16[10,256]{1,0:T(8,128)(2,1)S(1)}, bf16[10,256]{1,0:T(8,128)(2,1)}, u32[]{:S(2)}) copy-start(bf16[10,256]{1,0:T(8,128)(2,1)} %param.17) | copy-start | bytes 15364
  4.9 48.9 %all-to-all-start = ((bf16[64,5,2,1024]{3,2,1,0:T(2,128)(2,1)}), bf16[64,5,2,1024]{3,2,1,0:T(2,128)(2,1)S(1)}, u32[]{:S(2)}, u32[]{:S(2)}) async-start(bf16[64,5,2,1024]{3,2,1,0:T(2,128)(2,1)} %broadcast_in_dim.31), calls=%async_computation | async-start | bytes 2621440 | tf_op jit(solution)/shard_map/all_to_all | solution.py:236
  22.1 2.6 %copy-start.10 = (bf16[4,128,64]{1,2,0:T(8,128)(2,1)S(1)}, bf16[4,128,64]{1,2,0:T(8,128)(2,1)}, u32[]{:S(2)}) copy-start(bf16[4,128,64]{1,2,0:T(8,128)(2,1)} %param.11) | copy-start | bytes 196612
  22.1 2.8 %copy-start.6 = (bf16[4,128,384]{2,1,0:T(8,128)(2,1)S(1)}, bf16[4,128,384]{2,1,0:T(8,128)(2,1)}, u32[]{:S(2)}) copy-start(bf16[4,128,384]{2,1,0:T(8,128)(2,1)} %param.12) | copy-start | bytes 1179652
  24.7 11.7 %copy-start.14 = (s32[64]{0:T(128)S(1)}, s32[64]{0:T(128)}, u32[]{:S(2)}) copy-start(s32[64]{0:T(128)} %param.15) | copy-start | bytes 772
  24.7 12.4 %copy-start.13 = (f32[256]{0:T(256)S(1)}, f32[256]{0:T(256)}, u32[]{:S(2)}) copy-start(f32[256]{0:T(256)} %param.13) | copy-start | bytes 3076
  24.7 13.8 %copy-start.12 = (f32[1536]{0:T(1024)S(1)}, f32[1536]{0:T(1024)}, u32[]{:S(2)}) copy-start(f32[1536]{0:T(1024)} %param.14) | copy-start | bytes 18436
  25.8 18.9 %collective-permute-start.2 = (bf16[128,512]{1,0:T(8,128)(2,1)S(1)}, bf16[128,512]{1,0:T(8,128)(2,1)S(1)}, u32[]{:S(2)}, u32[]{:S(2)}) collective-permute-start(bf16[128,512]{1,0:T(8,128)(2,1)S(1)} %get-tuple-element.62), channel_id=1, source_target_pairs={{0,128},{128,256},{256,384},{384,0},{1,129},{129,257},{257,385},{3... | collective-permute-start | bytes 393224 | tf_op jit(solution)/shard_map/ppermute | solution.py:249
  28.9 15.8 %collective-permute-start.1 = (bf16[128,512]{1,0:T(8,128)(2,1)S(1)}, bf16[128,512]{1,0:T(8,128)(2,1)S(1)}, u32[]{:S(2)}, u32[]{:S(2)}) collective-permute-start(bf16[128,512]{1,0:T(8,128)(2,1)S(1)} %get-tuple-element.63), channel_id=1, source_target_pairs={{0,256},{128,384},{256,0},{384,128},{1,257},{129,385},{257,1},{385... | collective-permute-start | bytes 393224 | tf_op jit(solution)/shard_map/ppermute | solution.py:249
  33.3 11.5 %collective-permute-start = (bf16[128,512]{1,0:T(8,128)(2,1)S(1)}, bf16[128,512]{1,0:T(8,128)(2,1)S(1)}, u32[]{:S(2)}, u32[]{:S(2)}) collective-permute-start(bf16[128,512]{1,0:T(8,128)(2,1)S(1)} %get-tuple-element.64), channel_id=1, source_target_pairs={{0,384},{128,0},{256,128},{384,256},{1,385},{129,1},{257,129},{385... | collective-permute-start | bytes 393224 | tf_op jit(solution)/shard_map/ppermute | solution.py:249
  40.7 63.6 %copy-start.4 = (bf16[128,640]{1,0:T(8,128)(2,1)}, bf16[128,640]{1,0:T(8,128)(2,1)S(1)}, u32[]{:S(2)}) copy-start(bf16[128,640]{1,0:T(8,128)(2,1)S(1)} %fusion.42.tok_m) | copy-start | bytes 491524
  41.5 63.2 %copy-start.5 = (bf16[128,640]{1,0:T(8,128)(2,1)}, bf16[128,640]{1,0:T(8,128)(2,1)S(1)}, u32[]{:S(2)}) copy-start(bf16[128,640]{1,0:T(8,128)(2,1)S(1)} %fusion.39.tok_o) | copy-start | bytes 491524
  44.7 0.7 copy-start.7
  44.7 0.7 copy-start.8
  44.8 0.7 copy-start.9
  54.2 50.1 %copy-start.1 = (bf16[640,1024]{1,0:T(8,128)(2,1)}, bf16[640,1024]{1,0:T(8,128)(2,1)S(1)}, u32[]{:S(2)}) copy-start(bf16[640,1024]{1,0:T(8,128)(2,1)S(1)} %reshape.56.m0) | copy-start | bytes 3932164
  54.2 51.6 %all-to-all-start.1 = ((bf16[64,5,2,1280]{3,2,1,0:T(2,128)(2,1)}), bf16[64,5,2,1280]{3,2,1,0:T(2,128)(2,1)}, u32[]{:S(2)}, u32[]{:S(2)}) async-start(bf16[64,5,2,1280]{3,2,1,0:T(2,128)(2,1)} %broadcast_in_dim.33), calls=%async_computation.1 | async-start | bytes 3276800 | tf_op jit(solution)/shard_map/all_to_all | solution.py:236
  64.2 31.9 %collective-permute-start.5 = (bf16[640,1024]{1,0:T(8,128)(2,1)S(1)}, bf16[640,1024]{1,0:T(8,128)(2,1)}, u32[]{:S(2)}, u32[]{:S(2)}) collective-permute-start(bf16[640,1024]{1,0:T(8,128)(2,1)S(1)} %reshape.56.m0), channel_id=1, source_target_pairs={{0,128},{128,256},{256,384},{384,0},{1,129},{129,257},{257,385},{3... | collective-permute-start | bytes 3932168 | tf_op jit(solution)/shard_map/ppermute | solution.py:285
  67.3 30.4 %collective-permute-start.4 = (bf16[640,1024]{1,0:T(8,128)(2,1)S(1)}, bf16[640,1024]{1,0:T(8,128)(2,1)}, u32[]{:S(2)}, u32[]{:S(2)}) collective-permute-start(bf16[640,1024]{1,0:T(8,128)(2,1)S(1)} %reshape.56.m0), channel_id=1, source_target_pairs={{0,384},{128,0},{256,128},{384,256},{1,385},{129,1},{257,129},{385... | collective-permute-start | bytes 3932168 | tf_op jit(solution)/shard_map/ppermute | solution.py:284
  70.7 34.0 %collective-permute-start.3 = (bf16[640,1024]{1,0:T(8,128)(2,1)S(1)}, bf16[640,1024]{1,0:T(8,128)(2,1)S(1)}, u32[]{:S(2)}, u32[]{:S(2)}) collective-permute-start(bf16[640,1024]{1,0:T(8,128)(2,1)S(1)} %reshape.56.m0), channel_id=1, source_target_pairs={{0,4},{4,0},{1,5},{5,1},{2,6},{6,2},{3,7},{7,3},{8,12},{12,8},{9,1... | collective-permute-start | bytes 3932168 | tf_op jit(solution)/shard_map/ppermute | solution.py:281
  97.7 10.6 %collective-permute-start.6 = (bf16[640,1024]{1,0:T(8,128)(2,1)}, bf16[640,1024]{1,0:T(8,128)(2,1)}, u32[]{:S(2)}, u32[]{:S(2)}) collective-permute-start(bf16[640,1024]{1,0:T(8,128)(2,1)} %collective-permute-done.4.m1), channel_id=1, source_target_pairs={{0,4},{4,0},{1,5},{5,1},{2,6},{6,2},{3,7},{7,3},{8,12},{12,8},{9,1... | collective-permute-start | bytes 3932168 | tf_op jit(solution)/shard_map/ppermute | solution.py:281
  102.4 5.9 %collective-permute-start.7 = (bf16[640,1024]{1,0:T(8,128)(2,1)}, bf16[640,1024]{1,0:T(8,128)(2,1)}, u32[]{:S(2)}, u32[]{:S(2)}) collective-permute-start(bf16[640,1024]{1,0:T(8,128)(2,1)} %collective-permute-done.5.m3), channel_id=1, source_target_pairs={{0,4},{4,0},{1,5},{5,1},{2,6},{6,2},{3,7},{7,3},{8,12},{12,8},{9,1... | collective-permute-start | bytes 3932168 | tf_op jit(solution)/shard_map/ppermute | solution.py:281
  104.7 3.6 %copy-start.2 = (bf16[640,1024]{1,0:T(8,128)(2,1)}, bf16[640,1024]{1,0:T(8,128)(2,1)S(1)}, u32[]{:S(2)}) copy-start(bf16[640,1024]{1,0:T(8,128)(2,1)S(1)} %collective-permute-done.3.o0) | copy-start | bytes 3932164
  108.3 6.4 %collective-permute-start.8 = (bf16[640,1280]{1,0:T(8,128)(2,1)}, bf16[640,1280]{1,0:T(8,128)(2,1)S(1)}, u32[]{:S(2)}, u32[]{:S(2)}) collective-permute-start(bf16[640,1280]{1,0:T(8,128)(2,1)} %rows.1.m2), channel_id=1, source_target_pairs={{0,4},{4,0},{1,5},{5,1},{2,6},{6,2},{3,7},{7,3},{8,12},{12,8},{9,1... | collective-permute-start | bytes 4915208 | tf_op jit(solution)/shard_map/ppermute | solution.py:281
  114.7 1.2 copy-start.3
  123.2 13.4 %all-to-all-start.2 = ((f32[16,1,128]{2,1,0:T(1,128)}), f32[16,1,128]{2,1,0:T(1,128)S(1)}, u32[]{:S(2)}, u32[]{:S(2)}) async-start(f32[16,1,128]{2,1,0:T(1,128)} %get-tuple-element.50), calls=%async_computation.2 | async-start | bytes 16384 | tf_op jit(solution)/shard_map/all_to_all | solution.py:320
  137.2 17.7 %all-to-all-start.3 = ((f32[32,1,128]{2,1,0:T(1,128)}), f32[32,1,128]{2,1,0:T(1,128)S(1)}, u32[]{:S(2)}, u32[]{:S(2)}) async-start(f32[32,1,128]{2,1,0:T(1,128)} %broadcast_in_dim.37), calls=%async_computation.3 | async-start | bytes 32768 | tf_op jit(solution)/shard_map/all_to_all | solution.py:337

commit v7 on v6

--- a/solution.py
+++ b/solution.py
@@ -284,12 +284,12 @@
     next_m = lax.ppermute(own, "x", ring(4, -1))
     prev_m = lax.ppermute(own, "x", ring(4, 1))
     own_o = swap(own)
-    pre0 = dot(tok_m, own[:, :HALF]) + dot(tok_o, own_o[:, :HALF])
     next_m, prev_m = lax.optimization_barrier((next_m, prev_m))
     next_o, prev_o = swap(next_m), swap(prev_m)
-    opp_g, pre0 = lax.optimization_barrier((opp_g, pre0))
+    opp_g, own_o = lax.optimization_barrier((opp_g, own_o))
     opp = full_rows(opp_g)
     opp, next_o, prev_o = lax.optimization_barrier((opp, next_o, prev_o))
+    pre0 = dot(tok_m, own[:, :HALF]) + dot(tok_o, own_o[:, :HALF])
     slots = [(own, own_o), (next_m, next_o), (opp, swap(opp)), (prev_m, prev_o)]
     flat = [w for pair in slots for w in pair]
     anywhere = pl.BlockSpec(memory_space=pl.ANY)

time: 158 us -> 157 us (level)
  transfers between devices with their start and end apart: 13 -> 13, of which waited for: 6 -> 7; matrix products, arithmetic and copies ran while one was open for 8% -> 8% of each run, Pallas kernels for 12% -> 12%
where the time goes in v7:
time: 157 us; the launch traced here: 156 us
  starting transfers between devices  73.1 us (47%)
  waiting for transfers between devices  32.9 us (21%)
  Pallas kernels  26.4 us (17%)
  local copies, waits for them, and re-layouts  10.4 us (7%)
  other arithmetic  5.44 us (3%)
  matrix products  4.36 us (3%)
  between operations  3.8 us (2%)
    all_to_all x2, starting transfers between devices, gather_plane(): return lax.all_to_all(many, PLANE, split_axis=0, concat_axis=0, tiled=True)  27.2 us
    ppermute x1, waiting for transfers between devices, shards(): prev_m = lax.ppermute(own, 'x', ring(4, 1))  21.3 us
    ppermute x4, starting transfers between devices, swap(): return lax.ppermute(value, 'core', ring(2, 1))  14.4 us
    ppermute x3, starting transfers between devices, shards(): lax.ppermute(feat_for(s), 'x', ring(4, -s))  10.5 us
    all_to_all x1, starting transfers between devices, shards(): lax.all_to_all(loss, ('x', 'ylo', 'yhi'), split_axis=0, concat_axis=0, ti...  9.15 us
    pallas_call x1, Pallas kernels, shards(): pl.pallas_call(forward_kernel, out_shape=(jax.ShapeDtypeStruct((rows, SAM...  7.36 us
    pallas_call x1, Pallas kernels, shards(): pl.pallas_call(grad_kernel, out_shape=jax.ShapeDtypeStruct((rows, 2 * HAL...  7.24 us
    pallas_call x1, Pallas kernels, shards(): pl.pallas_call(hidden_kernel, out_shape=jax.ShapeDtypeStruct((4, rows, HA...  6.58 us
  transfers between devices with their start and end apart: 13, of which 7 were waited for; matrix products, arithmetic and copies ran while one was open for 8% of the time, Pallas kernels for 12%

profile of v7, /device:TPU:1, one launch (start us, length us, event | category | flops | bytes accessed | tf_op | source)
XLA Modules:
  0.0 156.4 jit_solution(2122185952047523746)
XLA Ops:
  0.6 0.0 copy-start
  0.8 0.7 constant_dynamic-slice_fusion
  1.5 1.5 fusion.45
  3.1 1.8 %broadcast_in_dim.31 = bf16[64,5,2,1024]{3,2,1,0:T(2,128)(2,1)} broadcast(bf16[5,2,1024]{2,1,0:T(2,128)(2,1)S(1)} %maximum_bitcast_fusion), dimensions={1,2,3} | broadcast | bytes 1331200 | tf_op jit(solution)/shard_map/broadcast_in_dim | solution.py:233
  4.9 17.3 %all-to-all-start = ((bf16[64,5,2,1024]{3,2,1,0:T(2,128)(2,1)}), bf16[64,5,2,1024]{3,2,1,0:T(2,128)(2,1)S(1)}, u32[]{:S(2)}, u32[]{:S(2)}) async-start(bf16[64,5,2,1024]{3,2,1,0:T(2,128)(2,1)} %broadcast_in_dim.31), calls=%async_computation | async-start | bytes 2621440 | tf_op jit(solution)/shard_map/all_to_all | solution.py:236
  22.1 0.0 copy-start.10
  22.1 0.0 copy-start.6
  22.3 0.1 reshape.57
  22.4 0.1 dynamic-slice_reduce_fusion
  22.6 0.1 concatenate.46
  22.7 2.0 %broadcast_in_dim.33 = bf16[64,5,2,1280]{3,2,1,0:T(2,128)(2,1)} broadcast(bf16[5,2,1280]{2,1,0:T(2,128)(2,1)S(1)} %bitcast.24), dimensions={1,2,3} | broadcast | bytes 1664000 | tf_op jit(solution)/shard_map/broadcast_in_dim | solution.py:233
  24.7 0.1 copy.33
  24.9 0.1 pad.12.clone
  25.0 0.1 maximum_maximum_fusion
  25.1 0.7 dynamic-slice_bitcast_fusion
  25.8 3.1 %collective-permute-start.2 = (bf16[128,512]{1,0:T(8,128)(2,1)S(1)}, bf16[128,512]{1,0:T(8,128)(2,1)S(1)}, u32[]{:S(2)}, u32[]{:S(2)}) collective-permute-start(bf16[128,512]{1,0:T(8,128)(2,1)S(1)} %get-tuple-element.62), channel_id=1, source_target_pairs={{0,128},{128,256},{256,384},{384,0},{1,129},{129,257},{257,385},{3... | collective-permute-start | bytes 393224 | tf_op jit(solution)/shard_map/ppermute | solution.py:249
  28.9 4.4 %collective-permute-start.1 = (bf16[128,512]{1,0:T(8,128)(2,1)S(1)}, bf16[128,512]{1,0:T(8,128)(2,1)S(1)}, u32[]{:S(2)}, u32[]{:S(2)}) collective-permute-start(bf16[128,512]{1,0:T(8,128)(2,1)S(1)} %get-tuple-element.63), channel_id=1, source_target_pairs={{0,256},{128,384},{256,0},{384,128},{1,257},{129,385},{257,1},{385... | collective-permute-start | bytes 393224 | tf_op jit(solution)/shard_map/ppermute | solution.py:249
  33.3 3.1 %collective-permute-start = (bf16[128,512]{1,0:T(8,128)(2,1)S(1)}, bf16[128,512]{1,0:T(8,128)(2,1)S(1)}, u32[]{:S(2)}, u32[]{:S(2)}) collective-permute-start(bf16[128,512]{1,0:T(8,128)(2,1)S(1)} %get-tuple-element.64), channel_id=1, source_target_pairs={{0,384},{128,0},{256,128},{384,256},{1,385},{129,1},{257,129},{385... | collective-permute-start | bytes 393224 | tf_op jit(solution)/shard_map/ppermute | solution.py:249
  36.4 0.7 dynamic_slice.87
  37.1 0.1 fusion.67
  37.2 0.7 pad_maximum_fusion.1
  37.8 0.7 clamp_reduce_fusion
  38.5 0.1 fusion.66
  38.6 1.3 fusion.52.live
  39.9 0.8 fusion.42.tok_m
  40.7 0.8 fusion.39.tok_o
  41.5 0.6 pad_add_fusion.where
  42.8 0.6 broadcast_in_dim.36.gain_d
  43.4 1.3 fusion.51.scale
  44.7 0.0 collective-permute-done.2.f3
  44.7 0.0 collective-permute-done.1.f2
  44.8 0.0 collective-permute-done.f1
  44.8 0.6 copy-done.7
  45.4 0.0 copy-done.8
  45.4 0.1 copy-done.9
  45.5 2.3 %target.1 = (bf16[128,256]{1,0:T(8,128)(2,1)}, bf16[128,1536]{1,0:T(8,128)(2,1)}) custom-call(bf16[128,512]{1,0:T(8,128)(2,1)} %get-tuple-element.65.f0, bf16[128,512]{1,0:T(8,128)(2,1)} %copy-done.9, bf16[128,512]{1,0:T(8,128)(2,1)} %copy-done.8, bf16[128,512]{1,0:T(8,128)(2,1)} %copy-done.7, f32[1,256]{1,0:T(1,128)} %bitcast.25, ...), custom_call_target="tpu_custom_call" | custom-call | tf_op jit(solution)/shard_map/target/pallas_call | solution.py:266
  47.8 5.9 %all-to-all-done = bf16[64,5,2,1024]{3,2,1,0:T(2,128)(2,1)S(1)} async-done(((bf16[64,5,2,1024]{3,2,1,0:T(2,128)(2,1)}), bf16[64,5,2,1024]{3,2,1,0:T(2,128)(2,1)S(1)}, u32[]{:S(2)}, u32[]{:S(2)}) %all-to-all-start) | async-done | bytes 1310752 | tf_op jit(solution)/shard_map/all_to_all | solution.py:236
  53.7 0.5 reshape.56.m0
  54.2 9.9 %all-to-all-start.1 = ((bf16[64,5,2,1280]{3,2,1,0:T(2,128)(2,1)}), bf16[64,5,2,1280]{3,2,1,0:T(2,128)(2,1)}, u32[]{:S(2)}, u32[]{:S(2)}) async-start(bf16[64,5,2,1280]{3,2,1,0:T(2,128)(2,1)} %broadcast_in_dim.33), calls=%async_computation.1 | async-start | bytes 3276800 | tf_op jit(solution)/shard_map/all_to_all | solution.py:236
  64.2 3.1 %collective-permute-start.5 = (bf16[640,1024]{1,0:T(8,128)(2,1)S(1)}, bf16[640,1024]{1,0:T(8,128)(2,1)}, u32[]{:S(2)}, u32[]{:S(2)}) collective-permute-start(bf16[640,1024]{1,0:T(8,128)(2,1)S(1)} %reshape.56.m0), channel_id=1, source_target_pairs={{0,128},{128,256},{256,384},{384,0},{1,129},{129,257},{257,385},{3... | collective-permute-start | bytes 3932168 | tf_op jit(solution)/shard_map/ppermute | solution.py:285
  67.3 3.4 %collective-permute-start.4 = (bf16[640,1024]{1,0:T(8,128)(2,1)S(1)}, bf16[640,1024]{1,0:T(8,128)(2,1)}, u32[]{:S(2)}, u32[]{:S(2)}) collective-permute-start(bf16[640,1024]{1,0:T(8,128)(2,1)S(1)} %reshape.56.m0), channel_id=1, source_target_pairs={{0,384},{128,0},{256,128},{384,256},{1,385},{129,1},{257,129},{385... | collective-permute-start | bytes 3932168 | tf_op jit(solution)/shard_map/ppermute | solution.py:284
  70.7 4.1 %collective-permute-start.3 = (bf16[640,1024]{1,0:T(8,128)(2,1)S(1)}, bf16[640,1024]{1,0:T(8,128)(2,1)S(1)}, u32[]{:S(2)}, u32[]{:S(2)}) collective-permute-start(bf16[640,1024]{1,0:T(8,128)(2,1)S(1)} %reshape.56.m0), channel_id=1, source_target_pairs={{0,4},{4,0},{1,5},{5,1},{2,6},{6,2},{3,7},{7,3},{8,12},{12,8},{9,1... | collective-permute-start | bytes 3932168 | tf_op jit(solution)/shard_map/ppermute | solution.py:281
  74.8 21.3 %collective-permute-done.5.m3 = bf16[640,1024]{1,0:T(8,128)(2,1)} collective-permute-done((bf16[640,1024]{1,0:T(8,128)(2,1)S(1)}, bf16[640,1024]{1,0:T(8,128)(2,1)}, u32[]{:S(2)}, u32[]{:S(2)}) %collective-permute-start.5) | collective-permute-done | bytes 1310752 | tf_op jit(solution)/shard_map/ppermute | solution.py:285
  96.0 1.6 %collective-permute-done.4.m1 = bf16[640,1024]{1,0:T(8,128)(2,1)} collective-permute-done((bf16[640,1024]{1,0:T(8,128)(2,1)S(1)}, bf16[640,1024]{1,0:T(8,128)(2,1)}, u32[]{:S(2)}, u32[]{:S(2)}) %collective-permute-start.4) | collective-permute-done | bytes 1310752 | tf_op jit(solution)/shard_map/ppermute | solution.py:284
  97.7 4.7 %collective-permute-start.6 = (bf16[640,1024]{1,0:T(8,128)(2,1)}, bf16[640,1024]{1,0:T(8,128)(2,1)}, u32[]{:S(2)}, u32[]{:S(2)}) collective-permute-start(bf16[640,1024]{1,0:T(8,128)(2,1)} %collective-permute-done.4.m1), channel_id=1, source_target_pairs={{0,4},{4,0},{1,5},{5,1},{2,6},{6,2},{3,7},{7,3},{8,12},{12,8},{9,1... | collective-permute-start | bytes 3932168 | tf_op jit(solution)/shard_map/ppermute | solution.py:281
  102.4 1.9 %collective-permute-start.7 = (bf16[640,1024]{1,0:T(8,128)(2,1)}, bf16[640,1024]{1,0:T(8,128)(2,1)}, u32[]{:S(2)}, u32[]{:S(2)}) collective-permute-start(bf16[640,1024]{1,0:T(8,128)(2,1)} %collective-permute-done.5.m3), channel_id=1, source_target_pairs={{0,4},{4,0},{1,5},{5,1},{2,6},{6,2},{3,7},{7,3},{8,12},{12,8},{9,1... | collective-permute-start | bytes 3932168 | tf_op jit(solution)/shard_map/ppermute | solution.py:281
  104.3 0.0 collective-permute-done.3.o0
  104.3 0.0 all-to-all-done.1
  104.4 2.9 %rows.1.m2 = bf16[640,1280]{1,0:T(8,128)(2,1)} custom-call(bf16[320,2,1280]{2,1,0:T(2,128)(2,1)} %bitcast.12.pairs), custom_call_target="tpu_custom_call" | custom-call | tf_op jit(solution)/shard_map/rows/pallas_call | solution.py:197
  107.3 0.4 collective-permute-done.7.o3
  107.7 3.7 %collective-permute-start.8 = (bf16[640,1280]{1,0:T(8,128)(2,1)}, bf16[640,1280]{1,0:T(8,128)(2,1)S(1)}, u32[]{:S(2)}, u32[]{:S(2)}) collective-permute-start(bf16[640,1280]{1,0:T(8,128)(2,1)} %rows.1.m2), channel_id=1, source_target_pairs={{0,4},{4,0},{1,5},{5,1},{2,6},{6,2},{3,7},{7,3},{8,12},{12,8},{9,1... | collective-permute-start | bytes 4915208 | tf_op jit(solution)/shard_map/ppermute | solution.py:281
  111.4 0.3 fusion.49
  111.7 1.1 convolution_add_fusion.pre0
  112.8 1.9 %collective-permute-done.8.o2 = bf16[640,1280]{1,0:T(8,128)(2,1)S(1)} collective-permute-done((bf16[640,1280]{1,0:T(8,128)(2,1)}, bf16[640,1280]{1,0:T(8,128)(2,1)S(1)}, u32[]{:S(2)}, u32[]{:S(2)}) %collective-permute-start.8) | collective-permute-done | bytes 1638432 | tf_op jit(solution)/shard_map/ppermute | solution.py:281
  114.7 1.2 copy-done.3
  115.8 7.4 %forward.1 = (f32[128,256]{1,0:T(8,128)}, f32[128,1536]{1,0:T(8,128)}, f32[4,128,640]{2,1,0:T(8,128)}, f32[128,4]{1,0:T(8,128)}, f32[16,1,128]{2,1,0:T(1,128)}) custom-call(s32[2]{0:T(128)} %pad_add_fusion.where, bf16[128,640]{1,0:T(8,128)(2,1)} %copy-done.4, bf16[128,640]{1,0:T(8,128)(2,1)} %copy-done.5, f32[128,640]{1,0:T(8,128)} %convolution_add_fusion.pre0, ...), custom_call_target="tpu_custom_call" | custom-call | tf_op jit(solution)/shard_map/forward/pallas_call | solution.py:298
  123.2 5.4 %all-to-all-start.2 = ((f32[16,1,128]{2,1,0:T(1,128)}), f32[16,1,128]{2,1,0:T(1,128)S(1)}, u32[]{:S(2)}, u32[]{:S(2)}) async-start(f32[16,1,128]{2,1,0:T(1,128)} %get-tuple-element.50), calls=%async_computation.2 | async-start | bytes 16384 | tf_op jit(solution)/shard_map/all_to_all | solution.py:320
  128.6 6.6 %hidden.1.hid = bf16[4,128,640]{2,1,0:T(8,128)(2,1)} custom-call(s32[2]{0:T(128)} %pad_add_fusion.where, f32[128,256]{1,0:T(8,128)} %get-tuple-element.51.pred_s, f32[128,1536]{1,0:T(8,128)} %get-tuple-element.52.pred_d, bf16[128,256]{1,0:T(8,128)(2,1)} %get-tuple-element.41.goal_s, bf16[128,1536]{1,0:T(8,128)(2,1)} %get-tuple-element.42.goal_d, ...), custom_call_target="tpu_custom_call" | custom-call | tf_op jit(solution)/shard_map/hidden/pallas_call | solution.py:321
  135.1 0.4 all-to-all-done.2
  135.6 0.6 broadcast_in_dim.37
  136.2 9.2 %all-to-all-start.3 = ((f32[32,1,128]{2,1,0:T(1,128)}), f32[32,1,128]{2,1,0:T(1,128)S(1)}, u32[]{:S(2)}, u32[]{:S(2)}) async-start(f32[32,1,128]{2,1,0:T(1,128)} %broadcast_in_dim.37), calls=%async_computation.3 | async-start | bytes 32768 | tf_op jit(solution)/shard_map/all_to_all | solution.py:337
  145.4 7.2 %grad.1 = bf16[128,1280]{1,0:T(8,128)(2,1)} custom-call(s32[2]{0:T(128)} %pad_add_fusion.where, bf16[4,128,640]{2,1,0:T(8,128)(2,1)} %hidden.1.hid, bf16[640,1024]{1,0:T(8,128)(2,1)} %copy-done.1, bf16[640,1024]{1,0:T(8,128)(2,1)} %copy-done.2, bf16[640,1024]{1,0:T(8,128)(2,1)} %collective-permute-done.4.m1, bf16[640,1024]{1,0:T(8,128)(2,1)} %collective-permute-done.6.o1, ...), custom_call_target="tpu_custom_call" | custom-call | tf_op jit(solution)/shard_map/grad/pallas_call | solution.py:340
  152.6 1.3 all-to-all-done.3
  154.0 0.6 slice_reduce_fusion
  (41 shorter events, 0.3 us)
Async XLA Ops:
  0.6 39.3 %copy-start = (bf16[128,1280]{1,0:T(8,128)(2,1)S(1)}, bf16[128,1280]{1,0:T(8,128)(2,1)}, u32[]{:S(2)}) copy-start(bf16[128,1280]{1,0:T(8,128)(2,1)} %param.10) | copy-start | bytes 983044
  4.9 17.4 %copy-start.11 = (bf16[10,256]{1,0:T(8,128)(2,1)S(1)}, bf16[10,256]{1,0:T(8,128)(2,1)}, u32[]{:S(2)}) copy-start(bf16[10,256]{1,0:T(8,128)(2,1)} %param.17) | copy-start | bytes 15364
  4.9 48.9 %all-to-all-start = ((bf16[64,5,2,1024]{3,2,1,0:T(2,128)(2,1)}), bf16[64,5,2,1024]{3,2,1,0:T(2,128)(2,1)S(1)}, u32[]{:S(2)}, u32[]{:S(2)}) async-start(bf16[64,5,2,1024]{3,2,1,0:T(2,128)(2,1)} %broadcast_in_dim.31), calls=%async_computation | async-start | bytes 2621440 | tf_op jit(solution)/shard_map/all_to_all | solution.py:236
  22.1 2.6 %copy-start.10 = (bf16[4,128,64]{1,2,0:T(8,128)(2,1)S(1)}, bf16[4,128,64]{1,2,0:T(8,128)(2,1)}, u32[]{:S(2)}) copy-start(bf16[4,128,64]{1,2,0:T(8,128)(2,1)} %param.11) | copy-start | bytes 196612
  22.1 2.8 %copy-start.6 = (bf16[4,128,384]{2,1,0:T(8,128)(2,1)S(1)}, bf16[4,128,384]{2,1,0:T(8,128)(2,1)}, u32[]{:S(2)}) copy-start(bf16[4,128,384]{2,1,0:T(8,128)(2,1)} %param.12) | copy-start | bytes 1179652
  24.7 11.7 %copy-start.14 = (s32[64]{0:T(128)S(1)}, s32[64]{0:T(128)}, u32[]{:S(2)}) copy-start(s32[64]{0:T(128)} %param.15) | copy-start | bytes 772
  24.7 12.4 %copy-start.13 = (f32[256]{0:T(256)S(1)}, f32[256]{0:T(256)}, u32[]{:S(2)}) copy-start(f32[256]{0:T(256)} %param.13) | copy-start | bytes 3076
  24.7 13.8 %copy-start.12 = (f32[1536]{0:T(1024)S(1)}, f32[1536]{0:T(1024)}, u32[]{:S(2)}) copy-start(f32[1536]{0:T(1024)} %param.14) | copy-start | bytes 18436
  25.8 18.9 %collective-permute-start.2 = (bf16[128,512]{1,0:T(8,128)(2,1)S(1)}, bf16[128,512]{1,0:T(8,128)(2,1)S(1)}, u32[]{:S(2)}, u32[]{:S(2)}) collective-permute-start(bf16[128,512]{1,0:T(8,128)(2,1)S(1)} %get-tuple-element.62), channel_id=1, source_target_pairs={{0,128},{128,256},{256,384},{384,0},{1,129},{129,257},{257,385},{3... | collective-permute-start | bytes 393224 | tf_op jit(solution)/shard_map/ppermute | solution.py:249
  28.9 15.8 %collective-permute-start.1 = (bf16[128,512]{1,0:T(8,128)(2,1)S(1)}, bf16[128,512]{1,0:T(8,128)(2,1)S(1)}, u32[]{:S(2)}, u32[]{:S(2)}) collective-permute-start(bf16[128,512]{1,0:T(8,128)(2,1)S(1)} %get-tuple-element.63), channel_id=1, source_target_pairs={{0,256},{128,384},{256,0},{384,128},{1,257},{129,385},{257,1},{385... | collective-permute-start | bytes 393224 | tf_op jit(solution)/shard_map/ppermute | solution.py:249
  33.3 11.5 %collective-permute-start = (bf16[128,512]{1,0:T(8,128)(2,1)S(1)}, bf16[128,512]{1,0:T(8,128)(2,1)S(1)}, u32[]{:S(2)}, u32[]{:S(2)}) collective-permute-start(bf16[128,512]{1,0:T(8,128)(2,1)S(1)} %get-tuple-element.64), channel_id=1, source_target_pairs={{0,384},{128,0},{256,128},{384,256},{1,385},{129,1},{257,129},{385... | collective-permute-start | bytes 393224 | tf_op jit(solution)/shard_map/ppermute | solution.py:249
  40.7 70.6 %copy-start.4 = (bf16[128,640]{1,0:T(8,128)(2,1)}, bf16[128,640]{1,0:T(8,128)(2,1)S(1)}, u32[]{:S(2)}) copy-start(bf16[128,640]{1,0:T(8,128)(2,1)S(1)} %fusion.42.tok_m) | copy-start | bytes 491524
  41.5 70.2 %copy-start.5 = (bf16[128,640]{1,0:T(8,128)(2,1)}, bf16[128,640]{1,0:T(8,128)(2,1)S(1)}, u32[]{:S(2)}) copy-start(bf16[128,640]{1,0:T(8,128)(2,1)S(1)} %fusion.39.tok_o) | copy-start | bytes 491524
  44.7 0.7 copy-start.7
  44.7 0.7 copy-start.8
  44.8 0.7 copy-start.9
  54.2 57.1 %copy-start.1 = (bf16[640,1024]{1,0:T(8,128)(2,1)}, bf16[640,1024]{1,0:T(8,128)(2,1)S(1)}, u32[]{:S(2)}) copy-start(bf16[640,1024]{1,0:T(8,128)(2,1)S(1)} %reshape.56.m0) | copy-start | bytes 3932164
  54.2 50.1 %all-to-all-start.1 = ((bf16[64,5,2,1280]{3,2,1,0:T(2,128)(2,1)}), bf16[64,5,2,1280]{3,2,1,0:T(2,128)(2,1)}, u32[]{:S(2)}, u32[]{:S(2)}) async-start(bf16[64,5,2,1280]{3,2,1,0:T(2,128)(2,1)} %broadcast_in_dim.33), calls=%async_computation.1 | async-start | bytes 3276800 | tf_op jit(solution)/shard_map/all_to_all | solution.py:236
  64.2 31.9 %collective-permute-start.5 = (bf16[640,1024]{1,0:T(8,128)(2,1)S(1)}, bf16[640,1024]{1,0:T(8,128)(2,1)}, u32[]{:S(2)}, u32[]{:S(2)}) collective-permute-start(bf16[640,1024]{1,0:T(8,128)(2,1)S(1)} %reshape.56.m0), channel_id=1, source_target_pairs={{0,128},{128,256},{256,384},{384,0},{1,129},{129,257},{257,385},{3... | collective-permute-start | bytes 3932168 | tf_op jit(solution)/shard_map/ppermute | solution.py:285
  67.3 30.4 %collective-permute-start.4 = (bf16[640,1024]{1,0:T(8,128)(2,1)S(1)}, bf16[640,1024]{1,0:T(8,128)(2,1)}, u32[]{:S(2)}, u32[]{:S(2)}) collective-permute-start(bf16[640,1024]{1,0:T(8,128)(2,1)S(1)} %reshape.56.m0), channel_id=1, source_target_pairs={{0,384},{128,0},{256,128},{384,256},{1,385},{129,1},{257,129},{385... | collective-permute-start | bytes 3932168 | tf_op jit(solution)/shard_map/ppermute | solution.py:284
  70.7 33.6 %collective-permute-start.3 = (bf16[640,1024]{1,0:T(8,128)(2,1)S(1)}, bf16[640,1024]{1,0:T(8,128)(2,1)S(1)}, u32[]{:S(2)}, u32[]{:S(2)}) collective-permute-start(bf16[640,1024]{1,0:T(8,128)(2,1)S(1)} %reshape.56.m0), channel_id=1, source_target_pairs={{0,4},{4,0},{1,5},{5,1},{2,6},{6,2},{3,7},{7,3},{8,12},{12,8},{9,1... | collective-permute-start | bytes 3932168 | tf_op jit(solution)/shard_map/ppermute | solution.py:281
  97.7 9.6 %collective-permute-start.6 = (bf16[640,1024]{1,0:T(8,128)(2,1)}, bf16[640,1024]{1,0:T(8,128)(2,1)}, u32[]{:S(2)}, u32[]{:S(2)}) collective-permute-start(bf16[640,1024]{1,0:T(8,128)(2,1)} %collective-permute-done.4.m1), channel_id=1, source_target_pairs={{0,4},{4,0},{1,5},{5,1},{2,6},{6,2},{3,7},{7,3},{8,12},{12,8},{9,1... | collective-permute-start | bytes 3932168 | tf_op jit(solution)/shard_map/ppermute | solution.py:281
  102.4 5.3 %collective-permute-start.7 = (bf16[640,1024]{1,0:T(8,128)(2,1)}, bf16[640,1024]{1,0:T(8,128)(2,1)}, u32[]{:S(2)}, u32[]{:S(2)}) collective-permute-start(bf16[640,1024]{1,0:T(8,128)(2,1)} %collective-permute-done.5.m3), channel_id=1, source_target_pairs={{0,4},{4,0},{1,5},{5,1},{2,6},{6,2},{3,7},{7,3},{8,12},{12,8},{9,1... | collective-permute-start | bytes 3932168 | tf_op jit(solution)/shard_map/ppermute | solution.py:281
  104.3 7.4 %copy-start.2 = (bf16[640,1024]{1,0:T(8,128)(2,1)}, bf16[640,1024]{1,0:T(8,128)(2,1)S(1)}, u32[]{:S(2)}) copy-start(bf16[640,1024]{1,0:T(8,128)(2,1)S(1)} %collective-permute-done.3.o0) | copy-start | bytes 3932164
  107.7 7.0 %collective-permute-start.8 = (bf16[640,1280]{1,0:T(8,128)(2,1)}, bf16[640,1280]{1,0:T(8,128)(2,1)S(1)}, u32[]{:S(2)}, u32[]{:S(2)}) collective-permute-start(bf16[640,1280]{1,0:T(8,128)(2,1)} %rows.1.m2), channel_id=1, source_target_pairs={{0,4},{4,0},{1,5},{5,1},{2,6},{6,2},{3,7},{7,3},{8,12},{12,8},{9,1... | collective-permute-start | bytes 4915208 | tf_op jit(solution)/shard_map/ppermute | solution.py:281
  114.7 1.2 copy-start.3
  123.2 12.4 %all-to-all-start.2 = ((f32[16,1,128]{2,1,0:T(1,128)}), f32[16,1,128]{2,1,0:T(1,128)S(1)}, u32[]{:S(2)}, u32[]{:S(2)}) async-start(f32[16,1,128]{2,1,0:T(1,128)} %get-tuple-element.50), calls=%async_computation.2 | async-start | bytes 16384 | tf_op jit(solution)/shard_map/all_to_all | solution.py:320
  136.2 17.8 %all-to-all-start.3 = ((f32[32,1,128]{2,1,0:T(1,128)}), f32[32,1,128]{2,1,0:T(1,128)S(1)}, u32[]{:S(2)}, u32[]{:S(2)}) async-start(f32[32,1,128]{2,1,0:T(1,128)} %broadcast_in_dim.37), calls=%async_computation.3 | async-start | bytes 32768 | tf_op jit(solution)/shard_map/all_to_all | solution.py:337
